TPU v7x, 32 devices: a whole 2x2x4 slice. The times are simulated.
32 devices in a mesh: groups: 2 (over x), space: 16 (over z, y, core).
Axes of the slice: x: 2, y: 2, z: 4, core: 2. Of those that a mesh axis runs over, the one named last changes fastest.
Arguments:
- grid_inputs: bfloat16 [16384, 474], P(('groups', 'space')), parts along dimension 0, may hold values from -6 to 6
- mesh_latent: bfloat16 [2048, 512], P(('groups', 'space')), parts along dimension 0, may hold values from -6 to 6
- cotangent: bfloat16 [2048, 512], P(('groups', 'space')), parts along dimension 0, may hold values from -6 to 6
- send_list: int32 [32, 16, 8], P(('groups', 'space')), parts along dimension 0, may hold values from 0 to 511
- enc_slot: int32 [2048, 16], P(('groups', 'space')), parts along dimension 0, may hold values from 0 to 639
- enc_mask: int32 [2048, 16], P(('groups', 'space')), parts along dimension 0, may hold values 0 or 1
- halo_list: int32 [32, 2, 64], P(('groups', 'space')), parts along dimension 0, may hold values from 0 to 63
- proc_slot: int32 [2048, 16], P(('groups', 'space')), parts along dimension 0, may hold values from 0 to 191
- proc_mask: int32 [2048, 16], P(('groups', 'space')), parts along dimension 0, may hold values 0 or 1
- w_embed: bfloat16 [474, 512], replicated, may hold values from -0.25 to 0.25
- enc_send: bfloat16 [512, 512], replicated, may hold values from -0.25 to 0.25
- enc_recv: bfloat16 [512, 512], replicated, may hold values from -0.25 to 0.25
- enc_out: bfloat16 [512, 512], replicated, may hold values from -0.25 to 0.25
- proc_send: bfloat16 [512, 512], replicated, may hold values from -0.25 to 0.25
- proc_recv: bfloat16 [512, 512], replicated, may hold values from -0.25 to 0.25
- proc_out: bfloat16 [512, 512], replicated, may hold values from -0.25 to 0.25
Outputs:
- mesh_out: bfloat16 [2048, 512], P(('groups', 'space')), parts along dimension 0
- grad_embed: float32 [948, 512], P('groups'), parts along dimension 0
- grad_enc_send: float32 [1024, 512], P('groups'), parts along dimension 0
- grad_enc_recv: float32 [1024, 512], P('groups'), parts along dimension 0
- grad_enc_out: float32 [1024, 512], P('groups'), parts along dimension 0
- grad_proc_send: float32 [1024, 512], P('groups'), parts along dimension 0
- grad_proc_recv: float32 [1024, 512], P('groups'), parts along dimension 0
- grad_proc_out: float32 [1024, 512], P('groups'), parts along dimension 0
There are 2 independent parts, one for each index of `groups`. A program takes and returns all parts, laid end to end along the dimension named above; an argument that names none is the same for every part. Nothing has to cross between parts.
All inputs are finite; a program needn't handle non-finite values. No bound on the sum of `enc_mask` or of `proc_mask` on one device may be relied on, other than what follows from the above.
Results may differ from a plain program's by a relative error of at most 0.0095.
Values may be sent and summed in bfloat16 or wider, within the bound.
No kernel may reach another device: no remote copies, remote signals or barrier semaphores. Data moves between devices by JAX's collectives and lax.ppermute only.
A program may use at most 128 MiB of HBM per device.

v0:
```python
import jax
import jax.numpy as jnp
from jax import lax
from jax.sharding import PartitionSpec as P


def passed_along(block, axis, distance):
    devices = range(lax.axis_size(axis))
    route = [((i - distance) % len(devices), i) for i in devices]
    return lax.ppermute(block, axis, route)


def pin(value):
    return value + lax.stop_gradient(value.astype(jnp.bfloat16).astype(jnp.float32) - value)


def mul(left, right):
    return jnp.dot(left, right, precision=lax.Precision.HIGHEST, preferred_element_type=jnp.float32)


def layer_norm(value):
    centred = value - jnp.mean(value, axis=-1, keepdims=True)
    return centred * lax.rsqrt(jnp.mean(centred * centred, axis=-1, keepdims=True) + 1e-05)


def embed(inputs, weight):
    return pin(jax.nn.silu(mul(inputs, weight)))


def project(rows, weight):
    return pin(mul(rows, weight))


def node_update(latent, summed, weight):
    return pin(latent + layer_norm(mul(summed, weight)))


def aggregate(table, slots, mask, recv_term):
    rows = table[slots]
    message = jax.nn.silu(rows + recv_term[:, None, :]) * mask[..., None].astype(jnp.float32)
    return pin(jnp.sum(message, axis=1))


def local(
    grid_inputs,
    mesh_latent,
    cotangent,
    send_list,
    enc_slot,
    enc_mask,
    halo_list,
    proc_slot,
    proc_mask,
    w_embed,
    enc_send,
    enc_recv,
    enc_out,
    proc_send,
    proc_recv,
    proc_out,
):
    peers = lax.axis_size("space")
    width = mesh_latent.shape[1]
    inputs = grid_inputs.astype(jnp.float32)
    mesh_start = mesh_latent.astype(jnp.float32)
    embed_w, esend_w, erecv_w, eout_w, psend_w, precv_w, pout_w = tuple(
        (
            item.astype(jnp.float32)
            for item in (w_embed, enc_send, enc_recv, enc_out, proc_send, proc_recv, proc_out)
        )
    )
    sends = send_list[0]
    source, grid_pull = jax.vjp(lambda first: embed(inputs, first), embed_w)
    outgoing = source[sends].astype(jnp.bfloat16)
    incoming = lax.all_to_all(outgoing, "space", split_axis=0, concat_axis=0, tiled=True)
    table = jnp.concatenate([source, incoming.reshape(-1, width).astype(jnp.float32)], axis=0)

    def encode(rows, send_w, recv_w, out_w, next_w):
        summed = aggregate(project(rows, send_w), enc_slot, enc_mask, mul(mesh_start, recv_w))
        middle = node_update(mesh_start, summed, out_w)
        return (middle, project(middle, next_w))

    (middle, mesh_proj), enc_pull = jax.vjp(encode, table, esend_w, erecv_w, eout_w, psend_w)
    boundary = mesh_proj[halo_list[0]].astype(jnp.bfloat16)
    from_left = passed_along(boundary[1], "space", 1)
    from_right = passed_along(boundary[0], "space", -1)
    proc_table = jnp.concatenate(
        [mesh_proj, from_left.astype(jnp.float32), from_right.astype(jnp.float32)], axis=0
    )

    def process(rows, latent, recv_w, out_w):
        summed = aggregate(rows, proc_slot, proc_mask, mul(latent, recv_w))
        return node_update(latent, summed, out_w)

    result, proc_pull = jax.vjp(process, proc_table, middle, precv_w, pout_w)
    grad_table, grad_middle, grad_precv, grad_pout = proc_pull(cotangent.astype(jnp.float32))
    mesh_rows = mesh_proj.shape[0]
    depth = halo_list.shape[2]
    back_right = passed_along(
        grad_table[mesh_rows : mesh_rows + depth].astype(jnp.bfloat16), "space", -1
    ).astype(jnp.float32)
    back_left = passed_along(
        grad_table[mesh_rows + depth :].astype(jnp.bfloat16), "space", 1
    ).astype(jnp.float32)
    grad_proj = (
        grad_table[:mesh_rows]
        .at[halo_list[0, 1]]
        .add(back_right)
        .at[halo_list[0, 0]]
        .add(back_left)
    )
    pulled = enc_pull((grad_middle, grad_proj))
    grad_rows = pulled[0]
    local_rows = source.shape[0]
    grad_incoming = grad_rows[local_rows:].reshape(peers, -1, width)
    returned = lax.all_to_all(
        grad_incoming.astype(jnp.bfloat16), "space", split_axis=0, concat_axis=0, tiled=True
    ).astype(grad_incoming.dtype)
    grad_source = grad_rows[:local_rows].at[sends.reshape(-1)].add(returned.reshape(-1, width))
    grid_grads = grid_pull(grad_source)
    grad_embed = grid_grads[0]
    grad_esend, grad_erecv, grad_eout, grad_psend = (pulled[1], pulled[2], pulled[3], pulled[4])
    grad_embed, grad_esend, grad_erecv, grad_eout, grad_psend, grad_precv, grad_pout = lax.psum(
        (grad_embed, grad_esend, grad_erecv, grad_eout, grad_psend, grad_precv, grad_pout), "space"
    )
    return (
        result.astype(jnp.bfloat16),
        grad_embed,
        grad_esend,
        grad_erecv,
        grad_eout,
        grad_psend,
        grad_precv,
        grad_pout,
    )


def solution(mesh):
    return jax.shard_map(
        local,
        mesh=mesh,
        in_specs=(
            P(("groups", "space"), None),
            P(("groups", "space"), None),
            P(("groups", "space"), None),
            P(("groups", "space"), None, None),
            P(("groups", "space"), None),
            P(("groups", "space"), None),
            P(("groups", "space"), None, None),
            P(("groups", "space"), None),
            P(("groups", "space"), None),
            P(),
            P(),
            P(),
            P(),
            P(),
            P(),
            P(),
        ),
        out_specs=(
            P(("groups", "space"), None),
            P("groups", None),
            P("groups", None),
            P("groups", None),
            P("groups", None),
            P("groups", None),
            P("groups", None),
            P("groups", None),
        ),
        check_vma=False,
    )
```

profile of v0, /device:TPU:0, one launch (start us, length us, event | category | flops | bytes accessed | tf_op | source)
XLA Modules:
  0.0 294.2 jit_solution(17043156809280361897)
XLA Ops:
  8.2 2.8 subtract_add_fusion.1
  12.4 7.4 %all-to-all-start = ((bf16[16,8,512]{2,1,0:T(8,128)(2,1)}), bf16[16,8,512]{2,1,0:T(8,128)(2,1)S(1)}, u32[]{:S(2)}, u32[]{:S(2)}) async-start(bf16[16,8,512]{2,1,0:T(8,128)(2,1)} %bitcast.41), calls=%async_computation | async-start | bytes 262144 | tf_op jit(solution)/shard_map/all_to_all | solution.py:75
  22.6 5.1 %all-to-all-done = bf16[16,8,512]{2,1,0:T(8,128)(2,1)S(1)} async-done(((bf16[16,8,512]{2,1,0:T(8,128)(2,1)}), bf16[16,8,512]{2,1,0:T(8,128)(2,1)S(1)}, u32[]{:S(2)}, u32[]{:S(2)}) %all-to-all-start) | async-done | bytes 131104 | tf_op jit(solution)/shard_map/all_to_all | solution.py:75
  29.0 4.9 %gather_fusion.1 = f32[1024,512]{1,0:T(8,128)} fusion(f32[640,512]{1,0:T(8,128)S(1)} %subtract_add_fusion, s32[1024]{0:T(1024)S(1)} %broadcast_clamp_fusion.1), kind=kCustom, calls=%fused_computation.1 | custom fusion | bytes 4198400 | tf_op jit(solution)/shard_map/jvp()/gather | solution.py:39
  33.8 2.6 multiply_reduce_fusion.1
  38.6 4.4 %collective-permute-start.1 = (bf16[64,512]{1,0:T(8,128)(2,1)S(1)}, bf16[64,512]{1,0:T(8,128)(2,1)S(1)}, u32[]{:S(2)}, u32[]{:S(2)}) collective-permute-start(bf16[64,512]{1,0:T(8,128)(2,1)S(1)} %get-tuple-element.45), channel_id=1, source_target_pairs={{1,0},{2,1},{3,2},{4,3},{5,4},{6,5},{7,6},{8,7},{9,8},{10,9},{11,1... | collective-permute-start | bytes 196616 | tf_op jit(solution)/shard_map/ppermute | solution.py:10
  45.0 3.5 %gather_fusion.3 = f32[1024,512]{1,0:T(8,128)S(1)} fusion(f32[192,512]{1,0:T(8,128)S(1)} %pad_maximum_fusion.5, s32[1024]{0:T(1024)S(1)} %broadcast_clamp_fusion), kind=kCustom, calls=%fused_computation.3 | custom fusion | bytes 4198400 | tf_op jit(solution)/shard_map/jvp()/gather | solution.py:39
  52.7 2.0 fusion.31
  54.7 3.2 %fusion.57 = (f32[64,512]{1,0:T(8,128)}, f32[64,16,512]{2,1,0:T(8,128)}) fusion(f32[64,512]{1,0:T(8,128)S(1)} %copy-done.11, f32[64,16]{1,0:T(8,128)S(1)} %copy-done.24, f32[64,512]{1,0:T(8,128)S(1)} %fusion.33, f32[1024,512]{1,0:T(8,128)S(1)} %gather_fusion.3), kind=kLoop, calls=%fused_computation.120 | loop fusion | flops 6258688 | bytes 4591616 | tf_op jit(solution)/shard_map/transpose(jvp())/reduce_sum | solution.py:40
  57.9 7.3 %scatter_custom_fusion = f32[192,512]{1,0:T(8,128)S(1)} fusion(s32[1024]{0:T(1024)S(1)} %reshape.258, f32[1024,512]{1,0:T(8,128)} %bitcast.72, f32[]{:T(128)} %constant.15.clone.1), kind=kCustom, calls=%fused_computation.47 | custom fusion | flops 524288 | bytes 393728 | tf_op jit(solution)/shard_map/transpose(jvp())/scatter-add | solution.py:39
  65.9 4.4 %collective-permute-start.2 = (bf16[64,512]{1,0:T(8,128)(2,1)S(1)}, bf16[64,512]{1,0:T(8,128)(2,1)}, u32[]{:S(2)}, u32[]{:S(2)}) collective-permute-start(bf16[64,512]{1,0:T(8,128)(2,1)S(1)} %get-tuple-element.42), channel_id=1, source_target_pairs={{1,0},{2,1},{3,2},{4,3},{5,4},{6,5},{7,6},{8,7},{9,8},{10,9},{11,1... | collective-permute-start | bytes 196616 | tf_op jit(solution)/shard_map/ppermute | solution.py:10
  70.4 2.9 fusion.68
  73.3 2.5 convolution_add_fusion.1
  76.4 2.8 scatter_custom_fusion.1
  79.2 2.8 scatter_custom_fusion.2
  86.3 3.4 %fusion.54 = (f32[64,512]{1,0:T(8,128)S(1)}, f32[64,16,512]{2,1,0:T(8,128)}) fusion(f32[64,512]{1,0:T(8,128)} %copy-done.10, f32[64,16]{1,0:T(8,128)} %copy-done.23, f32[64,512]{1,0:T(8,128)S(1)} %fusion.29, f32[1024,512]{1,0:T(8,128)S(1)} %copy-done.1), kind=kLoop, calls=%fused_computation.118 | loop fusion | flops 6258688 | bytes 4591616 | tf_op jit(solution)/shard_map/transpose(jvp())/reduce_sum | solution.py:40
  89.7 7.6 %scatter_custom_fusion.3 = f32[640,512]{1,0:T(8,128)S(1)} fusion(s32[1024]{0:T(1024)S(1)} %reshape.242, f32[1024,512]{1,0:T(8,128)} %bitcast.71, f32[]{:T(128)} %constant.15.clone.1), kind=kCustom, calls=%fused_computation.39 | custom fusion | flops 524288 | bytes 1311232 | tf_op jit(solution)/shard_map/transpose(jvp())/scatter-add | solution.py:39
  97.3 4.9 %fusion.4 = f32[512,512]{1,0:T(8,128)} fusion(f32[640,512]{1,0:T(8,128)S(1)} %scatter_custom_fusion.3, f32[128,512]{1,0:T(8,128)S(1)} %bitcast_convert_fusion, f32[512,512]{1,0:T(8,128)} %copy-done.2), kind=kOutput, calls=%fused_computation.31 | convolution fusion | flops 2013593600 | bytes 3670016 | tf_op jit(solution)/shard_map/transpose(jvp())/dot_general | solution.py:18
  108.2 3.5 %all-to-all-start.1 = ((bf16[16,8,512]{2,1,0:T(8,128)(2,1)}), bf16[16,8,512]{2,1,0:T(8,128)(2,1)S(1)}, u32[]{:S(2)}, u32[]{:S(2)}) async-start(bf16[16,8,512]{2,1,0:T(8,128)(2,1)} %fusion.21), calls=%async_computation.1 | async-start | bytes 262144 | tf_op jit(solution)/shard_map/all_to_all | solution.py:116
  113.3 6.2 %all-to-all-done.1 = bf16[16,8,512]{2,1,0:T(8,128)(2,1)S(1)} async-done(((bf16[16,8,512]{2,1,0:T(8,128)(2,1)}), bf16[16,8,512]{2,1,0:T(8,128)(2,1)S(1)}, u32[]{:S(2)}, u32[]{:S(2)}) %all-to-all-start.1) | async-done | bytes 131104 | tf_op jit(solution)/shard_map/all_to_all | solution.py:116
  119.6 2.1 scatter_custom_fusion.4
  121.7 3.6 %convolution_bitcast_fusion.1 = f32[474,512]{1,0:T(8,128)} fusion(bf16[512,474]{0,1:T(8,128)(2,1)S(1)} %copy-done.34, f32[512,512]{1,0:T(8,128)} %get-tuple-element.51, f32[512,512]{1,0:T(8,128)S(1)} %scatter_custom_fusion.4), kind=kOutput, calls=%fused_computation.27 | convolution fusion | flops 1493434368 | bytes 3553280 | tf_op jit(solution)/shard_map/transpose(jvp())/dot_general | solution.py:18
  125.3 153.5 %all-reduce.3.cloned.1.call-done = (f32[474,512]{1,0:T(8,128)}, f32[512,512]{1,0:T(8,128)}, f32[512,512]{0,1:T(8,128)}, f32[512,512]{1,0:T(8,128)}, f32[512,512]...) async-done(((f32[474,512]{1,0:T(8,128)}, f32[512,512]{1,0:T(8,128)}, f32[512,512]{0,1:T(8,128)}, f32[512,512]{1,0:T(8,128)}, f32[512,512]{1,0:T(8,128)}, ...) | async-done | bytes 7262224 | tf_op jit(solution)/shard_map/psum | solution.py:123
  278.9 2.7 copy.35
  (145 shorter events, 33.5 us)
Async XLA Ops:
  7.2 20.6 %copy-start = (bf16[512,512]{1,0:T(8,128)(2,1)S(1)}, bf16[512,512]{1,0:T(8,128)(2,1)}, u32[]{:S(2)}) copy-start(bf16[512,512]{1,0:T(8,128)(2,1)} %param.26) | copy-start | bytes 1572868
  8.1 11.7 %copy-start.30 = (s32[1,2,64]{2,1,0:T(2,128)S(1)}, s32[1,2,64]{2,1,0:T(2,128)}, u32[]{:S(2)}) copy-start(s32[1,2,64]{2,1,0:T(2,128)} %param.22) | copy-start | bytes 1540
  8.1 12.3 %copy-start.25 = (s32[1,16,8]{1,2,0:T(8,128)S(1)}, s32[1,16,8]{1,2,0:T(8,128)}, u32[]{:S(2)}) copy-start(s32[1,16,8]{1,2,0:T(8,128)} %param.19) | copy-start | bytes 1540
  8.1 12.4 %copy-start.26 = (s32[64,16]{0,1:T(8,128)S(1)}, s32[64,16]{0,1:T(8,128)}, u32[]{:S(2)}) copy-start(s32[64,16]{0,1:T(8,128)} %param.20) | copy-start | bytes 12292
  8.1 12.4 %copy-start.27 = (s32[64,16]{0,1:T(8,128)S(1)}, s32[64,16]{0,1:T(8,128)}, u32[]{:S(2)}) copy-start(s32[64,16]{0,1:T(8,128)} %param.23) | copy-start | bytes 12292
  8.2 13.4 %copy-start.28 = (s32[64,16]{0,1:T(8,128)S(1)}, s32[64,16]{0,1:T(8,128)}, u32[]{:S(2)}) copy-start(s32[64,16]{0,1:T(8,128)} %param.21) | copy-start | bytes 12292
  8.2 13.4 %copy-start.29 = (s32[64,16]{0,1:T(8,128)S(1)}, s32[64,16]{0,1:T(8,128)}, u32[]{:S(2)}) copy-start(s32[64,16]{0,1:T(8,128)} %param.24) | copy-start | bytes 12292
  8.2 14.2 %copy-start.19 = (bf16[64,512]{1,0:T(8,128)(2,1)S(1)}, bf16[64,512]{1,0:T(8,128)(2,1)}, u32[]{:S(2)}) copy-start(bf16[64,512]{1,0:T(8,128)(2,1)} %param.17) | copy-start | bytes 196612
  8.2 14.2 %copy-start.22 = (bf16[512,512]{1,0:T(8,128)(2,1)S(1)}, bf16[512,512]{1,0:T(8,128)(2,1)}, u32[]{:S(2)}) copy-start(bf16[512,512]{1,0:T(8,128)(2,1)} %param.27) | copy-start | bytes 1572868
  11.0 18.0 %copy-start.2 = (f32[512,512]{1,0:T(8,128)}, f32[512,512]{1,0:T(8,128)S(1)}, u32[]{:S(2)}) copy-start(f32[512,512]{1,0:T(8,128)S(1)} %get-tuple-element.50) | copy-start | bytes 3145732
  12.4 15.3 %all-to-all-start = ((bf16[16,8,512]{2,1,0:T(8,128)(2,1)}), bf16[16,8,512]{2,1,0:T(8,128)(2,1)S(1)}, u32[]{:S(2)}, u32[]{:S(2)}) async-start(bf16[16,8,512]{2,1,0:T(8,128)(2,1)} %bitcast.41), calls=%async_computation | async-start | bytes 262144 | tf_op jit(solution)/shard_map/all_to_all | solution.py:75
  22.3 11.5 %copy-start.23 = (f32[64,16]{1,0:T(8,128)}, f32[64,16]{1,0:T(8,128)S(1)}, u32[]{:S(2)}) copy-start(f32[64,16]{1,0:T(8,128)S(1)} %copy.31) | copy-start | bytes 12292
  22.6 11.2 %copy-start.10 = (f32[64,512]{1,0:T(8,128)}, f32[64,512]{1,0:T(8,128)S(1)}, u32[]{:S(2)}) copy-start(f32[64,512]{1,0:T(8,128)S(1)} %fusion.64) | copy-start | bytes 393220
  37.2 7.8 %copy-start.33 = (f32[64]{0:T(128)}, f32[64]{0:T(128)S(1)}, u32[]{:S(2)}) copy-start(f32[64]{0:T(128)S(1)} %multiply_reduce_fusion.4) | copy-start | bytes 772
  38.5 6.4 %collective-permute-start = (bf16[64,512]{1,0:T(8,128)(2,1)S(1)}, bf16[64,512]{1,0:T(8,128)(2,1)S(1)}, u32[]{:S(2)}, u32[]{:S(2)}) collective-permute-start(bf16[64,512]{1,0:T(8,128)(2,1)S(1)} %get-tuple-element.44), channel_id=1, source_target_pairs={{15,0},{0,1},{1,2},{2,3},{3,4},{4,5},{5,6},{6,7},{7,8},{8,9},{9,10... | collective-permute-start | bytes 196616 | tf_op jit(solution)/shard_map/ppermute | solution.py:10
  38.6 6.4 %collective-permute-start.1 = (bf16[64,512]{1,0:T(8,128)(2,1)S(1)}, bf16[64,512]{1,0:T(8,128)(2,1)S(1)}, u32[]{:S(2)}, u32[]{:S(2)}) collective-permute-start(bf16[64,512]{1,0:T(8,128)(2,1)S(1)} %get-tuple-element.45), channel_id=1, source_target_pairs={{1,0},{2,1},{3,2},{4,3},{5,4},{6,5},{7,6},{8,7},{9,8},{10,9},{11,1... | collective-permute-start | bytes 196616 | tf_op jit(solution)/shard_map/ppermute | solution.py:10
  65.3 8.0 %copy-start.12 = (f32[64,512]{1,0:T(8,128)S(1)}, f32[64,512]{1,0:T(8,128)}, u32[]{:S(2)}) copy-start(f32[64,512]{1,0:T(8,128)} %get-tuple-element.37) | copy-start | bytes 393220
  65.3 19.1 %copy-start.32 = (f32[64]{0:T(128)S(1)}, f32[64]{0:T(128)}, u32[]{:S(2)}) copy-start(f32[64]{0:T(128)} %copy-done.31) | copy-start | bytes 772
  65.9 13.3 %collective-permute-start.3 = (bf16[64,512]{1,0:T(8,128)(2,1)}, bf16[64,512]{1,0:T(8,128)(2,1)}, u32[]{:S(2)}, u32[]{:S(2)}) collective-permute-start(bf16[64,512]{1,0:T(8,128)(2,1)} %get-tuple-element.41), channel_id=1, source_target_pairs={{15,0},{0,1},{1,2},{2,3},{3,4},{4,5},{5,6},{6,7},{7,8},{8,9},{9,10... | collective-permute-start | bytes 196616 | tf_op jit(solution)/shard_map/ppermute | solution.py:10
  65.9 10.5 %collective-permute-start.2 = (bf16[64,512]{1,0:T(8,128)(2,1)S(1)}, bf16[64,512]{1,0:T(8,128)(2,1)}, u32[]{:S(2)}, u32[]{:S(2)}) collective-permute-start(bf16[64,512]{1,0:T(8,128)(2,1)S(1)} %get-tuple-element.42), channel_id=1, source_target_pairs={{1,0},{2,1},{3,2},{4,3},{5,4},{6,5},{7,6},{8,7},{9,8},{10,9},{11,1... | collective-permute-start | bytes 196616 | tf_op jit(solution)/shard_map/ppermute | solution.py:10
  73.3 13.0 %copy-start.1 = (f32[1024,512]{1,0:T(8,128)S(1)}, f32[1024,512]{1,0:T(8,128)}, u32[]{:S(2)}) copy-start(f32[1024,512]{1,0:T(8,128)} %gather_fusion.1) | copy-start | bytes 6291460
  106.2 15.6 %copy-start.34 = (bf16[512,474]{0,1:T(8,128)(2,1)S(1)}, bf16[512,474]{0,1:T(8,128)(2,1)}, u32[]{:S(2)}) copy-start(bf16[512,474]{0,1:T(8,128)(2,1)} %param.16) | copy-start | bytes 1456132
  108.2 11.4 %all-to-all-start.1 = ((bf16[16,8,512]{2,1,0:T(8,128)(2,1)}), bf16[16,8,512]{2,1,0:T(8,128)(2,1)S(1)}, u32[]{:S(2)}, u32[]{:S(2)}) async-start(bf16[16,8,512]{2,1,0:T(8,128)(2,1)} %fusion.21), calls=%async_computation.1 | async-start | bytes 262144 | tf_op jit(solution)/shard_map/all_to_all | solution.py:116
  111.7 167.2 %all-reduce.3.cloned.1.call-start = ((), (), s32[]{:S(2)}) async-start(), calls=%async_computation.2 | async-start | bytes 14548992 | tf_op jit(solution)/shard_map/psum | solution.py:123
  (18 other events, 60.6 us)
Sparse Core Ops, SparseCore 0:
  125.4 153.3 all-reduce.2
where the time goes:
time: 295 us; the launch traced here: 294 us
  waiting for transfers between devices  166 us (56%)
  other arithmetic  37.9 us (13%)
  matrix products  33.3 us (11%)
  local copies, waits for them, and re-layouts  22.7 us (8%)
  starting transfers between devices  19.9 us (7%)
  between operations  14.6 us (5%)
    psum x1, waiting for transfers between devices, local(): lax.psum((grad_embed, grad_esend, grad_erecv, grad_eout, grad_psend, grad...  154 us
    dot_general x19, matrix products, mul(): jnp.dot(left, right, precision=lax.Precision.HIGHEST, preferred_element_t...  33.3 us
    scatter-add x2, other arithmetic, aggregate(): rows = table[slots]  14.9 us
    ppermute x4, starting transfers between devices, passed_along(): return lax.ppermute(block, axis, route)  8.93 us
    unnamed x78, local copies, waits for them, and re-layouts  8.72 us
    gather x2, local copies, waits for them, and re-layouts, aggregate(): rows = table[slots]  8.36 us
    all_to_all x1, starting transfers between devices, local(): lax.all_to_all(outgoing, 'space', split_axis=0, concat_axis=0, tiled=True)  7.39 us
    reduce_sum x2, other arithmetic, aggregate(): rows + recv_term[:, None, :]  6.55 us
  transfers between devices with their start and end apart: 7, of which 4 were waited for; matrix products, arithmetic and copies ran while one was open for 5% of the time, Pallas kernels for 0%

commit v1 on v0

v1 whole, which is shorter than its diff:
```python
import functools

import jax
import jax.numpy as jnp
from jax import lax
from jax.experimental import pallas as pl
from jax.experimental.pallas import tpu as pltpu
from jax.sharding import PartitionSpec as P

BF = jnp.bfloat16
F32 = jnp.float32
VMEM_BYTES = 40 * 1024 * 1024
BLOCKS = 16


def dot(a, b):
    return lax.dot_general(a, b, (((1,), (0,)), ((), ())), preferred_element_type=F32)


def dot_t(a, b):
    return lax.dot_general(a, b, (((1,), (1,)), ((), ())), preferred_element_type=F32)


def t_dot(a, b):
    return lax.dot_general(a, b, (((0,), (0,)), ((), ())), preferred_element_type=F32)


def sigmoid(v):
    return 0.5 * jnp.tanh(0.5 * v) + 0.5


def silu_slope(v, s):
    return s * (1.0 + v * (1.0 - s))


def normalized(u):
    c = u - jnp.mean(u, axis=-1, keepdims=True)
    r = lax.rsqrt(jnp.mean(c * c, axis=-1, keepdims=True) + 1e-05)
    return c * r, r


def normalized_grad(y, r, g):
    return r * (g - jnp.mean(g, axis=-1, keepdims=True) - y * jnp.mean(g * y, axis=-1, keepdims=True))


def call(body, outs, scratch=(), **kw):
    return pl.pallas_call(
        body,
        out_shape=[jax.ShapeDtypeStruct(s, d) for s, d in outs],
        scratch_shapes=[pltpu.VMEM(s, d) for s, d in scratch],
        compiler_params=pltpu.CompilerParams(vmem_limit_bytes=VMEM_BYTES),
        **kw,
    )


def embed_rows(x, we, ws):
    pre = dot(x, we)
    s = sigmoid(pre)
    lat = (pre * s).astype(BF)
    return lat, silu_slope(pre, s).astype(BF), dot(lat, ws).astype(BF)


def embed_body(x, we, ws, lat, slope, proj):
    lat[...], slope[...], proj[...] = embed_rows(x[...], we[...], ws[...])


def fill_onehot(onehot, slots):
    m, fan = slots.shape
    wide = onehot.shape[1]
    lanes = lax.broadcasted_iota(jnp.int32, (m, wide), 1)
    for f in range(fan):
        onehot[f * m : (f + 1) * m, :] = jnp.where(slots[:, f : f + 1] == lanes, 1.0, 0.0).astype(BF)


def fill_onehot_t(onehot, rows):
    parts, wide = rows.shape
    tall = onehot.shape[0]
    subs = lax.broadcasted_iota(jnp.int32, (tall, wide), 0)
    for p in range(parts):
        onehot[:, p * wide : (p + 1) * wide] = jnp.where(rows[p : p + 1, :] == subs, 1.0, 0.0).astype(BF)


def messages(rows, recv, mask, slope):
    m, fan = mask.shape
    total = None
    for f in range(fan):
        at = slice(f * m, (f + 1) * m)
        v = rows[at, :] + recv
        s = sigmoid(v)
        k = mask[:, f : f + 1].astype(F32)
        slope[at, :] = (silu_slope(v, s) * k).astype(slope.dtype)
        part = v * s * k
        total = part if total is None else total + part
    return total


def encode_body(
    proj, x, we, ws, slots, mask, latent, wrecv, wout, wnext, halo,
    mid, boundary, mesh_proj, agg, y, r, slope, lat_far, slope_far,
    table, onehot, rows,
):
    near = proj.shape[0]
    fill_onehot(onehot, slots)
    table[:near, :] = proj[...]
    lat_far[...], slope_far[...], far = embed_rows(x[...], we[...], ws[...])
    table[near:, :] = far
    rows[...] = dot(onehot[...], table[...])
    recv = dot(latent[...], wrecv[...])
    summed = messages(rows, recv, mask, slope).astype(BF)
    agg[...] = summed
    normed, scale = normalized(dot(summed, wout[...]))
    y[...] = normed
    r[...] = jnp.broadcast_to(scale, r.shape)
    middle = (latent[...].astype(F32) + normed).astype(BF)
    mid[...] = middle
    sent = dot(middle, wnext[...]).astype(BF)
    mesh_proj[...] = sent
    depth = halo.shape[0] // 2
    lanes = lax.broadcasted_iota(jnp.int32, (2 * depth, sent.shape[0]), 1)
    pick = jnp.where(halo[...] == lanes, 1.0, 0.0).astype(BF)
    boundary[...] = dot(pick, sent).astype(BF)


def process_body(
    mesh_proj, left, right, slots, slots_t, mask, mid, wrecv, wout, cotangent,
    out, back, grad_rows, grad_mid, agg, grad_u, grad_recv,
    table, onehot, onehot_t, rows, slope, grad_msg,
):
    m = mesh_proj.shape[0]
    depth = left.shape[0]
    fill_onehot(onehot, slots)
    table[:m, :] = mesh_proj[...]
    table[m : m + depth, :] = left[...]
    table[m + depth : m + 2 * depth, :] = right[...]
    rows[...] = dot(onehot[...], table[...])
    recv = dot(mid[...], wrecv[...])
    summed = messages(rows, recv, mask, slope).astype(BF)
    agg[...] = summed
    normed, scale = normalized(dot(summed, wout[...]))
    out[...] = (mid[...].astype(F32) + normed).astype(BF)
    ct = cotangent[...].astype(F32)
    gu = normalized_grad(normed, scale, ct).astype(BF)
    grad_u[...] = gu
    gagg = dot_t(gu, wout[...])
    gr = message_grads(grad_msg, slope, gagg, mask.shape[1])
    grad_recv[...] = gr
    fill_onehot_t(onehot_t, slots_t)
    grads = dot(onehot_t[...], grad_msg[...])
    grad_rows[...] = grads[:m, :]
    back[...] = grads[m:, :].astype(BF)
    grad_mid[...] = ct + dot_t(gr, wrecv[...])


def message_grads(grad_msg, slope, gagg, fan):
    m = gagg.shape[0]
    total = None
    for f in range(fan):
        at = slice(f * m, (f + 1) * m)
        g = slope[at, :].astype(F32) * gagg
        grad_msg[at, :] = g.astype(BF)
        total = g if total is None else total + g
    return total.astype(BF)


def block_of(place, me, order):
    flips = 0
    for i, step in enumerate(order):
        if place >> (len(order) - 1 - i) & 1:
            flips ^= step
    return me ^ flips


def spread(me, order, grads, keep, send):
    deep = grads[0].shape[0] // BLOCKS
    half = BLOCKS // 2
    for place in range(BLOCKS):
        at = pl.multiple_of(block_of(place, me, order) * deep, deep)
        for g, grad in enumerate(grads):
            rows = grad[pl.ds(at, deep), :]
            to = ((place % half) * len(grads) + g) * deep
            if place < half:
                keep[to : to + deep, :] = rows
            else:
                send[to : to + deep, :] = rows.astype(BF)


def process_grads_body(order, me, agg, grad_u, mid, grad_recv, keep, send, one, two):
    one[...] = t_dot(agg[...], grad_u[...])
    two[...] = t_dot(mid[...], grad_recv[...])
    spread(me[0], order, (one, two), keep, send)


def encode_grads_body(
    order, me, back_left, back_right, halo_t, grad_rows, grad_mid, mid, wnext,
    y, r, agg, wout, slope, slots_t, latent, lat, lat_far, ws, slope_near, slope_far, x, x_far,
    keep, send,
    onehot_t, grad_msg, g_next, g_out, g_recv, g_send, g_embed,
):
    m = mid.shape[0]
    fill_onehot_t(onehot_t, slots_t)
    subs = lax.broadcasted_iota(jnp.int32, (m, halo_t.shape[1]), 0)
    to_left = jnp.where(halo_t[0:1, :] == subs, 1.0, 0.0).astype(BF)
    to_right = jnp.where(halo_t[1:2, :] == subs, 1.0, 0.0).astype(BF)
    gp = (grad_rows[...] + dot(to_right, back_right[...]) + dot(to_left, back_left[...])).astype(BF)
    g_next[...] = t_dot(mid[...], gp)
    gmid = grad_mid[...] + dot_t(gp, wnext[...])
    gu = normalized_grad(y[...], r[:, 0:1], gmid).astype(BF)
    g_out[...] = t_dot(agg[...], gu)
    gagg = dot_t(gu, wout[...])
    gr = message_grads(grad_msg, slope, gagg, grad_msg.shape[0] // m)
    g_recv[...] = t_dot(latent[...], gr)
    gtab = dot(onehot_t[...], grad_msg[...]).astype(BF)
    near = lat.shape[0]
    g_near, g_far = gtab[:near, :], gtab[near:, :]
    g_send[...] = t_dot(lat[...], g_near) + t_dot(lat_far[...], g_far)
    p_near = (dot_t(g_near, ws[...]) * slope_near[...].astype(F32)).astype(BF)
    p_far = (dot_t(g_far, ws[...]) * slope_far[...].astype(F32)).astype(BF)
    fin = x.shape[1]
    tail = fin // 32 * 32
    g_embed[tail:, :] = jnp.zeros((g_embed.shape[0] - tail, g_embed.shape[1]), F32)
    g_embed[:fin, :] = t_dot(x[...], p_near) + t_dot(x_far[...], p_far)
    spread(me[0], order, (g_next, g_out, g_recv, g_send, g_embed), keep, send)


def collect_body(order, counts, *refs):
    me = refs[0][0]
    n_outs = sum(counts)
    ins = refs[1 : 1 + 2 * len(counts)]
    outs = refs[1 + 2 * len(counts) : 1 + 2 * len(counts) + n_outs]
    whole = refs[-1]
    half = BLOCKS // 2
    base = 0
    for i, count in enumerate(counts):
        for place in range(BLOCKS):
            source = ins[2 * i + place // half]
            block = block_of(place, me, order)
            for g in range(count):
                out = outs[base + g]
                short = out.shape[0] != whole.shape[0]
                deep = whole.shape[0] // BLOCKS
                at = pl.multiple_of(block * deep, deep)
                frm = ((place % half) * count + g) * deep
                (whole if short else out)[pl.ds(at, deep), :] = source[frm : frm + deep, :].astype(F32)
        for g in range(count):
            out = outs[base + g]
            if out.shape[0] != whole.shape[0]:
                out[...] = whole[: out.shape[0], :]
        base += count


def exchange(value, step):
    n = lax.axis_size("space")
    return lax.ppermute(value, "space", [(i, i ^ step) for i in range(n)])


def all_sum(keep, send, order, rest):
    for i, step in enumerate(order):
        kept = keep + exchange(send, step).astype(F32)
        if i + 1 < len(order):
            half = kept.shape[0] // 2
            keep, send = kept[:half], kept[half:].astype(BF)
    value = kept.astype(BF)
    for step in rest:
        value = (value.astype(F32) + exchange(value, step).astype(F32)).astype(BF)
    for step in order[:0:-1]:
        value = jnp.concatenate([value, exchange(value, step)], axis=0)
    return value, exchange(value, order[0])


def passed_along(block, distance):
    n = lax.axis_size("space")
    return lax.ppermute(block, "space", [((i - distance) % n, i) for i in range(n)])


SMEM = pl.BlockSpec(memory_space=pltpu.SMEM)
VMEM = pl.BlockSpec(memory_space=pltpu.VMEM)


def local(
    grid_inputs, mesh_latent, cotangent, send_list, enc_slot, enc_mask, halo_list, proc_slot, proc_mask,
    w_embed, enc_send, enc_recv, enc_out, proc_send, proc_recv, proc_out,
):
    n = lax.axis_size("space")
    me = lax.axis_index("space").astype(jnp.int32)
    bits = [1 << i for i in range(n.bit_length() - 1)]
    order, rest = tuple(bits[:4]), tuple(bits[4:])
    mine = (me & (BLOCKS - 1)).reshape(1)
    near, fin = grid_inputs.shape
    m, width = mesh_latent.shape
    edges_e = m * enc_slot.shape[1]
    edges_p = m * proc_slot.shape[1]
    depth = halo_list.shape[2]
    far = send_list.shape[1] * send_list.shape[2]
    enc_rows = enc_slot.T.reshape(-1, 128)
    proc_rows = proc_slot.T.reshape(-1, 128)
    halo = halo_list[0]

    outgoing = grid_inputs[send_list[0]]
    incoming = lax.all_to_all(outgoing, "space", split_axis=0, concat_axis=0, tiled=True)
    x_far = incoming.reshape(far, fin)

    lat, slope_near, proj = call(embed_body, [((near, width), BF)] * 3)(grid_inputs, w_embed, enc_send)

    mid, boundary, mesh_proj, agg, y, r, slope, lat_far, slope_far = call(
        encode_body,
        [((m, width), BF), ((2 * depth, width), BF), ((m, width), BF), ((m, width), BF), ((m, width), F32),
         ((m, 128), F32), ((edges_e, width), BF), ((far, width), BF), ((far, width), BF)],
        [((near + far, width), BF), ((edges_e, near + far), BF), ((edges_e, width), F32)],
    )(proj, x_far, w_embed, enc_send, enc_slot, enc_mask, mesh_latent, enc_recv, enc_out, proc_send,
      halo.reshape(-1, 1))

    from_left = passed_along(boundary[depth:], 1)
    from_right = passed_along(boundary[:depth], -1)

    wide = m + 2 * depth
    out, back, grad_rows, grad_mid, agg2, grad_u, grad_recv = call(
        process_body,
        [((m, width), BF), ((2 * depth, width), BF), ((m, width), F32), ((m, width), F32), ((m, width), BF),
         ((m, width), BF), ((m, width), BF)],
        [((wide, width), BF), ((edges_p, wide), BF), ((wide, edges_p), BF), ((edges_p, width), F32),
         ((edges_p, width), F32), ((edges_p, width), BF)],
    )(mesh_proj, from_left, from_right, proc_slot, proc_rows, proc_mask, mid, proc_recv, proc_out, cotangent)

    back_right = passed_along(back[:depth], -1)
    back_left = passed_along(back[depth:], 1)

    def halves(count):
        rows = count * width // 2
        return [((rows, width), F32), ((rows, width), BF)]

    square = ((width, width), F32)
    keep_p, send_p = call(
        functools.partial(process_grads_body, order), halves(2), [square] * 2, in_specs=[SMEM] + [VMEM] * 4
    )(mine, agg2, grad_u, mid, grad_recv)
    first = all_sum(keep_p, send_p, order, rest)

    keep_e, send_e = call(
        functools.partial(encode_grads_body, order),
        halves(5),
        [((near + far, edges_e), BF), ((edges_e, width), BF)] + [square] * 5,
        in_specs=[SMEM] + [VMEM] * 21,
    )(mine, back_left, back_right, halo, grad_rows, grad_mid, mid, proc_send, y, r, agg, enc_out, slope, enc_rows,
      mesh_latent, lat, lat_far, enc_send, slope_near, slope_far, grid_inputs, x_far)
    second = all_sum(keep_e, send_e, order, rest)

    counts = (2, 5)
    g_pout, g_precv, g_psend, g_eout, g_erecv, g_esend, g_embed = call(
        functools.partial(collect_body, order, counts),
        [square] * 6 + [((fin, width), F32)],
        [square],
        in_specs=[SMEM] + [VMEM] * 4,
    )(mine, *first, *second)
    return out, g_embed, g_esend, g_erecv, g_eout, g_psend, g_precv, g_pout


def solution(mesh):
    rows = P(("groups", "space"), None)
    lists = P(("groups", "space"), None, None)
    return jax.shard_map(
        local,
        mesh=mesh,
        in_specs=(rows, rows, rows, lists, rows, rows, lists, rows, rows) + (P(),) * 7,
        out_specs=(rows,) + (P("groups", None),) * 7,
        check_vma=False,
    )
```

time: 295 us -> 145 us (0.49)
  waiting for transfers between devices: 166 us -> 92 us
  other arithmetic: 37.9 us -> 2.02 us
  matrix products: 33.3 us -> 0 us
  Pallas kernels: 0 us -> 14.1 us
  between operations: 14.6 us -> 1.16 us
  local copies, waits for them, and re-layouts: 22.7 us -> 18.7 us
  starting transfers between devices: 19.9 us -> 16.5 us
    psum x1 -> x0, waiting for transfers between devices: 154 us -> none  [local(): lax.psum((grad_embed, grad_esend, grad_erecv, grad_eout, grad_psend, grad...]
    ppermute x4 -> x20, waiting for transfers between devices: 0.9 us -> 87.9 us  [the longest x16 76.4 us: exchange(): return lax.ppermute(value, 'space', [(i, i ^ step) for i in range(n)])]
    dot_general x19 -> x0, matrix products: 33.3 us -> none  [mul(): jnp.dot(left, right, precision=lax.Precision.HIGHEST, preferred_element_t...]
    scatter-add x5 -> x0, other arithmetic: 22.6 us -> none  [the longest x2 14.9 us: aggregate(): rows = table[slots]]
    pallas_call x0 -> x6, Pallas kernels: none -> 14.1 us  [the longest x1 3.83 us: local(): call(functools.partial(encode_grads_body, order), halves(5), [((near + fa...]
    reduce_sum x8 -> x0, other arithmetic: 12.5 us -> none  [the longest x2 6.55 us: aggregate(): rows + recv_term[:, None, :]]
    gather x4 -> x1, local copies, waits for them, and re-layouts: 10.5 us -> 1.5 us  [local(): outgoing = grid_inputs[send_list[0]]]
    unnamed x78 -> x77, local copies, waits for them, and re-layouts: 8.72 us -> 15.9 us
  transfers between devices with their start and end apart: 7 -> 21, of which waited for: 4 -> 17; matrix products, arithmetic and copies ran while one was open for 5% -> 1% of each run, Pallas kernels for 0% -> 1%
where the time goes in v1:
time: 145 us; the launch traced here: 144 us
  waiting for transfers between devices  92 us (63%)
  local copies, waits for them, and re-layouts  18.7 us (13%)
  starting transfers between devices  16.5 us (11%)
  Pallas kernels  14.1 us (10%)
  other arithmetic  2.02 us (1%)
    ppermute x16, waiting for transfers between devices, exchange(): return lax.ppermute(value, 'space', [(i, i ^ step) for i in range(n)])  76.4 us
    unnamed x77, local copies, waits for them, and re-layouts  15.9 us
    ppermute x4, waiting for transfers between devices, passed_along(): lax.ppermute(block, 'space', [((i - distance) % n, i) for i in range(n)])  11.5 us
    ppermute x16, starting transfers between devices, exchange(): return lax.ppermute(value, 'space', [(i, i ^ step) for i in range(n)])  7.83 us
    all_to_all x1, starting transfers between devices, local(): lax.all_to_all(outgoing, 'space', split_axis=0, concat_axis=0, tiled=True)  7.39 us
    all_to_all x1, waiting for transfers between devices, local(): lax.all_to_all(outgoing, 'space', split_axis=0, concat_axis=0, tiled=True)  4.1 us
    pallas_call x1, Pallas kernels, local(): call(functools.partial(encode_grads_body, order), halves(5), [((near + fa...  3.83 us
    pallas_call x1, Pallas kernels, local(): call(functools.partial(collect_body, order, counts), [square] * 6 + [((fi...  3.03 us
  transfers between devices with their start and end apart: 21, of which 17 were waited for; matrix products, arithmetic and copies ran while one was open for 1% of the time, Pallas kernels for 1%

profile of v1, /device:TPU:0, one launch (start us, length us, event | category | flops | bytes accessed | tf_op | source)
XLA Modules:
  0.0 144.5 jit_solution(15610295800832417775)
XLA Ops:
  1.6 1.3 copy.33.x
  2.9 1.5 %gather_fusion = bf16[128,474]{1,0:T(8,128)(2,1)} fusion(bf16[512,474]{1,0:T(8,128)(2,1)S(1)} %copy.33.x, s32[1024]{0:T(1024)S(1)} %pad_clamp_fusion), kind=kCustom, calls=%fused_computation | custom fusion | bytes 243200 | tf_op jit(solution)/shard_map/gather | solution.py:298
  4.5 7.4 %all-to-all-start = ((bf16[16,8,474]{2,1,0:T(8,128)(2,1)}), bf16[16,8,474]{2,1,0:T(8,128)(2,1)S(1)}, u32[]{:S(2)}, u32[]{:S(2)}) async-start(bf16[16,8,474]{2,1,0:T(8,128)(2,1)} %bitcast.1), calls=%async_computation | async-start | bytes 262144 | tf_op jit(solution)/shard_map/all_to_all | solution.py:299
  15.7 4.1 %all-to-all-done = bf16[16,8,474]{2,1,0:T(8,128)(2,1)S(1)} async-done(((bf16[16,8,474]{2,1,0:T(8,128)(2,1)}), bf16[16,8,474]{2,1,0:T(8,128)(2,1)S(1)}, u32[]{:S(2)}, u32[]{:S(2)}) %all-to-all-start) | async-done | bytes 121376 | tf_op jit(solution)/shard_map/all_to_all | solution.py:299
  20.8 2.9 %shard_map.216 = (bf16[64,512]{1,0:T(8,128)(2,1)S(1)}, bf16[128,512]{1,0:T(8,128)(2,1)S(1)}, bf16[64,512]{1,0:T(8,128)(2,1)S(1)}, bf16[64,512]{1,0:T(8,128)(2,1)...) custom-call(bf16[512,512]{1,0:T(8,128)(2,1)S(1)} %copy-done.10, ...), custom_call_target="tpu_custom_call" | custom-call | tf_op jit(solution)/shard_map/pallas_call | solution.py:304
  29.4 4.5 %collective-permute-done.left = bf16[64,512]{1,0:T(8,128)(2,1)S(1)} collective-permute-done((bf16[64,512]{1,0:T(8,128)(2,1)S(1)}, bf16[64,512]{1,0:T(8,128)(2,1)S(1)}, u32[]{:S(2)}, u32[]{:S(2)}) %collective-permute-start) | collective-permute-done | bytes 65568 | tf_op jit(solution)/shard_map/ppermute | solution.py:272
  37.6 2.8 %shard_map.217 = (bf16[64,512]{1,0:T(8,128)(2,1)}, bf16[128,512]{1,0:T(8,128)(2,1)S(1)}, f32[64,512]{1,0:T(8,128)S(1)}, f32[64,512]{1,0:T(8,128)S(1)}, bf16[64,5...) custom-call(bf16[64,512]{1,0:T(8,128)(2,1)S(1)} %copy-done.26, ...), custom_call_target="tpu_custom_call" | custom-call | tf_op jit(solution)/shard_map/pallas_call | solution.py:316
  41.6 1.6 %collective-permute-done.11.back_right = bf16[64,512]{1,0:T(8,128)(2,1)S(1)} collective-permute-done((bf16[64,512]{1,0:T(8,128)(2,1)}, bf16[64,512]{1,0:T(8,128)(2,1)S(1)}, u32[]{:S(2)}, u32[]{:S(2)}) %collective-permute-start.11) | collective-permute-done | bytes 65568 | tf_op jit(solution)/shard_map/ppermute | solution.py:272
  43.3 4.4 %collective-permute-done.10.back_left = bf16[64,512]{1,0:T(8,128)(2,1)S(1)} collective-permute-done((bf16[64,512]{1,0:T(8,128)(2,1)S(1)}, bf16[64,512]{1,0:T(8,128)(2,1)S(1)}, u32[]{:S(2)}, u32[]{:S(2)}) %collective-permute-start.10) | collective-permute-done | bytes 65568 | tf_op jit(solution)/shard_map/ppermute | solution.py:272
  51.0 3.8 %shard_map.219 = (f32[1280,512]{1,0:T(8,128)S(1)}, bf16[1280,512]{1,0:T(8,128)(2,1)S(1)}) custom-call(s32[1]{0:T(128)} %bitcast.4.me.refs_0_, bf16[64,512]{1,0:T(8,128)(2,1)S(1)} %collective-permute-done.10.back_left, bf16[64,512]{1,0:T(8,128)(2,1)S(1)} %collective-permute-done.11.back_right, s32[2,64]{1,0:T(2,128)S(1)} %bitcast.12, ...), custom_call_target="tpu_custom_call" | custom-call | tf_op jit(solution)/shard_map/pallas_call | solution.py:337
  54.9 3.0 %collective-permute-done.12 = bf16[1280,512]{1,0:T(8,128)(2,1)S(1)} collective-permute-done((bf16[1280,512]{1,0:T(8,128)(2,1)S(1)}, bf16[1280,512]{1,0:T(8,128)(2,1)S(1)}, u32[]{:S(2)}, u32[]{:S(2)}) %collective-permute-start.12) | collective-permute-done | bytes 1310752 | tf_op jit(solution)/shard_map/ppermute | solution.py:253
  58.6 16.8 %collective-permute-done.13 = bf16[640,512]{1,0:T(8,128)(2,1)S(1)} collective-permute-done((bf16[640,512]{1,0:T(8,128)(2,1)S(1)}, bf16[640,512]{1,0:T(8,128)(2,1)S(1)}, u32[]{:S(2)}, u32[]{:S(2)}) %collective-permute-start.13) | collective-permute-done | bytes 655392 | tf_op jit(solution)/shard_map/ppermute | solution.py:253
  76.3 8.3 %collective-permute-done.14 = bf16[320,512]{1,0:T(8,128)(2,1)S(1)} collective-permute-done((bf16[320,512]{1,0:T(8,128)(2,1)S(1)}, bf16[320,512]{1,0:T(8,128)(2,1)S(1)}, u32[]{:S(2)}, u32[]{:S(2)}) %collective-permute-start.14) | collective-permute-done | bytes 327712 | tf_op jit(solution)/shard_map/ppermute | solution.py:253
  84.8 8.9 %collective-permute-done.15 = bf16[160,512]{1,0:T(8,128)(2,1)S(1)} collective-permute-done((bf16[160,512]{1,0:T(8,128)(2,1)S(1)}, bf16[160,512]{1,0:T(8,128)(2,1)S(1)}, u32[]{:S(2)}, u32[]{:S(2)}) %collective-permute-start.15) | collective-permute-done | bytes 163872 | tf_op jit(solution)/shard_map/ppermute | solution.py:253
  95.1 6.0 %collective-permute-done.16 = bf16[160,512]{1,0:T(8,128)(2,1)S(1)} collective-permute-done((bf16[160,512]{1,0:T(8,128)(2,1)S(1)}, bf16[160,512]{1,0:T(8,128)(2,1)S(1)}, u32[]{:S(2)}, u32[]{:S(2)}) %collective-permute-start.16) | collective-permute-done | bytes 163872 | tf_op jit(solution)/shard_map/ppermute | solution.py:253
  102.0 1.4 collective-permute-start.4
  103.4 8.1 %collective-permute-done.17 = bf16[320,512]{1,0:T(8,128)(2,1)S(1)} collective-permute-done((bf16[320,512]{1,0:T(8,128)(2,1)S(1)}, bf16[320,512]{1,0:T(8,128)(2,1)S(1)}, u32[]{:S(2)}, u32[]{:S(2)}) %collective-permute-start.17) | collective-permute-done | bytes 327712 | tf_op jit(solution)/shard_map/ppermute | solution.py:253
  113.8 4.8 %collective-permute-done.5 = bf16[64,512]{1,0:T(8,128)(2,1)S(1)} collective-permute-done((bf16[64,512]{1,0:T(8,128)(2,1)S(1)}, bf16[64,512]{1,0:T(8,128)(2,1)S(1)}, u32[]{:S(2)}, u32[]{:S(2)}) %collective-permute-start.5) | collective-permute-done | bytes 65568 | tf_op jit(solution)/shard_map/ppermute | solution.py:253
  119.1 6.1 %collective-permute-done.18 = bf16[640,512]{1,0:T(8,128)(2,1)S(1)} collective-permute-done((bf16[640,512]{1,0:T(8,128)(2,1)S(1)}, bf16[640,512]{1,0:T(8,128)(2,1)S(1)}, u32[]{:S(2)}, u32[]{:S(2)}) %collective-permute-start.18) | collective-permute-done | bytes 655392 | tf_op jit(solution)/shard_map/ppermute | solution.py:253
  126.1 5.3 %collective-permute-done.7 = bf16[128,512]{1,0:T(8,128)(2,1)S(1)} collective-permute-done((bf16[128,512]{1,0:T(8,128)(2,1)S(1)}, bf16[128,512]{1,0:T(8,128)(2,1)S(1)}, u32[]{:S(2)}, u32[]{:S(2)}) %collective-permute-start.7) | collective-permute-done | bytes 131104 | tf_op jit(solution)/shard_map/ppermute | solution.py:253
  131.4 1.5 %collective-permute-start.8 = (bf16[256,512]{1,0:T(8,128)(2,1)S(1)}, bf16[256,512]{1,0:T(8,128)(2,1)S(1)}, u32[]{:S(2)}, u32[]{:S(2)}) collective-permute-start(bf16[256,512]{1,0:T(8,128)(2,1)S(1)} %pad_maximum_fusion.4), channel_id=1, source_target_pairs={{0,2},{1,3},{2,0},{3,1},{4,6},{5,7},{6,4},{7,5},{8,10},{9,11},{10,... | collective-permute-start | bytes 786440 | tf_op jit(solution)/shard_map/ppermute | solution.py:253
  132.9 6.5 %collective-permute-done.8 = bf16[256,512]{1,0:T(8,128)(2,1)S(1)} collective-permute-done((bf16[256,512]{1,0:T(8,128)(2,1)S(1)}, bf16[256,512]{1,0:T(8,128)(2,1)S(1)}, u32[]{:S(2)}, u32[]{:S(2)}) %collective-permute-start.8) | collective-permute-done | bytes 262176 | tf_op jit(solution)/shard_map/ppermute | solution.py:253
  139.5 1.9 %collective-permute-done.9.refs_2_ = bf16[512,512]{1,0:T(8,128)(2,1)S(1)} collective-permute-done((bf16[512,512]{1,0:T(8,128)(2,1)S(1)}, bf16[512,512]{1,0:T(8,128)(2,1)S(1)}, u32[]{:S(2)}, u32[]{:S(2)}) %collective-permute-start.9) | collective-permute-done | bytes 524320 | tf_op jit(solution)/shard_map/ppermute | solution.py:253
  141.4 3.0 %shard_map.220 = (f32[512,512]{1,0:T(8,128)}, f32[512,512]{1,0:T(8,128)}, f32[512,512]{1,0:T(8,128)}, f32[512,512]{1,0:T(8,128)}, f32[512,512]{1,0:T(8,128)}, /*index=5*/f32[512,512]{1,0:T(8,128)}, f32[474,512]{1,0:T(8,128)}) custom-call(s32[1]{0:T(128)} %bitcast.4.me.refs_0_, bf16[512,512]{1,0:T(8,128)(2,1)S(1)} %pad_maximum_fusion.2.refs_1_, ...), custom_call_target="tpu_custom_call" | custom-call | tf_op jit(solution)/shard_map/pallas_call | solution.py:347
  (131 shorter events, 27.3 us)
Async XLA Ops:
  4.5 15.3 %all-to-all-start = ((bf16[16,8,474]{2,1,0:T(8,128)(2,1)}), bf16[16,8,474]{2,1,0:T(8,128)(2,1)S(1)}, u32[]{:S(2)}, u32[]{:S(2)}) async-start(bf16[16,8,474]{2,1,0:T(8,128)(2,1)} %bitcast.1), calls=%async_computation | async-start | bytes 262144 | tf_op jit(solution)/shard_map/all_to_all | solution.py:299
  26.7 21.0 %copy-start.17 = (f32[64,512]{1,0:T(8,128)S(1)}, f32[64,512]{1,0:T(8,128)}, u32[]{:S(2)}) copy-start(f32[64,512]{1,0:T(8,128)} %copy-done.16) | copy-start | bytes 393220
  26.7 21.0 %copy-start.19 = (bf16[128,512]{1,0:T(8,128)(2,1)S(1)}, bf16[128,512]{1,0:T(8,128)(2,1)}, u32[]{:S(2)}) copy-start(bf16[128,512]{1,0:T(8,128)(2,1)} %copy-done.18) | copy-start | bytes 393220
  26.7 2.7 %collective-permute-start.1 = (bf16[64,512]{1,0:T(8,128)(2,1)S(1)}, bf16[64,512]{1,0:T(8,128)(2,1)S(1)}, u32[]{:S(2)}, u32[]{:S(2)}) collective-permute-start(bf16[64,512]{1,0:T(8,128)(2,1)S(1)} %get-tuple-element.70), channel_id=1, source_target_pairs={{1,0},{2,1},{3,2},{4,3},{5,4},{6,5},{7,6},{8,7},{9,8},{10,9},{11,1... | collective-permute-start | bytes 196616 | tf_op jit(solution)/shard_map/ppermute | solution.py:272
  27.5 6.4 %collective-permute-start = (bf16[64,512]{1,0:T(8,128)(2,1)S(1)}, bf16[64,512]{1,0:T(8,128)(2,1)S(1)}, u32[]{:S(2)}, u32[]{:S(2)}) collective-permute-start(bf16[64,512]{1,0:T(8,128)(2,1)S(1)} %get-tuple-element.71), channel_id=1, source_target_pairs={{15,0},{0,1},{1,2},{2,3},{3,4},{4,5},{5,6},{6,7},{7,8},{8,9},{9,10... | collective-permute-start | bytes 196616 | tf_op jit(solution)/shard_map/ppermute | solution.py:272
  27.5 20.2 %copy-start.23 = (bf16[64,512]{1,0:T(8,128)(2,1)S(1)}, bf16[64,512]{1,0:T(8,128)(2,1)}, u32[]{:S(2)}) copy-start(bf16[64,512]{1,0:T(8,128)(2,1)} %copy-done.22) | copy-start | bytes 196612
  41.0 2.2 %collective-permute-start.11 = (bf16[64,512]{1,0:T(8,128)(2,1)}, bf16[64,512]{1,0:T(8,128)(2,1)S(1)}, u32[]{:S(2)}, u32[]{:S(2)}) collective-permute-start(bf16[64,512]{1,0:T(8,128)(2,1)} %get-tuple-element.68), channel_id=1, source_target_pairs={{1,0},{2,1},{3,2},{4,3},{5,4},{6,5},{7,6},{8,7},{9,8},{10,9},{11,1... | collective-permute-start | bytes 196616 | tf_op jit(solution)/shard_map/ppermute | solution.py:272
  41.1 6.6 %collective-permute-start.10 = (bf16[64,512]{1,0:T(8,128)(2,1)S(1)}, bf16[64,512]{1,0:T(8,128)(2,1)S(1)}, u32[]{:S(2)}, u32[]{:S(2)}) collective-permute-start(bf16[64,512]{1,0:T(8,128)(2,1)S(1)} %get-tuple-element.69), channel_id=1, source_target_pairs={{15,0},{0,1},{1,2},{2,3},{3,4},{4,5},{5,6},{6,7},{7,8},{8,9},{9,10... | collective-permute-start | bytes 196616 | tf_op jit(solution)/shard_map/ppermute | solution.py:272
  54.9 3.1 %collective-permute-start.12 = (bf16[1280,512]{1,0:T(8,128)(2,1)S(1)}, bf16[1280,512]{1,0:T(8,128)(2,1)S(1)}, u32[]{:S(2)}, u32[]{:S(2)}) collective-permute-start(bf16[1280,512]{1,0:T(8,128)(2,1)S(1)} %get-tuple-element.60), channel_id=1, source_target_pairs={{0,1},{1,0},{2,3},{3,2},{4,5},{5,4},{6,7},{7,6},{8,9},{9,8},{10,11... | collective-permute-start | bytes 3932168 | tf_op jit(solution)/shard_map/ppermute | solution.py:253
  58.5 16.8 %collective-permute-start.13 = (bf16[640,512]{1,0:T(8,128)(2,1)S(1)}, bf16[640,512]{1,0:T(8,128)(2,1)S(1)}, u32[]{:S(2)}, u32[]{:S(2)}) collective-permute-start(bf16[640,512]{1,0:T(8,128)(2,1)S(1)} %slice.100), channel_id=1, source_target_pairs={{0,2},{1,3},{2,0},{3,1},{4,6},{5,7},{6,4},{7,5},{8,10},{9,11},{10,... | collective-permute-start | bytes 1966088 | tf_op jit(solution)/shard_map/ppermute | solution.py:253
  75.6 9.0 %collective-permute-start.14 = (bf16[320,512]{1,0:T(8,128)(2,1)S(1)}, bf16[320,512]{1,0:T(8,128)(2,1)S(1)}, u32[]{:S(2)}, u32[]{:S(2)}) collective-permute-start(bf16[320,512]{1,0:T(8,128)(2,1)S(1)} %slice.101), channel_id=1, source_target_pairs={{0,4},{1,5},{2,6},{3,7},{4,0},{5,1},{6,2},{7,3},{8,12},{9,13},{10,... | collective-permute-start | bytes 983048 | tf_op jit(solution)/shard_map/ppermute | solution.py:253
  76.3 17.6 %collective-permute-start.2 = (bf16[512,512]{1,0:T(8,128)(2,1)S(1)}, bf16[512,512]{1,0:T(8,128)(2,1)S(1)}, u32[]{:S(2)}, u32[]{:S(2)}) collective-permute-start(bf16[512,512]{1,0:T(8,128)(2,1)S(1)} %get-tuple-element.47), channel_id=1, source_target_pairs={{0,1},{1,0},{2,3},{3,2},{4,5},{5,4},{6,7},{7,6},{8,9},{9,8},{10,11... | collective-permute-start | bytes 1572872 | tf_op jit(solution)/shard_map/ppermute | solution.py:253
  84.8 9.0 %collective-permute-start.15 = (bf16[160,512]{1,0:T(8,128)(2,1)S(1)}, bf16[160,512]{1,0:T(8,128)(2,1)S(1)}, u32[]{:S(2)}, u32[]{:S(2)}) collective-permute-start(bf16[160,512]{1,0:T(8,128)(2,1)S(1)} %slice.103), channel_id=1, source_target_pairs={{0,8},{1,9},{2,10},{3,11},{4,12},{5,13},{6,14},{7,15},{8,0},{9,1},... | collective-permute-start | bytes 491528 | tf_op jit(solution)/shard_map/ppermute | solution.py:253
  93.8 7.3 %collective-permute-start.16 = (bf16[160,512]{1,0:T(8,128)(2,1)S(1)}, bf16[160,512]{1,0:T(8,128)(2,1)S(1)}, u32[]{:S(2)}, u32[]{:S(2)}) collective-permute-start(bf16[160,512]{1,0:T(8,128)(2,1)S(1)} %fusion), channel_id=1, source_target_pairs={{0,8},{1,9},{2,10},{3,11},{4,12},{5,13},{6,14},{7,15},{8,0},{9,1},... | collective-permute-start | bytes 491528 | tf_op jit(solution)/shard_map/ppermute | solution.py:253
  94.1 7.8 %collective-permute-start.3 = (bf16[256,512]{1,0:T(8,128)(2,1)S(1)}, bf16[256,512]{1,0:T(8,128)(2,1)S(1)}, u32[]{:S(2)}, u32[]{:S(2)}) collective-permute-start(bf16[256,512]{1,0:T(8,128)(2,1)S(1)} %slice.102), channel_id=1, source_target_pairs={{0,2},{1,3},{2,0},{3,1},{4,6},{5,7},{6,4},{7,5},{8,10},{9,11},{10,... | collective-permute-start | bytes 786440 | tf_op jit(solution)/shard_map/ppermute | solution.py:253
  101.1 10.4 %collective-permute-start.17 = (bf16[320,512]{1,0:T(8,128)(2,1)S(1)}, bf16[320,512]{1,0:T(8,128)(2,1)S(1)}, u32[]{:S(2)}, u32[]{:S(2)}) collective-permute-start(bf16[320,512]{1,0:T(8,128)(2,1)S(1)} %pad_maximum_fusion.3), channel_id=1, source_target_pairs={{0,4},{1,5},{2,6},{3,7},{4,0},{5,1},{6,2},{7,3},{8,12},{9,13},{10,... | collective-permute-start | bytes 983048 | tf_op jit(solution)/shard_map/ppermute | solution.py:253
  102.0 11.0 %collective-permute-start.4 = (bf16[128,512]{1,0:T(8,128)(2,1)S(1)}, bf16[128,512]{1,0:T(8,128)(2,1)S(1)}, u32[]{:S(2)}, u32[]{:S(2)}) collective-permute-start(bf16[128,512]{1,0:T(8,128)(2,1)S(1)} %slice.104), channel_id=1, source_target_pairs={{0,4},{1,5},{2,6},{3,7},{4,0},{5,1},{6,2},{7,3},{8,12},{9,13},{10,... | collective-permute-start | bytes 393224 | tf_op jit(solution)/shard_map/ppermute | solution.py:253
  111.6 13.7 %collective-permute-start.18 = (bf16[640,512]{1,0:T(8,128)(2,1)S(1)}, bf16[640,512]{1,0:T(8,128)(2,1)S(1)}, u32[]{:S(2)}, u32[]{:S(2)}) collective-permute-start(bf16[640,512]{1,0:T(8,128)(2,1)S(1)} %pad_maximum_fusion.1), channel_id=1, source_target_pairs={{0,2},{1,3},{2,0},{3,1},{4,6},{5,7},{6,4},{7,5},{8,10},{9,11},{10,... | collective-permute-start | bytes 1966088 | tf_op jit(solution)/shard_map/ppermute | solution.py:253
  113.0 5.7 %collective-permute-start.5 = (bf16[64,512]{1,0:T(8,128)(2,1)S(1)}, bf16[64,512]{1,0:T(8,128)(2,1)S(1)}, u32[]{:S(2)}, u32[]{:S(2)}) collective-permute-start(bf16[64,512]{1,0:T(8,128)(2,1)S(1)} %slice.105), channel_id=1, source_target_pairs={{0,8},{1,9},{2,10},{3,11},{4,12},{5,13},{6,14},{7,15},{8,0},{9,1},... | collective-permute-start | bytes 196616 | tf_op jit(solution)/shard_map/ppermute | solution.py:253
  118.6 6.8 %collective-permute-start.6 = (bf16[64,512]{1,0:T(8,128)(2,1)S(1)}, bf16[64,512]{1,0:T(8,128)(2,1)S(1)}, u32[]{:S(2)}, u32[]{:S(2)}) collective-permute-start(bf16[64,512]{1,0:T(8,128)(2,1)S(1)} %fusion.1), channel_id=1, source_target_pairs={{0,8},{1,9},{2,10},{3,11},{4,12},{5,13},{6,14},{7,15},{8,0},{9,1},... | collective-permute-start | bytes 196616 | tf_op jit(solution)/shard_map/ppermute | solution.py:253
  125.3 16.1 %collective-permute-start.19 = (bf16[1280,512]{1,0:T(8,128)(2,1)S(1)}, bf16[1280,512]{1,0:T(8,128)(2,1)S(1)}, u32[]{:S(2)}, u32[]{:S(2)}) collective-permute-start(bf16[1280,512]{1,0:T(8,128)(2,1)S(1)} %pad_maximum_fusion.refs_3_), channel_id=1, source_target_pairs={{0,1},{1,0},{2,3},{3,2},{4,5},{5,4},{6,7},{7,6},{8,9},{9,8},{10,11... | collective-permute-start | bytes 3932168 | tf_op jit(solution)/shard_map/ppermute | solution.py:253
  125.5 6.0 %collective-permute-start.7 = (bf16[128,512]{1,0:T(8,128)(2,1)S(1)}, bf16[128,512]{1,0:T(8,128)(2,1)S(1)}, u32[]{:S(2)}, u32[]{:S(2)}) collective-permute-start(bf16[128,512]{1,0:T(8,128)(2,1)S(1)} %pad_maximum_fusion.5), channel_id=1, source_target_pairs={{0,4},{1,5},{2,6},{3,7},{4,0},{5,1},{6,2},{7,3},{8,12},{9,13},{10,... | collective-permute-start | bytes 393224 | tf_op jit(solution)/shard_map/ppermute | solution.py:253
  131.4 8.0 %collective-permute-start.8 = (bf16[256,512]{1,0:T(8,128)(2,1)S(1)}, bf16[256,512]{1,0:T(8,128)(2,1)S(1)}, u32[]{:S(2)}, u32[]{:S(2)}) collective-permute-start(bf16[256,512]{1,0:T(8,128)(2,1)S(1)} %pad_maximum_fusion.4), channel_id=1, source_target_pairs={{0,2},{1,3},{2,0},{3,1},{4,6},{5,7},{6,4},{7,5},{8,10},{9,11},{10,... | collective-permute-start | bytes 786440 | tf_op jit(solution)/shard_map/ppermute | solution.py:253
  139.4 2.0 %collective-permute-start.9 = (bf16[512,512]{1,0:T(8,128)(2,1)S(1)}, bf16[512,512]{1,0:T(8,128)(2,1)S(1)}, u32[]{:S(2)}, u32[]{:S(2)}) collective-permute-start(bf16[512,512]{1,0:T(8,128)(2,1)S(1)} %pad_maximum_fusion.2.refs_1_), channel_id=1, source_target_pairs={{0,1},{1,0},{2,3},{3,2},{4,5},{5,4},{6,7},{7,6},{8,9},{9,8},{10,11... | collective-permute-start | bytes 1572872 | tf_op jit(solution)/shard_map/ppermute | solution.py:253
  (33 other events, 204.9 us)

commit v2 on v1

v2 whole, which is shorter than its diff:
```python
import functools

import jax
import jax.numpy as jnp
from jax import lax
from jax.experimental import pallas as pl
from jax.experimental.pallas import tpu as pltpu
from jax.sharding import PartitionSpec as P

BF = jnp.bfloat16
F32 = jnp.float32
VMEM_BYTES = 16 * 1024 * 1024
BLOCKS = 8


def dot(a, b):
    return lax.dot_general(a, b, (((1,), (0,)), ((), ())), preferred_element_type=F32)


def dot_t(a, b):
    return lax.dot_general(a, b, (((1,), (1,)), ((), ())), preferred_element_type=F32)


def t_dot(a, b):
    return lax.dot_general(a, b, (((0,), (0,)), ((), ())), preferred_element_type=F32)


def sigmoid(v):
    return 0.5 * jnp.tanh(0.5 * v) + 0.5


def silu_slope(v, s):
    return s * (1.0 + v * (1.0 - s))


def normalized(u):
    c = u - jnp.mean(u, axis=-1, keepdims=True)
    r = lax.rsqrt(jnp.mean(c * c, axis=-1, keepdims=True) + 1e-05)
    return c * r, r


def normalized_grad(y, r, g):
    return r * (g - jnp.mean(g, axis=-1, keepdims=True) - y * jnp.mean(g * y, axis=-1, keepdims=True))


class Far:
    def __init__(self, value):
        self.value = pltpu.with_memory_space_constraint(value, pltpu.HBM)
        self.shape, self.dtype = value.shape, value.dtype


class Kept:
    def __init__(self, value):
        self.value = pltpu.with_memory_space_constraint(value, pltpu.HBM)
        self.shape, self.dtype = value.shape, value.dtype


class Input:
    def __init__(self, source, held=None, sem=None):
        self.held, self.copy = source if held is None else held, None
        if held is not None:
            self.copy = pltpu.make_async_copy(source, held, sem)
            self.copy.start()

    def __call__(self):
        if self.copy is not None:
            self.copy.wait()
            self.copy = None
        return self.held


class Output:
    def __init__(self, target, held=None, sem=None):
        self.held, self.copy, self.started = target if held is None else held, None, False
        if held is not None:
            self.copy = pltpu.make_async_copy(held, target, sem)

    def send(self):
        if self.copy is not None:
            self.copy.start()
        self.started = True

    def set(self, value):
        self.held[...] = value.astype(self.held.dtype)
        self.send()


def call(body, name, ins, outs, scratch=(), place=False):
    kept = [v for v in ins if isinstance(v, Kept)]
    far_in = [isinstance(v, (Far, Kept)) for v in ins]
    far_out = [len(v) > 2 for v in outs]
    n_in, n_out, n_kept = len(ins), len(outs), len(kept)

    def kernel(*refs):
        sources, targets = refs[:n_in], refs[n_in : n_in + n_out]
        kept_refs = list(refs[n_in + n_out : n_in + n_out + n_kept])
        rest = list(refs[n_in + n_out + n_kept :])
        out_sems, in_sems = rest.pop(), rest.pop()
        inputs, outputs = [], []
        for i, v in enumerate(ins):
            if isinstance(v, Kept):
                inputs.append(Input(sources[i], kept_refs.pop(0), in_sems.at[i]))
            elif isinstance(v, Far):
                inputs.append(Input(sources[i], rest.pop(0), in_sems.at[i]))
            else:
                inputs.append(Input(sources[i]))
        for i, is_far in enumerate(far_out):
            outputs.append(Output(targets[i], rest.pop(0), out_sems.at[i]) if is_far else Output(targets[i]))
        lead = (lax.axis_index("space").astype(jnp.int32) & (BLOCKS - 1),) if place else ()
        body(*lead, inputs, outputs, rest)
        for value in inputs:
            value()
        for value in outputs:
            if not value.started:
                value.send()
        for value in outputs:
            if value.copy is not None:
                value.copy.wait()

    anywhere, near = pl.BlockSpec(memory_space=pl.ANY), pl.BlockSpec(memory_space=pltpu.VMEM)
    held = [pltpu.VMEM(v.shape, v.dtype) for v in ins if isinstance(v, Far)]
    held += [pltpu.VMEM(v[0], v[1]) for v in outs if len(v) > 2]
    return pl.pallas_call(
        kernel,
        name=name,
        out_shape=[(pltpu.HBM if far else pltpu.VMEM)(v[0], v[1]) for v, far in zip(outs, far_out)]
        + [pltpu.VMEM(v.shape, v.dtype) for v in kept],
        in_specs=[anywhere if far else near for far in far_in],
        out_specs=[anywhere if far else near for far in far_out] + [near] * n_kept,
        scratch_shapes=held
        + [pltpu.VMEM(shape, dtype) for shape, dtype in scratch]
        + [pltpu.SemaphoreType.DMA((n_in,)), pltpu.SemaphoreType.DMA((max(n_out, 1),))],
        compiler_params=pltpu.CompilerParams(vmem_limit_bytes=VMEM_BYTES),
    )(*(v.value if far else v for v, far in zip(ins, far_in)))


def pick_body(ins, outs, _):
    sends_t, x_t = ins
    sends = sends_t()[...]
    cap, peers = sends.shape
    lanes = lax.broadcasted_iota(jnp.int32, (cap, x_t.held.shape[1]), 1)
    pick = [jnp.where(sends[:, d : d + 1] == lanes, 1.0, 0.0) for d in range(peers)]
    pick = jnp.concatenate(pick, axis=0).astype(BF)
    outs[0].set(dot_t(pick, x_t()[...]))


def embed_rows(pre, ws):
    s = sigmoid(pre)
    lat = (pre * s).astype(BF)
    return lat, silu_slope(pre, s).astype(BF), dot(lat, ws).astype(BF)


def embed_body(ins, outs, _):
    x_t, we, ws, latent, wrecv = ins[:5]
    lat, slope, proj, recv = outs
    x_t()
    at = t_dot(x_t()[...], we()[...])
    one, two, three = embed_rows(at, ws()[...])
    lat.set(one)
    slope.set(two)
    proj.set(three)
    recv.set(dot(latent()[...], wrecv()[...]))


def fill_onehot(onehot, slots):
    m, fan = slots.shape
    wide = onehot.shape[1]
    lanes = lax.broadcasted_iota(jnp.int32, (m, wide), 1)
    for f in range(fan):
        onehot[f * m : (f + 1) * m, :] = jnp.where(slots[:, f : f + 1] == lanes, 1.0, 0.0).astype(BF)


def fill_onehot_t(onehot, slots_t):
    fan, m = slots_t.shape
    tall = onehot.shape[0]
    subs = lax.broadcasted_iota(jnp.int32, (tall, 2 * m), 0)
    for f in range(0, fan, 2):
        pair = jnp.concatenate([slots_t[f : f + 1, :], slots_t[f + 1 : f + 2, :]], axis=1)
        onehot[:, f * m : (f + 2) * m] = jnp.where(pair == subs, 1.0, 0.0).astype(BF)


def messages(rows, recv, mask, slope):
    m, fan = mask.shape
    total = None
    for f in range(fan):
        at = slice(f * m, (f + 1) * m)
        v = rows[at, :] + recv
        s = sigmoid(v)
        k = mask[:, f : f + 1].astype(F32)
        slope[at, :] = (silu_slope(v, s) * k).astype(slope.dtype)
        part = v * s * k
        total = part if total is None else total + part
    return total.astype(BF)


def encode_body(ins, outs, scratch):
    slots_t, mask_t, x, we, ws, proj, recv, wout, latent, wnext, halo = ins
    mid, to_left, to_right, mesh_proj, agg, y, r, slope, lat_far, slope_far = outs
    table, onehot, rows = scratch
    near = proj.held.shape[0]
    fill_onehot(onehot, slots_t()[...].T)
    mask = mask_t()[...].T
    x()
    pre = dot(x()[...], we()[...])
    one, two, far = embed_rows(pre, ws()[...])
    lat_far.set(one)
    slope_far.set(two)
    table[near:, :] = far
    table[:near, :] = proj()[...]
    rows[...] = dot(onehot[...], table[...])
    summed = messages(rows, recv()[...], mask, slope.held)
    slope.send()
    agg.set(summed)
    normed, scale = normalized(dot(summed, wout()[...]))
    y.set(normed)
    r.set(jnp.broadcast_to(scale, r.held.shape))
    middle = (latent()[...].astype(F32) + normed).astype(BF)
    mid.set(middle)
    sent = dot(middle, wnext()[...]).astype(BF)
    mesh_proj.set(sent)
    lists = halo()[...]
    subs = lax.broadcasted_iota(jnp.int32, (sent.shape[0], lists.shape[1]), 0)
    to_left.set(t_dot(jnp.where(lists[0:1, :] == subs, 1.0, 0.0).astype(BF), sent))
    to_right.set(t_dot(jnp.where(lists[1:2, :] == subs, 1.0, 0.0).astype(BF), sent))


def process_body(ins, outs, scratch):
    slots_t, mask_t, mesh_proj, left, right, mid, wrecv, wout, cotangent = ins
    out, to_left, to_right, grad_rows, grad_mid, agg, grad_u, grad_recv = outs
    table, onehot, onehot_t, rows, slope, grad_msg = scratch
    m = mesh_proj.held.shape[0]
    depth = left.held.shape[0]
    slots = slots_t()[...]
    fill_onehot(onehot, slots.T)
    mask = mask_t()[...].T
    fill_onehot_t(onehot_t, slots)
    table[:m, :] = mesh_proj()[...]
    table[m : m + depth, :] = left()[...]
    table[m + depth : m + 2 * depth, :] = right()[...]
    rows[...] = dot(onehot[...], table[...])
    middle = mid()[...]
    summed = messages(rows, dot(middle, wrecv()[...]), mask, slope)
    agg.set(summed)
    normed, scale = normalized(dot(summed, wout()[...]))
    out.set(middle.astype(F32) + normed)
    ct = cotangent()[...].astype(F32)
    gu = normalized_grad(normed, scale, ct).astype(BF)
    grad_u.set(gu)
    gr = message_grads(grad_msg, slope, dot_t(gu, wout()[...]), mask.shape[1])
    grad_recv.set(gr)
    grads = dot(onehot_t[...], grad_msg[...])
    to_left.set(grads[m : m + depth, :])
    to_right.set(grads[m + depth :, :])
    grad_rows.set(grads[:m, :])
    grad_mid.set(ct + dot_t(gr, wrecv()[...]))


def message_grads(grad_msg, slope, gagg, fan):
    m = gagg.shape[0]
    total = None
    for f in range(fan):
        at = slice(f * m, (f + 1) * m)
        g = slope[at, :].astype(F32) * gagg
        grad_msg[at, :] = g.astype(BF)
        total = g if total is None else total + g
    return total.astype(BF)


def block_of(place, me, order):
    flips = 0
    for i, step in enumerate(order):
        if place >> (len(order) - 1 - i) & 1:
            flips ^= step
    return me ^ flips


def spread(me, order, grads, keep, send):
    deep = grads[0].shape[0] // BLOCKS
    half = BLOCKS // 2
    for place in reversed(range(BLOCKS)):
        at = pl.multiple_of(block_of(place, me, order) * deep, deep)
        for g, grad in enumerate(grads):
            to = ((place % half) * len(grads) + g) * deep
            target = keep if place < half else send
            target.held[to : to + deep, :] = grad[pl.ds(at, deep), :].astype(target.held.dtype)
        if place == half:
            send.send()
    keep.send()


def process_grads_body(order, me, ins, outs, scratch):
    agg, grad_u, mid, grad_recv = ins
    one, two = scratch
    one[...] = t_dot(agg()[...], grad_u()[...])
    two[...] = t_dot(mid()[...], grad_recv()[...])
    spread(me, order, (one, two), *outs)


def mesh_grads_body(order, me, ins, outs, scratch):
    slots_t, back_left, back_right, halo, grad_rows, wnext, grad_mid, y, r, wout, slope, mid, agg, latent = ins
    keep, send, grad_table = outs
    onehot_t, grad_msg, g_next, g_out, g_recv = scratch
    m = mid.held.shape[0]
    fill_onehot_t(onehot_t, slots_t()[...])
    lists = halo()[...]
    subs = lax.broadcasted_iota(jnp.int32, (m, lists.shape[1]), 0)
    to_left = jnp.where(lists[0:1, :] == subs, 1.0, 0.0).astype(BF)
    to_right = jnp.where(lists[1:2, :] == subs, 1.0, 0.0).astype(BF)
    gp = (grad_rows()[...] + dot(to_right, back_right()[...]) + dot(to_left, back_left()[...])).astype(BF)
    gmid = grad_mid()[...] + dot_t(gp, wnext()[...])
    gu = normalized_grad(y()[...], r()[:, 0:1], gmid).astype(BF)
    gagg = dot_t(gu, wout()[...])
    gr = message_grads(grad_msg, slope(), gagg, grad_msg.shape[0] // m)
    grad_table.set(dot(onehot_t[...], grad_msg[...]))
    g_next[...] = t_dot(mid()[...], gp)
    g_out[...] = t_dot(agg()[...], gu)
    g_recv[...] = t_dot(latent()[...], gr)
    spread(me, order, (g_next, g_out, g_recv), keep, send)


def grid_grads_body(order, me, ins, outs, scratch):
    grad_table, ws, slope_near, slope_far, x_t, x_far, lat, lat_far = ins
    g_send, g_embed = scratch
    near = lat.held.shape[0]
    g_near, g_far = grad_table()[:near, :], grad_table()[near:, :]
    p_near = (dot_t(g_near, ws()[...]) * slope_near()[...].astype(F32)).astype(BF)
    p_far = (dot_t(g_far, ws()[...]) * slope_far()[...].astype(F32)).astype(BF)
    fin = x_t.held.shape[0]
    tail = fin // 32 * 32
    g_embed[tail:, :] = jnp.zeros((g_embed.shape[0] - tail, g_embed.shape[1]), F32)
    g_embed[:fin, :] = dot(x_t()[...], p_near) + t_dot(x_far()[...], p_far)
    g_send[...] = t_dot(lat()[...], g_near) + t_dot(lat_far()[...], g_far)
    spread(me, order, (g_send, g_embed), *outs)


def collect_body(order, me, ins, outs, scratch):
    whole = scratch[0] if scratch else outs[0].held
    half = BLOCKS // 2
    deep = whole.shape[0] // BLOCKS
    for g, out in enumerate(outs):
        short = out.held.shape[0] != whole.shape[0]
        for place in range(BLOCKS):
            source = ins[place // half]()
            at = pl.multiple_of(block_of(place, me, order) * deep, deep)
            frm = ((place % half) * len(outs) + g) * deep
            (whole if short else out.held)[pl.ds(at, deep), :] = source[frm : frm + deep, :].astype(F32)
        if short:
            out.held[...] = whole[: out.held.shape[0], :]
        out.send()


def add_body(ins, outs, _):
    kept, got = ins
    total = kept()[...].astype(F32) + got()[...].astype(F32)
    deep = 0
    for out in outs:
        out.set(total[deep : deep + out.held.shape[0], :])
        deep += out.held.shape[0]


def join_body(ins, outs, _):
    half = ins[0].held.shape[0]
    outs[0].held[:half, :] = ins[0]()[...]
    outs[0].held[half:, :] = ins[1]()[...]


def load_body(ins, outs, _):
    for value in ins:
        value()


def exchange(value, step):
    n = lax.axis_size("space")
    return lax.ppermute(value, "space", [(i, i ^ step) for i in range(n)])


def all_sum(name, keep, send, order, rest):
    for i, step in enumerate(order):
        rows, width = keep.shape
        if i + 1 < len(order):
            outs = [((rows // 2, width), F32), ((rows // 2, width), BF)]
        else:
            outs = [((rows, width), BF)]
        got = call(add_body, f"{name}_add", [keep, exchange(send, step)], outs)
        if i + 1 < len(order):
            keep, send = got
    (value,) = got
    for step in rest:
        (value,) = call(add_body, f"{name}_add", [value, exchange(value, step)], [(value.shape, BF)])
    for step in order[:0:-1]:
        rows, width = value.shape
        (value,) = call(join_body, f"{name}_join", [value, exchange(value, step)], [((2 * rows, width), BF)])
    return value, exchange(value, order[0])


def passed_along(block, distance):
    n = lax.axis_size("space")
    return lax.ppermute(block, "space", [((i - distance) % n, i) for i in range(n)])


def local(
    grid_inputs, mesh_latent, cotangent, send_list, enc_slot, enc_mask, halo_list, proc_slot, proc_mask,
    w_embed, enc_send, enc_recv, enc_out, proc_send, proc_recv, proc_out,
):
    n = lax.axis_size("space")
    bits = [1 << i for i in range(n.bit_length() - 1)]
    y_first = tuple(bits[:3])
    z_first = (bits[0], bits[2], bits[1])
    rest = tuple(bits[3:])
    near, fin = grid_inputs.shape
    m, width = mesh_latent.shape
    edges_e = m * enc_slot.shape[1]
    edges_p = m * proc_slot.shape[1]
    depth = halo_list.shape[2]
    far = send_list.shape[1] * send_list.shape[2]
    x_t, sends_t, enc_slot_t, enc_mask_t, proc_slot_t, proc_mask_t = (
        v.T for v in (grid_inputs, send_list[0], enc_slot, enc_mask, proc_slot, proc_mask)
    )
    halo = halo_list[0]

    (outgoing,) = call(pick_body, "pick", [Far(sends_t), Far(x_t)], [((far, fin), BF, "far")])
    incoming = lax.all_to_all(outgoing.reshape(n, -1, fin), "space", split_axis=0, concat_axis=0, tiled=True)
    x_far = incoming.reshape(far, fin)

    patch, edge_rows, patch_f32 = ((m, width), BF), ((depth, width), BF), ((m, width), F32)
    grid_rows, far_rows = ((near, width), BF), ((far, width), BF)
    lat, slope_near, proj, recv, w_embed, enc_send, latent, enc_out, proc_send, halo, enc_slot_t, enc_mask_t = call(
        embed_body,
        "embed",
        [Far(x_t), Kept(w_embed), Kept(enc_send), Kept(mesh_latent), Far(enc_recv), Kept(enc_out), Kept(proc_send),
         Kept(halo), Kept(enc_slot_t), Kept(enc_mask_t)],
        [(*grid_rows, "far"), (*grid_rows, "far"), grid_rows, patch_f32],
    )

    mid, to_left, to_right, mesh_proj, agg, y, r, slope, lat_far, slope_far = call(
        encode_body,
        "encode",
        [enc_slot_t, enc_mask_t, x_far, w_embed, enc_send, proj, recv, enc_out, latent, proc_send, halo],
        [patch, edge_rows, edge_rows, patch, patch, patch_f32, ((m, 128), F32), ((edges_e, width), BF), far_rows,
         far_rows],
        [((near + far, width), BF), ((edges_e, near + far), BF), ((edges_e, width), F32)],
    )

    from_left = passed_along(to_right, 1)
    from_right = passed_along(to_left, -1)

    after = (x_t, lat, slope_near, proc_recv, proc_out, cotangent, proc_slot_t, proc_mask_t, mid)
    x_t, lat, slope_near, proc_recv, proc_out, cotangent, proc_slot_t, proc_mask_t, mid = lax.optimization_barrier(after)
    x_t, lat, slope_near, proc_recv, proc_out, cotangent, proc_slot_t, proc_mask_t = call(
        load_body,
        "load",
        [Kept(v) for v in (x_t, lat, slope_near, proc_recv, proc_out, cotangent, proc_slot_t, proc_mask_t)],
        [],
    )

    wide = m + 2 * depth
    out, back_to_left, back_to_right, grad_rows, grad_mid, agg2, grad_u, grad_recv = call(
        process_body,
        "process",
        [proc_slot_t, proc_mask_t, mesh_proj, from_left, from_right, mid, proc_recv, proc_out, cotangent],
        [(*patch, "far"), edge_rows, edge_rows, patch_f32, patch_f32, patch, patch, patch],
        [((wide, width), BF), ((edges_p, wide), BF), ((wide, edges_p), BF), ((edges_p, width), F32),
         ((edges_p, width), F32), ((edges_p, width), BF)],
    )

    back_right = passed_along(back_to_left, -1)
    back_left = passed_along(back_to_right, 1)

    def halves(count):
        rows = count * width // 2
        return [((rows, width), F32), ((rows, width), BF)]

    square = ((width, width), F32)

    def collected(name, order, pair, outs, scratch=()):
        outs = [(*v, "far") for v in outs]
        return call(functools.partial(collect_body, order), name, pair, outs, scratch, True)

    keep_p, send_p = call(
        functools.partial(process_grads_body, z_first), "process_grads", [agg2, grad_u, mid, grad_recv], halves(2),
        [square] * 2, True,
    )
    grad_rows, keep_p, send_p = lax.optimization_barrier((grad_rows, keep_p, send_p))
    first = all_sum("process", keep_p, send_p, z_first, rest)

    keep_m, send_m, grad_table = call(
        functools.partial(mesh_grads_body, y_first),
        "mesh_grads",
        [enc_slot_t, back_left, back_right, halo, grad_rows, proc_send, grad_mid, y, r, enc_out, slope, mid, agg,
         latent],
        halves(3) + [((near + far, width), BF)],
        [((near + far, edges_e), BF), ((edges_e, width), BF)] + [square] * 3,
        True,
    )
    second = all_sum("mesh", keep_m, send_m, y_first, rest)

    keep_g, send_g = call(
        functools.partial(grid_grads_body, z_first),
        "grid_grads",
        [grad_table, enc_send, slope_near, slope_far, x_t, x_far, lat, lat_far],
        halves(2),
        [square] * 2,
        True,
    )
    third = all_sum("grid", keep_g, send_g, z_first, rest)

    g_pout, g_precv = collected("collect_process", z_first, first, [square] * 2)
    g_psend, g_eout, g_erecv = collected("collect_mesh", y_first, second, [square] * 3)
    g_esend, g_embed = collected("collect_grid", z_first, third, [square, ((fin, width), F32)], [square])
    return out, g_embed, g_esend, g_erecv, g_eout, g_psend, g_precv, g_pout


def solution(mesh):
    rows = P(("groups", "space"), None)
    lists = P(("groups", "space"), None, None)
    return jax.shard_map(
        local,
        mesh=mesh,
        in_specs=(rows, rows, rows, lists, rows, rows, lists, rows, rows) + (P(),) * 7,
        out_specs=(rows,) + (P("groups", None),) * 7,
        check_vma=False,
    )
```

time: 145 us -> 119 us (0.82)
  waiting for transfers between devices: 92 us -> 62.3 us
  local copies, waits for them, and re-layouts: 18.7 us -> 0 us
  starting transfers between devices: 16.5 us -> 31.1 us
  Pallas kernels: 14.1 us -> 23.7 us
  other arithmetic: 2.02 us -> 0 us
    ppermute x16 -> x21, waiting for transfers between devices: 76.4 us -> 56.1 us  [exchange(): return lax.ppermute(value, 'space', [(i, i ^ step) for i in range(n)])]
    unnamed x77 -> x0, local copies, waits for them, and re-layouts: 15.9 us -> none
    ppermute x4, waiting for transfers between devices: 11.5 us -> 1.5 us  [passed_along(): lax.ppermute(block, 'space', [((i - distance) % n, i) for i in range(n)])]
    pallas_call x6 -> x29, Pallas kernels: 14.1 us -> 23.7 us  [call(): pl.pallas_call(kernel, name=name, out_shape=[(pltpu.HBM if far else pltpu...]
    ppermute x4, starting transfers between devices: 1.26 us -> 9.22 us  [passed_along(): lax.ppermute(block, 'space', [((i - distance) % n, i) for i in range(n)])]
    ppermute x16 -> x21, starting transfers between devices: 7.83 us -> 14.5 us  [exchange(): return lax.ppermute(value, 'space', [(i, i ^ step) for i in range(n)])]
    gather x1 -> x0, local copies, waits for them, and re-layouts: 1.5 us -> none  [local(): outgoing = grid_inputs[send_list[0]]]
  transfers between devices with their start and end apart: 21 -> 26, of which waited for: 17 -> 19; matrix products, arithmetic and copies ran while one was open for 1% -> 0% of each run, Pallas kernels for 1% -> 10%
where the time goes in v2:
time: 119 us; the launch traced here: 118 us
  waiting for transfers between devices  62.3 us (52%)
  starting transfers between devices  31.1 us (26%)
  Pallas kernels  23.7 us (20%)
    ppermute x21, waiting for transfers between devices, exchange(): return lax.ppermute(value, 'space', [(i, i ^ step) for i in range(n)])  56.1 us
    pallas_call x29, Pallas kernels, call(): pl.pallas_call(kernel, name=name, out_shape=[(pltpu.HBM if far else pltpu...  23.7 us
    ppermute x21, starting transfers between devices, exchange(): return lax.ppermute(value, 'space', [(i, i ^ step) for i in range(n)])  14.5 us
    ppermute x4, starting transfers between devices, passed_along(): lax.ppermute(block, 'space', [((i - distance) % n, i) for i in range(n)])  9.22 us
    all_to_all x1, starting transfers between devices, local(): lax.all_to_all(outgoing.reshape(n, -1, fin), 'space', split_axis=0, conca...  7.4 us
    all_to_all x1, waiting for transfers between devices, local(): lax.all_to_all(outgoing.reshape(n, -1, fin), 'space', split_axis=0, conca...  4.73 us
  transfers between devices with their start and end apart: 26, of which 19 were waited for; matrix products, arithmetic and copies ran while one was open for 0% of the time, Pallas kernels for 10%

profile of v2, /device:TPU:0, one launch (start us, length us, event | category | flops | bytes accessed | tf_op | source)
XLA Modules:
  0.0 118.3 jit_solution(12799573954885332131)
XLA Ops:
  0.6 2.0 %pick.1 = bf16[128,474]{1,0:T(8,128)(2,1)} custom-call(s32[8,16]{1,0:T(8,128)} %bitcast.21, bf16[474,512]{1,0:T(8,128)(2,1)} %bitcast.13), custom_call_target="tpu_custom_call" | custom-call | tf_op jit(solution)/shard_map/pick/pallas_call | solution.py:123
  2.7 7.4 %all-to-all-start = ((bf16[16,8,474]{2,1,0:T(8,128)(2,1)}), bf16[16,8,474]{2,1,0:T(8,128)(2,1)S(1)}, u32[]{:S(2)}, u32[]{:S(2)}) async-start(bf16[16,8,474]{2,1,0:T(8,128)(2,1)} %bitcast.16), calls=%async_computation | async-start | bytes 262144 | tf_op jit(solution)/shard_map/all_to_all | solution.py:422
  10.1 3.2 %embed.1 = (bf16[512,512]{1,0:T(8,128)(2,1)}, bf16[512,512]{1,0:T(8,128)(2,1)}, bf16[512,512]{1,0:T(8,128)(2,1)S(1)}, f32[64,512]{1,0:T(8,128)S(1)}, bf16[474,51...) custom-call(bf16[474,512]{1,0:T(8,128)(2,1)} %bitcast.14, ...), custom_call_target="tpu_custom_call" | custom-call | tf_op jit(solution)/shard_map/embed/pallas_call | solution.py:123
  13.3 4.7 %all-to-all-done = bf16[16,8,474]{2,1,0:T(8,128)(2,1)S(1)} async-done(((bf16[16,8,474]{2,1,0:T(8,128)(2,1)}), bf16[16,8,474]{2,1,0:T(8,128)(2,1)S(1)}, u32[]{:S(2)}, u32[]{:S(2)}) %all-to-all-start) | async-done | bytes 121376 | tf_op jit(solution)/shard_map/all_to_all | solution.py:422
  18.0 3.0 %encode.1 = (bf16[64,512]{1,0:T(8,128)(2,1)S(1)}, bf16[64,512]{1,0:T(8,128)(2,1)S(1)}, bf16[64,512]{1,0:T(8,128)(2,1)S(1)}, bf16[64,512]{1,0:T(8,128)(2,1)S(1)},...) custom-call(s32[16,64]{1,0:T(8,128)S(1)} %get-tuple-element.86.refs_, ...), custom_call_target="tpu_custom_call" | custom-call | tf_op jit(solution)/shard_map/encode/pallas_call | solution.py:123
  21.1 4.4 %collective-permute-start.1 = (bf16[64,512]{1,0:T(8,128)(2,1)S(1)}, bf16[64,512]{1,0:T(8,128)(2,1)S(1)}, u32[]{:S(2)}, u32[]{:S(2)}) collective-permute-start(bf16[64,512]{1,0:T(8,128)(2,1)S(1)} %get-tuple-element.109), channel_id=1, source_target_pairs={{1,0},{2,1},{3,2},{4,3},{5,4},{6,5},{7,6},{8,7},{9,8},{10,9},{11,1... | collective-permute-start | bytes 196616 | tf_op jit(solution)/shard_map/ppermute | solution.py:398
  27.5 3.0 %process.1 = (bf16[64,512]{1,0:T(8,128)(2,1)}, bf16[64,512]{1,0:T(8,128)(2,1)S(1)}, bf16[64,512]{1,0:T(8,128)(2,1)S(1)}, f32[64,512]{1,0:T(8,128)S(1)}, f32[64,5...) custom-call(s32[16,64]{1,0:T(8,128)S(1)} %get-tuple-element.105.refs_0_,, ...), custom_call_target="tpu_custom_call" | custom-call | tf_op jit(solution)/shard_map/process/pallas_call | solution.py:123
  30.5 4.7 %collective-permute-start.3 = (bf16[64,512]{1,0:T(8,128)(2,1)S(1)}, bf16[64,512]{1,0:T(8,128)(2,1)S(1)}, u32[]{:S(2)}, u32[]{:S(2)}) collective-permute-start(bf16[64,512]{1,0:T(8,128)(2,1)S(1)} %get-tuple-element.116), channel_id=1, source_target_pairs={{1,0},{2,1},{3,2},{4,3},{5,4},{6,5},{7,6},{8,7},{9,8},{10,9},{11,1... | collective-permute-start | bytes 196616 | tf_op jit(solution)/shard_map/ppermute | solution.py:398
  37.1 2.3 %mesh_grads.1 = (f32[768,512]{1,0:T(8,128)S(1)}, bf16[768,512]{1,0:T(8,128)(2,1)S(1)}, bf16[640,512]{1,0:T(8,128)(2,1)S(1)}) custom-call(s32[16,64]{1,0:T(8,128)S(1)} %get-tuple-element.86.refs_0_, bf16[64,512]{1,0:T(8,128)(2,1)S(1)} %collective-permute-done.2.refs_1_, bf16[64,512]{1,0:T(8,128)(2,1)S(1)} %collective-permute-done.3.refs_2_, ...), custom_call_target="tpu_custom_call" | custom-call | tf_op jit(solution)/shard_map/mesh_grads/pallas_call | solution.py:123
  39.5 2.3 %collective-permute-done.11.refs_1_ = bf16[768,512]{1,0:T(8,128)(2,1)S(1)} collective-permute-done((bf16[768,512]{1,0:T(8,128)(2,1)S(1)}, bf16[768,512]{1,0:T(8,128)(2,1)S(1)}, u32[]{:S(2)}, u32[]{:S(2)}) %collective-permute-start.11) | collective-permute-done | bytes 786464 | tf_op jit(solution)/shard_map/ppermute | solution.py:374
  44.4 8.8 %collective-permute-done.12.refs_1_ = bf16[384,512]{1,0:T(8,128)(2,1)S(1)} collective-permute-done((bf16[384,512]{1,0:T(8,128)(2,1)S(1)}, bf16[384,512]{1,0:T(8,128)(2,1)S(1)}, u32[]{:S(2)}, u32[]{:S(2)}) %collective-permute-start.12) | collective-permute-done | bytes 393248 | tf_op jit(solution)/shard_map/ppermute | solution.py:374
  53.4 6.1 %collective-permute-done.13.refs_1_ = bf16[192,512]{1,0:T(8,128)(2,1)S(1)} collective-permute-done((bf16[192,512]{1,0:T(8,128)(2,1)S(1)}, bf16[192,512]{1,0:T(8,128)(2,1)S(1)}, u32[]{:S(2)}, u32[]{:S(2)}) %collective-permute-start.13) | collective-permute-done | bytes 196640 | tf_op jit(solution)/shard_map/ppermute | solution.py:374
  59.5 3.0 %collective-permute-start.14 = (bf16[192,512]{1,0:T(8,128)(2,1)S(1)}, bf16[192,512]{1,0:T(8,128)(2,1)S(1)}, u32[]{:S(2)}, u32[]{:S(2)}) collective-permute-start(bf16[192,512]{1,0:T(8,128)(2,1)S(1)} %mesh_add.6.refs_0_), channel_id=1, source_target_pairs={{0,8},{1,9},{2,10},{3,11},{4,12},{5,13},{6,14},{7,15},{8,0},{9,1},... | collective-permute-start | bytes 589832 | tf_op jit(solution)/shard_map/ppermute | solution.py:374
  62.6 1.8 %collective-permute-start.19 = (bf16[256,512]{1,0:T(8,128)(2,1)S(1)}, bf16[256,512]{1,0:T(8,128)(2,1)S(1)}, u32[]{:S(2)}, u32[]{:S(2)}) collective-permute-start(bf16[256,512]{1,0:T(8,128)(2,1)S(1)} %get-tuple-element.155), channel_id=1, source_target_pairs={{0,4},{1,5},{2,6},{3,7},{4,0},{5,1},{6,2},{7,3},{8,12},{9,13},{10,... | collective-permute-start | bytes 786440 | tf_op jit(solution)/shard_map/ppermute | solution.py:374
  64.9 6.2 %collective-permute-done.14.refs_1_ = bf16[192,512]{1,0:T(8,128)(2,1)S(1)} collective-permute-done((bf16[192,512]{1,0:T(8,128)(2,1)S(1)}, bf16[192,512]{1,0:T(8,128)(2,1)S(1)}, u32[]{:S(2)}, u32[]{:S(2)}) %collective-permute-start.14) | collective-permute-done | bytes 196640 | tf_op jit(solution)/shard_map/ppermute | solution.py:374
  71.9 3.2 %collective-permute-done.19.refs_1_ = bf16[256,512]{1,0:T(8,128)(2,1)S(1)} collective-permute-done((bf16[256,512]{1,0:T(8,128)(2,1)S(1)}, bf16[256,512]{1,0:T(8,128)(2,1)S(1)}, u32[]{:S(2)}, u32[]{:S(2)}) %collective-permute-start.19) | collective-permute-done | bytes 262176 | tf_op jit(solution)/shard_map/ppermute | solution.py:374
  76.4 4.2 %collective-permute-done.5.refs_1_ = bf16[256,512]{1,0:T(8,128)(2,1)S(1)} collective-permute-done((bf16[256,512]{1,0:T(8,128)(2,1)S(1)}, bf16[256,512]{1,0:T(8,128)(2,1)S(1)}, u32[]{:S(2)}, u32[]{:S(2)}) %collective-permute-start.5) | collective-permute-done | bytes 262176 | tf_op jit(solution)/shard_map/ppermute | solution.py:374
  85.2 2.0 %collective-permute-done.6.refs_1_ = bf16[128,512]{1,0:T(8,128)(2,1)S(1)} collective-permute-done((bf16[128,512]{1,0:T(8,128)(2,1)S(1)}, bf16[128,512]{1,0:T(8,128)(2,1)S(1)}, u32[]{:S(2)}, u32[]{:S(2)}) %collective-permute-start.6) | collective-permute-done | bytes 131104 | tf_op jit(solution)/shard_map/ppermute | solution.py:374
  87.9 6.9 %collective-permute-done.21.refs_1_ = bf16[128,512]{1,0:T(8,128)(2,1)S(1)} collective-permute-done((bf16[128,512]{1,0:T(8,128)(2,1)S(1)}, bf16[128,512]{1,0:T(8,128)(2,1)S(1)}, u32[]{:S(2)}, u32[]{:S(2)}) %collective-permute-start.21) | collective-permute-done | bytes 131104 | tf_op jit(solution)/shard_map/ppermute | solution.py:374
  98.0 2.7 %collective-permute-done.22.refs_1_ = bf16[128,512]{1,0:T(8,128)(2,1)S(1)} collective-permute-done((bf16[128,512]{1,0:T(8,128)(2,1)S(1)}, bf16[128,512]{1,0:T(8,128)(2,1)S(1)}, u32[]{:S(2)}, u32[]{:S(2)}) %collective-permute-start.22) | collective-permute-done | bytes 131104 | tf_op jit(solution)/shard_map/ppermute | solution.py:374
  100.8 2.0 %collective-permute-done.8.refs_1_ = bf16[128,512]{1,0:T(8,128)(2,1)S(1)} collective-permute-done((bf16[128,512]{1,0:T(8,128)(2,1)S(1)}, bf16[128,512]{1,0:T(8,128)(2,1)S(1)}, u32[]{:S(2)}, u32[]{:S(2)}) %collective-permute-start.8) | collective-permute-done | bytes 131104 | tf_op jit(solution)/shard_map/ppermute | solution.py:374
  103.1 6.6 %collective-permute-done.23.refs_1_ = bf16[256,512]{1,0:T(8,128)(2,1)S(1)} collective-permute-done((bf16[256,512]{1,0:T(8,128)(2,1)S(1)}, bf16[256,512]{1,0:T(8,128)(2,1)S(1)}, u32[]{:S(2)}, u32[]{:S(2)}) %collective-permute-start.23) | collective-permute-done | bytes 262176 | tf_op jit(solution)/shard_map/ppermute | solution.py:374
  109.8 2.9 %collective-permute-done.9.refs_1_ = bf16[256,512]{1,0:T(8,128)(2,1)S(1)} collective-permute-done((bf16[256,512]{1,0:T(8,128)(2,1)S(1)}, bf16[256,512]{1,0:T(8,128)(2,1)S(1)}, u32[]{:S(2)}, u32[]{:S(2)}) %collective-permute-start.9) | collective-permute-done | bytes 262176 | tf_op jit(solution)/shard_map/ppermute | solution.py:374
  116.2 1.9 %collect_mesh.1 = (f32[512,512]{1,0:T(8,128)}, f32[512,512]{1,0:T(8,128)}, f32[512,512]{1,0:T(8,128)}) custom-call(bf16[768,512]{1,0:T(8,128)(2,1)S(1)} %mesh_join.3.refs_0_, bf16[768,512]{1,0:T(8,128)(2,1)S(1)} %collective-permute-done.17.refs_1_), custom_call_target="tpu_custom_call" | custom-call | tf_op jit(solution)/shard_map/collect_mesh/pallas_call | solution.py:123
  (57 shorter events, 21.9 us)
Async XLA Ops:
  2.7 15.3 %all-to-all-start = ((bf16[16,8,474]{2,1,0:T(8,128)(2,1)}), bf16[16,8,474]{2,1,0:T(8,128)(2,1)S(1)}, u32[]{:S(2)}, u32[]{:S(2)}) async-start(bf16[16,8,474]{2,1,0:T(8,128)(2,1)} %bitcast.16), calls=%async_computation | async-start | bytes 262144 | tf_op jit(solution)/shard_map/all_to_all | solution.py:422
  21.0 6.4 %collective-permute-start = (bf16[64,512]{1,0:T(8,128)(2,1)S(1)}, bf16[64,512]{1,0:T(8,128)(2,1)S(1)}, u32[]{:S(2)}, u32[]{:S(2)}) collective-permute-start(bf16[64,512]{1,0:T(8,128)(2,1)S(1)} %get-tuple-element.108), channel_id=1, source_target_pairs={{15,0},{0,1},{1,2},{2,3},{3,4},{4,5},{5,6},{6,7},{7,8},{8,9},{9,10... | collective-permute-start | bytes 196616 | tf_op jit(solution)/shard_map/ppermute | solution.py:398
  21.1 6.4 %collective-permute-start.1 = (bf16[64,512]{1,0:T(8,128)(2,1)S(1)}, bf16[64,512]{1,0:T(8,128)(2,1)S(1)}, u32[]{:S(2)}, u32[]{:S(2)}) collective-permute-start(bf16[64,512]{1,0:T(8,128)(2,1)S(1)} %get-tuple-element.109), channel_id=1, source_target_pairs={{1,0},{2,1},{3,2},{4,3},{5,4},{6,5},{7,6},{8,7},{9,8},{10,9},{11,1... | collective-permute-start | bytes 196616 | tf_op jit(solution)/shard_map/ppermute | solution.py:398
  30.5 6.4 %collective-permute-start.2 = (bf16[64,512]{1,0:T(8,128)(2,1)S(1)}, bf16[64,512]{1,0:T(8,128)(2,1)S(1)}, u32[]{:S(2)}, u32[]{:S(2)}) collective-permute-start(bf16[64,512]{1,0:T(8,128)(2,1)S(1)} %get-tuple-element.115), channel_id=1, source_target_pairs={{15,0},{0,1},{1,2},{2,3},{3,4},{4,5},{5,6},{6,7},{7,8},{8,9},{9,10... | collective-permute-start | bytes 196616 | tf_op jit(solution)/shard_map/ppermute | solution.py:398
  30.5 6.6 %collective-permute-start.3 = (bf16[64,512]{1,0:T(8,128)(2,1)S(1)}, bf16[64,512]{1,0:T(8,128)(2,1)S(1)}, u32[]{:S(2)}, u32[]{:S(2)}) collective-permute-start(bf16[64,512]{1,0:T(8,128)(2,1)S(1)} %get-tuple-element.116), channel_id=1, source_target_pairs={{1,0},{2,1},{3,2},{4,3},{5,4},{6,5},{7,6},{8,7},{9,8},{10,9},{11,1... | collective-permute-start | bytes 196616 | tf_op jit(solution)/shard_map/ppermute | solution.py:398
  41.9 11.2 %collective-permute-start.12 = (bf16[384,512]{1,0:T(8,128)(2,1)S(1)}, bf16[384,512]{1,0:T(8,128)(2,1)S(1)}, u32[]{:S(2)}, u32[]{:S(2)}) collective-permute-start(bf16[384,512]{1,0:T(8,128)(2,1)S(1)} %get-tuple-element.146), channel_id=1, source_target_pairs={{0,2},{1,3},{2,0},{3,1},{4,6},{5,7},{6,4},{7,5},{8,10},{9,11},{10,... | collective-permute-start | bytes 1179656 | tf_op jit(solution)/shard_map/ppermute | solution.py:374
  42.0 20.5 %collective-permute-start.18 = (bf16[512,512]{1,0:T(8,128)(2,1)S(1)}, bf16[512,512]{1,0:T(8,128)(2,1)S(1)}, u32[]{:S(2)}, u32[]{:S(2)}) collective-permute-start(bf16[512,512]{1,0:T(8,128)(2,1)S(1)} %get-tuple-element.153), channel_id=1, source_target_pairs={{0,1},{1,0},{2,3},{3,2},{4,5},{5,4},{6,7},{7,6},{8,9},{9,8},{10,11... | collective-permute-start | bytes 1572872 | tf_op jit(solution)/shard_map/ppermute | solution.py:374
  43.9 20.5 %collective-permute-start.4 = (bf16[512,512]{1,0:T(8,128)(2,1)S(1)}, bf16[512,512]{1,0:T(8,128)(2,1)S(1)}, u32[]{:S(2)}, u32[]{:S(2)}) collective-permute-start(bf16[512,512]{1,0:T(8,128)(2,1)S(1)} %get-tuple-element.136), channel_id=1, source_target_pairs={{0,1},{1,0},{2,3},{3,2},{4,5},{5,4},{6,7},{7,6},{8,9},{9,8},{10,11... | collective-permute-start | bytes 1572872 | tf_op jit(solution)/shard_map/ppermute | solution.py:374
  53.3 6.2 %collective-permute-start.13 = (bf16[192,512]{1,0:T(8,128)(2,1)S(1)}, bf16[192,512]{1,0:T(8,128)(2,1)S(1)}, u32[]{:S(2)}, u32[]{:S(2)}) collective-permute-start(bf16[192,512]{1,0:T(8,128)(2,1)S(1)} %get-tuple-element.148), channel_id=1, source_target_pairs={{0,4},{1,5},{2,6},{3,7},{4,0},{5,1},{6,2},{7,3},{8,12},{9,13},{10,... | collective-permute-start | bytes 589832 | tf_op jit(solution)/shard_map/ppermute | solution.py:374
  59.5 11.6 %collective-permute-start.14 = (bf16[192,512]{1,0:T(8,128)(2,1)S(1)}, bf16[192,512]{1,0:T(8,128)(2,1)S(1)}, u32[]{:S(2)}, u32[]{:S(2)}) collective-permute-start(bf16[192,512]{1,0:T(8,128)(2,1)S(1)} %mesh_add.6.refs_0_), channel_id=1, source_target_pairs={{0,8},{1,9},{2,10},{3,11},{4,12},{5,13},{6,14},{7,15},{8,0},{9,1},... | collective-permute-start | bytes 589832 | tf_op jit(solution)/shard_map/ppermute | solution.py:374
  62.6 12.4 %collective-permute-start.19 = (bf16[256,512]{1,0:T(8,128)(2,1)S(1)}, bf16[256,512]{1,0:T(8,128)(2,1)S(1)}, u32[]{:S(2)}, u32[]{:S(2)}) collective-permute-start(bf16[256,512]{1,0:T(8,128)(2,1)S(1)} %get-tuple-element.155), channel_id=1, source_target_pairs={{0,4},{1,5},{2,6},{3,7},{4,0},{5,1},{6,2},{7,3},{8,12},{9,13},{10,... | collective-permute-start | bytes 786440 | tf_op jit(solution)/shard_map/ppermute | solution.py:374
  64.6 16.1 %collective-permute-start.5 = (bf16[256,512]{1,0:T(8,128)(2,1)S(1)}, bf16[256,512]{1,0:T(8,128)(2,1)S(1)}, u32[]{:S(2)}, u32[]{:S(2)}) collective-permute-start(bf16[256,512]{1,0:T(8,128)(2,1)S(1)} %get-tuple-element.138), channel_id=1, source_target_pairs={{0,4},{1,5},{2,6},{3,7},{4,0},{5,1},{6,2},{7,3},{8,12},{9,13},{10,... | collective-permute-start | bytes 786440 | tf_op jit(solution)/shard_map/ppermute | solution.py:374
  71.2 11.7 %collective-permute-start.15 = (bf16[192,512]{1,0:T(8,128)(2,1)S(1)}, bf16[192,512]{1,0:T(8,128)(2,1)S(1)}, u32[]{:S(2)}, u32[]{:S(2)}) collective-permute-start(bf16[192,512]{1,0:T(8,128)(2,1)S(1)} %mesh_add.7.refs_0_), channel_id=1, source_target_pairs={{0,4},{1,5},{2,6},{3,7},{4,0},{5,1},{6,2},{7,3},{8,12},{9,13},{10,... | collective-permute-start | bytes 589832 | tf_op jit(solution)/shard_map/ppermute | solution.py:374
  75.2 9.1 %collective-permute-start.20 = (bf16[128,512]{1,0:T(8,128)(2,1)S(1)}, bf16[128,512]{1,0:T(8,128)(2,1)S(1)}, u32[]{:S(2)}, u32[]{:S(2)}) collective-permute-start(bf16[128,512]{1,0:T(8,128)(2,1)S(1)} %get-tuple-element.157), channel_id=1, source_target_pairs={{0,2},{1,3},{2,0},{3,1},{4,6},{5,7},{6,4},{7,5},{8,10},{9,11},{10,... | collective-permute-start | bytes 393224 | tf_op jit(solution)/shard_map/ppermute | solution.py:374
  80.8 6.4 %collective-permute-start.6 = (bf16[128,512]{1,0:T(8,128)(2,1)S(1)}, bf16[128,512]{1,0:T(8,128)(2,1)S(1)}, u32[]{:S(2)}, u32[]{:S(2)}) collective-permute-start(bf16[128,512]{1,0:T(8,128)(2,1)S(1)} %get-tuple-element.140), channel_id=1, source_target_pairs={{0,2},{1,3},{2,0},{3,1},{4,6},{5,7},{6,4},{7,5},{8,10},{9,11},{10,... | collective-permute-start | bytes 393224 | tf_op jit(solution)/shard_map/ppermute | solution.py:374
  83.0 19.9 %collective-permute-start.16 = (bf16[384,512]{1,0:T(8,128)(2,1)S(1)}, bf16[384,512]{1,0:T(8,128)(2,1)S(1)}, u32[]{:S(2)}, u32[]{:S(2)}) collective-permute-start(bf16[384,512]{1,0:T(8,128)(2,1)S(1)} %mesh_join.2.refs_0_), channel_id=1, source_target_pairs={{0,2},{1,3},{2,0},{3,1},{4,6},{5,7},{6,4},{7,5},{8,10},{9,11},{10,... | collective-permute-start | bytes 1179656 | tf_op jit(solution)/shard_map/ppermute | solution.py:374
  84.4 10.5 %collective-permute-start.21 = (bf16[128,512]{1,0:T(8,128)(2,1)S(1)}, bf16[128,512]{1,0:T(8,128)(2,1)S(1)}, u32[]{:S(2)}, u32[]{:S(2)}) collective-permute-start(bf16[128,512]{1,0:T(8,128)(2,1)S(1)} %process_add.6.refs_0_), channel_id=1, source_target_pairs={{0,8},{1,9},{2,10},{3,11},{4,12},{5,13},{6,14},{7,15},{8,0},{9,1},... | collective-permute-start | bytes 393224 | tf_op jit(solution)/shard_map/ppermute | solution.py:374
  87.2 9.8 %collective-permute-start.7 = (bf16[128,512]{1,0:T(8,128)(2,1)S(1)}, bf16[128,512]{1,0:T(8,128)(2,1)S(1)}, u32[]{:S(2)}, u32[]{:S(2)}) collective-permute-start(bf16[128,512]{1,0:T(8,128)(2,1)S(1)} %grid_add.6.refs_0_), channel_id=1, source_target_pairs={{0,8},{1,9},{2,10},{3,11},{4,12},{5,13},{6,14},{7,15},{8,0},{9,1},... | collective-permute-start | bytes 393224 | tf_op jit(solution)/shard_map/ppermute | solution.py:374
  94.9 5.8 %collective-permute-start.22 = (bf16[128,512]{1,0:T(8,128)(2,1)S(1)}, bf16[128,512]{1,0:T(8,128)(2,1)S(1)}, u32[]{:S(2)}, u32[]{:S(2)}) collective-permute-start(bf16[128,512]{1,0:T(8,128)(2,1)S(1)} %process_add.7.refs_0_), channel_id=1, source_target_pairs={{0,2},{1,3},{2,0},{3,1},{4,6},{5,7},{6,4},{7,5},{8,10},{9,11},{10,... | collective-permute-start | bytes 393224 | tf_op jit(solution)/shard_map/ppermute | solution.py:374
  97.1 5.6 %collective-permute-start.8 = (bf16[128,512]{1,0:T(8,128)(2,1)S(1)}, bf16[128,512]{1,0:T(8,128)(2,1)S(1)}, u32[]{:S(2)}, u32[]{:S(2)}) collective-permute-start(bf16[128,512]{1,0:T(8,128)(2,1)S(1)} %grid_add.7.refs_0_), channel_id=1, source_target_pairs={{0,2},{1,3},{2,0},{3,1},{4,6},{5,7},{6,4},{7,5},{8,10},{9,11},{10,... | collective-permute-start | bytes 393224 | tf_op jit(solution)/shard_map/ppermute | solution.py:374
  100.7 9.0 %collective-permute-start.23 = (bf16[256,512]{1,0:T(8,128)(2,1)S(1)}, bf16[256,512]{1,0:T(8,128)(2,1)S(1)}, u32[]{:S(2)}, u32[]{:S(2)}) collective-permute-start(bf16[256,512]{1,0:T(8,128)(2,1)S(1)} %process_join.2.refs_0_), channel_id=1, source_target_pairs={{0,4},{1,5},{2,6},{3,7},{4,0},{5,1},{6,2},{7,3},{8,12},{9,13},{10,... | collective-permute-start | bytes 786440 | tf_op jit(solution)/shard_map/ppermute | solution.py:374
  102.8 10.0 %collective-permute-start.9 = (bf16[256,512]{1,0:T(8,128)(2,1)S(1)}, bf16[256,512]{1,0:T(8,128)(2,1)S(1)}, u32[]{:S(2)}, u32[]{:S(2)}) collective-permute-start(bf16[256,512]{1,0:T(8,128)(2,1)S(1)} %grid_join.2.refs_0_), channel_id=1, source_target_pairs={{0,4},{1,5},{2,6},{3,7},{4,0},{5,1},{6,2},{7,3},{8,12},{9,13},{10,... | collective-permute-start | bytes 786440 | tf_op jit(solution)/shard_map/ppermute | solution.py:374
  103.0 13.2 %collective-permute-start.17 = (bf16[768,512]{1,0:T(8,128)(2,1)S(1)}, bf16[768,512]{1,0:T(8,128)(2,1)S(1)}, u32[]{:S(2)}, u32[]{:S(2)}) collective-permute-start(bf16[768,512]{1,0:T(8,128)(2,1)S(1)} %mesh_join.3.refs_0_), channel_id=1, source_target_pairs={{0,1},{1,0},{2,3},{3,2},{4,5},{5,4},{6,7},{7,6},{8,9},{9,8},{10,11... | collective-permute-start | bytes 2359304 | tf_op jit(solution)/shard_map/ppermute | solution.py:374
  109.7 3.2 %collective-permute-start.24 = (bf16[512,512]{1,0:T(8,128)(2,1)S(1)}, bf16[512,512]{1,0:T(8,128)(2,1)S(1)}, u32[]{:S(2)}, u32[]{:S(2)}) collective-permute-start(bf16[512,512]{1,0:T(8,128)(2,1)S(1)} %process_join.3.refs_0_), channel_id=1, source_target_pairs={{0,1},{1,0},{2,3},{3,2},{4,5},{5,4},{6,7},{7,6},{8,9},{9,8},{10,11... | collective-permute-start | bytes 1572872 | tf_op jit(solution)/shard_map/ppermute | solution.py:374
  (2 other events, 4.3 us)

commit v3 on v2

--- a/solution.py
+++ b/solution.py
@@ -11,6 +11,10 @@
 F32 = jnp.float32
 VMEM_BYTES = 16 * 1024 * 1024
 BLOCKS = 8
+ORDER_P, ORDER_M, ORDER_G = (1, 2, 4), (1, 2, 4), (1, 4, 2)
+PLAN = "p2 mesh1 m2 grid2 p2 g2 m2 g2 p2 m2 p2 g2 p2 m2 g2 p2 m2 g2 p2 m2 g2 p2 g2 m2 g2 m2"
+WEIGHTS = (1, 10**9, 10**10, 10**11)
+FIRST = (0, 0, 0, 0, 0, 0)
 
 
 def dot(a, b):
@@ -85,13 +89,15 @@
         self.send()
 
 
-def call(body, name, ins, outs, scratch=(), place=False):
+def call(body, name, ins, outs, scratch=(), place=False, after=None, weight=0):
     kept = [v for v in ins if isinstance(v, Kept)]
     far_in = [isinstance(v, (Far, Kept)) for v in ins]
     far_out = [len(v) > 2 for v in outs]
     n_in, n_out, n_kept = len(ins), len(outs), len(kept)
+    lead = () if after is None else (after,)
 
     def kernel(*refs):
+        refs = refs[len(lead) :]
         sources, targets = refs[:n_in], refs[n_in : n_in + n_out]
         kept_refs = list(refs[n_in + n_out : n_in + n_out + n_kept])
         rest = list(refs[n_in + n_out + n_kept :])
@@ -106,8 +112,8 @@
                 inputs.append(Input(sources[i]))
         for i, is_far in enumerate(far_out):
             outputs.append(Output(targets[i], rest.pop(0), out_sems.at[i]) if is_far else Output(targets[i]))
-        lead = (lax.axis_index("space").astype(jnp.int32) & (BLOCKS - 1),) if place else ()
-        body(*lead, inputs, outputs, rest)
+        where = (lax.axis_index("space").astype(jnp.int32) & (BLOCKS - 1),) if place else ()
+        body(*where, inputs, outputs, rest)
         for value in inputs:
             value()
         for value in outputs:
@@ -125,13 +131,14 @@
         name=name,
         out_shape=[(pltpu.HBM if far else pltpu.VMEM)(v[0], v[1]) for v, far in zip(outs, far_out)]
         + [pltpu.VMEM(v.shape, v.dtype) for v in kept],
-        in_specs=[anywhere if far else near for far in far_in],
+        in_specs=[anywhere] * len(lead) + [anywhere if far else near for far in far_in],
         out_specs=[anywhere if far else near for far in far_out] + [near] * n_kept,
         scratch_shapes=held
         + [pltpu.VMEM(shape, dtype) for shape, dtype in scratch]
         + [pltpu.SemaphoreType.DMA((n_in,)), pltpu.SemaphoreType.DMA((max(n_out, 1),))],
         compiler_params=pltpu.CompilerParams(vmem_limit_bytes=VMEM_BYTES),
-    )(*(v.value if far else v for v, far in zip(ins, far_in)))
+        cost_estimate=pl.CostEstimate(flops=WEIGHTS[weight], bytes_accessed=1, transcendentals=0),
+    )(*lead, *(v.value if far else v for v, far in zip(ins, far_in)))
 
 
 def pick_body(ins, outs, _):
@@ -374,23 +381,33 @@
     return lax.ppermute(value, "space", [(i, i ^ step) for i in range(n)])
 
 
-def all_sum(name, keep, send, order, rest):
-    for i, step in enumerate(order):
-        rows, width = keep.shape
-        if i + 1 < len(order):
-            outs = [((rows // 2, width), F32), ((rows // 2, width), BF)]
+class Sum:
+    def __init__(self, name, order, rest, keep, send, outs, scratch=()):
+        self.name, self.order, self.outs, self.scratch = name, order, [(*v, "far") for v in outs], scratch
+        halve = [("halve", order[i + 1]) for i in range(len(order) - 1)]
+        whole = [("add", step) for step in (*rest, order[-1])]
+        double = [("join", step) for step in order[-2::-1]]
+        self.steps = halve + whole + double
+        self.value, self.results = keep, None
+        self.coming = exchange(send, order[0])
+
+    def step(self, after, weight):
+        rows, width = self.value.shape
+        ins = [self.value, self.coming]
+        if not self.steps:
+            body = functools.partial(collect_body, self.order)
+            self.results = call(body, f"{self.name}_collect", ins, self.outs, self.scratch, True, after, weight)
+            return self.value
+        kind, step = self.steps.pop(0)
+        if kind == "halve":
+            made = [((rows // 2, width), F32), ((rows // 2, width), BF)]
+            self.value, sent = call(add_body, f"{self.name}_add", ins, made, after=after, weight=weight)
         else:
-            outs = [((rows, width), BF)]
-        got = call(add_body, f"{name}_add", [keep, exchange(send, step)], outs)
-        if i + 1 < len(order):
-            keep, send = got
-    (value,) = got
-    for step in rest:
-        (value,) = call(add_body, f"{name}_add", [value, exchange(value, step)], [(value.shape, BF)])
-    for step in order[:0:-1]:
-        rows, width = value.shape
-        (value,) = call(join_body, f"{name}_join", [value, exchange(value, step)], [((2 * rows, width), BF)])
-    return value, exchange(value, order[0])
+            body, made = (add_body, rows) if kind == "add" else (join_body, 2 * rows)
+            (self.value,) = call(body, f"{self.name}_{kind}", ins, [((made, width), BF)], after=after, weight=weight)
+            sent = self.value
+        self.coming = exchange(sent, step)
+        return self.value
 
 
 def passed_along(block, distance):
@@ -403,10 +420,7 @@
     w_embed, enc_send, enc_recv, enc_out, proc_send, proc_recv, proc_out,
 ):
     n = lax.axis_size("space")
-    bits = [1 << i for i in range(n.bit_length() - 1)]
-    y_first = tuple(bits[:3])
-    z_first = (bits[0], bits[2], bits[1])
-    rest = tuple(bits[3:])
+    rest = tuple(1 << i for i in range(3, n.bit_length() - 1))
     near, fin = grid_inputs.shape
     m, width = mesh_latent.shape
     edges_e = m * enc_slot.shape[1]
@@ -418,7 +432,9 @@
     )
     halo = halo_list[0]
 
-    (outgoing,) = call(pick_body, "pick", [Far(sends_t), Far(x_t)], [((far, fin), BF, "far")])
+    (outgoing,) = call(
+        pick_body, "pick", [Far(sends_t), Far(x_t)], [((far, fin), BF, "far")], weight=FIRST[0]
+    )
     incoming = lax.all_to_all(outgoing.reshape(n, -1, fin), "space", split_axis=0, concat_axis=0, tiled=True)
     x_far = incoming.reshape(far, fin)
 
@@ -430,6 +446,7 @@
         [Far(x_t), Kept(w_embed), Kept(enc_send), Kept(mesh_latent), Far(enc_recv), Kept(enc_out), Kept(proc_send),
          Kept(halo), Kept(enc_slot_t), Kept(enc_mask_t)],
         [(*grid_rows, "far"), (*grid_rows, "far"), grid_rows, patch_f32],
+        weight=FIRST[1],
     )
 
     mid, to_left, to_right, mesh_proj, agg, y, r, slope, lat_far, slope_far = call(
@@ -451,6 +468,7 @@
         "load",
         [Kept(v) for v in (x_t, lat, slope_near, proc_recv, proc_out, cotangent, proc_slot_t, proc_mask_t)],
         [],
+        weight=FIRST[3],
     )
 
     wide = m + 2 * depth
@@ -461,6 +479,7 @@
         [(*patch, "far"), edge_rows, edge_rows, patch_f32, patch_f32, patch, patch, patch],
         [((wide, width), BF), ((edges_p, wide), BF), ((wide, edges_p), BF), ((edges_p, width), F32),
          ((edges_p, width), F32), ((edges_p, width), BF)],
+        weight=FIRST[4],
     )
 
     back_right = passed_along(back_to_left, -1)
@@ -472,41 +491,49 @@
 
     square = ((width, width), F32)
 
-    def collected(name, order, pair, outs, scratch=()):
-        outs = [(*v, "far") for v in outs]
-        return call(functools.partial(collect_body, order), name, pair, outs, scratch, True)
-
-    keep_p, send_p = call(
-        functools.partial(process_grads_body, z_first), "process_grads", [agg2, grad_u, mid, grad_recv], halves(2),
-        [square] * 2, True,
-    )
-    grad_rows, keep_p, send_p = lax.optimization_barrier((grad_rows, keep_p, send_p))
-    first = all_sum("process", keep_p, send_p, z_first, rest)
-
-    keep_m, send_m, grad_table = call(
-        functools.partial(mesh_grads_body, y_first),
-        "mesh_grads",
-        [enc_slot_t, back_left, back_right, halo, grad_rows, proc_send, grad_mid, y, r, enc_out, slope, mid, agg,
-         latent],
-        halves(3) + [((near + far, width), BF)],
-        [((near + far, edges_e), BF), ((edges_e, width), BF)] + [square] * 3,
-        True,
-    )
-    second = all_sum("mesh", keep_m, send_m, y_first, rest)
-
-    keep_g, send_g = call(
-        functools.partial(grid_grads_body, z_first),
-        "grid_grads",
-        [grad_table, enc_send, slope_near, slope_far, x_t, x_far, lat, lat_far],
-        halves(2),
-        [square] * 2,
-        True,
-    )
-    third = all_sum("grid", keep_g, send_g, z_first, rest)
-
-    g_pout, g_precv = collected("collect_process", z_first, first, [square] * 2)
-    g_psend, g_eout, g_erecv = collected("collect_mesh", y_first, second, [square] * 3)
-    g_esend, g_embed = collected("collect_grid", z_first, third, [square, ((fin, width), F32)], [square])
+    keep, send = call(
+        functools.partial(process_grads_body, ORDER_P), "process_grads", [agg2, grad_u, mid, grad_recv], halves(2),
+        [square] * 2, True, weight=FIRST[5],
+    )
+    sums = {"p": Sum("process", ORDER_P, rest, keep, send, [square] * 2)}
+    token = keep
+    for item in PLAN.split():
+        item, weight = item[:-1], int(item[-1])
+        if item == "mesh":
+            keep, send, grad_table = call(
+                functools.partial(mesh_grads_body, ORDER_M),
+                "mesh_grads",
+                [enc_slot_t, back_left, back_right, halo, grad_rows, proc_send, grad_mid, y, r, enc_out, slope, mid,
+                 agg, latent],
+                halves(3) + [((near + far, width), BF)],
+                [((near + far, edges_e), BF), ((edges_e, width), BF)] + [square] * 3,
+                True,
+                token,
+                weight,
+            )
+            token = keep
+            sums["m"] = Sum("mesh", ORDER_M, rest, keep, send, [square] * 3)
+        elif item == "grid":
+            keep, send = call(
+                functools.partial(grid_grads_body, ORDER_G),
+                "grid_grads",
+                [grad_table, enc_send, slope_near, slope_far, x_t, x_far, lat, lat_far],
+                halves(2),
+                [square] * 2,
+                True,
+                token,
+                weight,
+            )
+            token = keep
+            sums["g"] = Sum("grid", ORDER_G, rest, keep, send, [square, ((fin, width), F32)], [square])
+        else:
+            token = sums[item].step(token, weight)
+    for total in sums.values():
+        while total.results is None:
+            token = total.step(token, 0)
+    g_pout, g_precv = sums["p"].results
+    g_psend, g_eout, g_erecv = sums["m"].results
+    g_esend, g_embed = sums["g"].results
     return out, g_embed, g_esend, g_erecv, g_eout, g_psend, g_precv, g_pout
 
 

time: 119 us -> 104 us (0.87)
  waiting for transfers between devices: 62.3 us -> 49 us
    ppermute x21, waiting for transfers between devices: 56.1 us -> 42.3 us  [exchange(): return lax.ppermute(value, 'space', [(i, i ^ step) for i in range(n)])]
  transfers between devices with their start and end apart: 26 -> 26, of which waited for: 19 -> 17; matrix products, arithmetic and copies ran while one was open for 0% -> 0% of each run, Pallas kernels for 10% -> 11%
where the time goes in v3:
time: 104 us
  waiting for transfers between devices  49 us (47%)
  starting transfers between devices  30 us (29%)
  Pallas kernels  23.7 us (23%)
  between operations  1.17 us (1%)
    ppermute x21, waiting for transfers between devices, exchange(): return lax.ppermute(value, 'space', [(i, i ^ step) for i in range(n)])  42.3 us
    pallas_call x29, Pallas kernels, call(): pl.pallas_call(kernel, name=name, out_shape=[(pltpu.HBM if far else pltpu...  23.7 us
    ppermute x21, starting transfers between devices, exchange(): return lax.ppermute(value, 'space', [(i, i ^ step) for i in range(n)])  13.3 us
    ppermute x4, starting transfers between devices, passed_along(): lax.ppermute(block, 'space', [((i - distance) % n, i) for i in range(n)])  9.23 us
    all_to_all x1, starting transfers between devices, local(): lax.all_to_all(outgoing.reshape(n, -1, fin), 'space', split_axis=0, conca...  7.4 us
    all_to_all x1, waiting for transfers between devices, local(): lax.all_to_all(outgoing.reshape(n, -1, fin), 'space', split_axis=0, conca...  4.73 us
  transfers between devices with their start and end apart: 26, of which 17 were waited for; matrix products, arithmetic and copies ran while one was open for 0% of the time, Pallas kernels for 11%

profile of v3, /device:TPU:0, one launch (start us, length us, event | category | flops | bytes accessed | tf_op | source)
XLA Modules:
  0.0 103.8 jit_solution(14348801226785115538)
XLA Ops:
  0.6 2.0 %pick.1 = bf16[128,474]{1,0:T(8,128)(2,1)} custom-call(s32[8,16]{1,0:T(8,128)} %bitcast.21, bf16[474,512]{1,0:T(8,128)(2,1)} %bitcast.13), custom_call_target="tpu_custom_call" | custom-call | flops 1 | bytes 1 | tf_op jit(solution)/shard_map/pick/pallas_call | solution.py:129
  2.7 7.4 %all-to-all-start = ((bf16[16,8,474]{2,1,0:T(8,128)(2,1)}), bf16[16,8,474]{2,1,0:T(8,128)(2,1)S(1)}, u32[]{:S(2)}, u32[]{:S(2)}) async-start(bf16[16,8,474]{2,1,0:T(8,128)(2,1)} %bitcast.16), calls=%async_computation | async-start | bytes 262144 | tf_op jit(solution)/shard_map/all_to_all | solution.py:438
  10.1 3.2 %embed.1 = (bf16[512,512]{1,0:T(8,128)(2,1)}, bf16[512,512]{1,0:T(8,128)(2,1)}, bf16[512,512]{1,0:T(8,128)(2,1)S(1)}, f32[64,512]{1,0:T(8,128)S(1)}, bf16[474,51...) custom-call(bf16[474,512]{1,0:T(8,128)(2,1)} %bitcast.14, ...), custom_call_target="tpu_custom_call" | custom-call | flops 1 | bytes 1 | tf_op jit(solution)/shard_map/embed/pallas_call | solution.py:129
  13.3 4.7 %all-to-all-done = bf16[16,8,474]{2,1,0:T(8,128)(2,1)S(1)} async-done(((bf16[16,8,474]{2,1,0:T(8,128)(2,1)}), bf16[16,8,474]{2,1,0:T(8,128)(2,1)S(1)}, u32[]{:S(2)}, u32[]{:S(2)}) %all-to-all-start) | async-done | bytes 121376 | tf_op jit(solution)/shard_map/all_to_all | solution.py:438
  18.0 3.0 %encode.1 = (bf16[64,512]{1,0:T(8,128)(2,1)S(1)}, bf16[64,512]{1,0:T(8,128)(2,1)S(1)}, bf16[64,512]{1,0:T(8,128)(2,1)S(1)}, bf16[64,512]{1,0:T(8,128)(2,1)S(1)},...) custom-call(s32[16,64]{1,0:T(8,128)S(1)} %get-tuple-element.83.refs_, ...), custom_call_target="tpu_custom_call" | custom-call | flops 1 | bytes 1 | tf_op jit(solution)/shard_map/encode/pallas_call | solution.py:129
  21.1 4.4 %collective-permute-start.1 = (bf16[64,512]{1,0:T(8,128)(2,1)S(1)}, bf16[64,512]{1,0:T(8,128)(2,1)S(1)}, u32[]{:S(2)}, u32[]{:S(2)}) collective-permute-start(bf16[64,512]{1,0:T(8,128)(2,1)S(1)} %get-tuple-element.106), channel_id=1, source_target_pairs={{1,0},{2,1},{3,2},{4,3},{5,4},{6,5},{7,6},{8,7},{9,8},{10,9},{11,1... | collective-permute-start | bytes 196616 | tf_op jit(solution)/shard_map/ppermute | solution.py:415
  27.5 3.0 %process.1 = (bf16[64,512]{1,0:T(8,128)(2,1)}, bf16[64,512]{1,0:T(8,128)(2,1)S(1)}, bf16[64,512]{1,0:T(8,128)(2,1)S(1)}, f32[64,512]{1,0:T(8,128)S(1)}, f32[64,5...) custom-call(s32[16,64]{1,0:T(8,128)S(1)} %get-tuple-element.102.refs_0_,, ...), custom_call_target="tpu_custom_call" | custom-call | flops 1 | bytes 1 | tf_op jit(solution)/shard_map/process/pallas_call | solution.py:129
  31.6 4.2 %collective-permute-start.4 = (bf16[64,512]{1,0:T(8,128)(2,1)S(1)}, bf16[64,512]{1,0:T(8,128)(2,1)S(1)}, u32[]{:S(2)}, u32[]{:S(2)}) collective-permute-start(bf16[64,512]{1,0:T(8,128)(2,1)S(1)} %get-tuple-element.119), channel_id=1, source_target_pairs={{1,0},{2,1},{3,2},{4,3},{5,4},{6,5},{7,6},{8,7},{9,8},{10,9},{11,1... | collective-permute-start | bytes 196616 | tf_op jit(solution)/shard_map/ppermute | solution.py:415
  37.8 2.3 %mesh_grads.1 = (f32[768,512]{1,0:T(8,128)S(1)}, bf16[768,512]{1,0:T(8,128)(2,1)S(1)}, bf16[640,512]{1,0:T(8,128)(2,1)S(1)}) custom-call(f32[256,512]{1,0:T(8,128)S(1)} %get-tuple-element.117.refs_0_.refs_1_, s32[16,64]{1,0:T(8,128)S(1)} %get-tuple-element.83.refs_0_.refs_1_, bf16[64,512]{1,0:T(8,128)(2,1)S(1)} %collective-permute-done.3.refs_2_, ...), custom_call_target="tpu_custom_call" | custom-call | flops 1000000000 | bytes 1 | tf_op jit(solution)/shard_map/mesh_grads/pallas_call | solution.py:129
  40.3 2.2 %collective-permute-done.5.refs_2_ = bf16[768,512]{1,0:T(8,128)(2,1)S(1)} collective-permute-done((bf16[768,512]{1,0:T(8,128)(2,1)S(1)}, bf16[768,512]{1,0:T(8,128)(2,1)S(1)}, u32[]{:S(2)}, u32[]{:S(2)}) %collective-permute-start.5) | collective-permute-done | bytes 786464 | tf_op jit(solution)/shard_map/ppermute | solution.py:381
  44.5 4.8 %collective-permute-done.6.refs_2_ = bf16[256,512]{1,0:T(8,128)(2,1)S(1)} collective-permute-done((bf16[256,512]{1,0:T(8,128)(2,1)S(1)}, bf16[256,512]{1,0:T(8,128)(2,1)S(1)}, u32[]{:S(2)}, u32[]{:S(2)}) %collective-permute-start.6) | collective-permute-done | bytes 262176 | tf_op jit(solution)/shard_map/ppermute | solution.py:381
  49.7 2.1 %collective-permute-start.9 = (bf16[256,512]{1,0:T(8,128)(2,1)S(1)}, bf16[256,512]{1,0:T(8,128)(2,1)S(1)}, u32[]{:S(2)}, u32[]{:S(2)}) collective-permute-start(bf16[256,512]{1,0:T(8,128)(2,1)S(1)} %get-tuple-element.142), channel_id=1, source_target_pairs={{0,4},{1,5},{2,6},{3,7},{4,0},{5,1},{6,2},{7,3},{8,12},{9,13},{10,... | collective-permute-start | bytes 786440 | tf_op jit(solution)/shard_map/ppermute | solution.py:381
  51.7 5.6 %collective-permute-done.8.refs_2_ = bf16[384,512]{1,0:T(8,128)(2,1)S(1)} collective-permute-done((bf16[384,512]{1,0:T(8,128)(2,1)S(1)}, bf16[384,512]{1,0:T(8,128)(2,1)S(1)}, u32[]{:S(2)}, u32[]{:S(2)}) %collective-permute-start.8) | collective-permute-done | bytes 393248 | tf_op jit(solution)/shard_map/ppermute | solution.py:381
  57.5 2.2 %collective-permute-done.9.refs_2_ = bf16[256,512]{1,0:T(8,128)(2,1)S(1)} collective-permute-done((bf16[256,512]{1,0:T(8,128)(2,1)S(1)}, bf16[256,512]{1,0:T(8,128)(2,1)S(1)}, u32[]{:S(2)}, u32[]{:S(2)}) %collective-permute-start.9) | collective-permute-done | bytes 262176 | tf_op jit(solution)/shard_map/ppermute | solution.py:381
  59.9 2.5 %collective-permute-start.12 = (bf16[128,512]{1,0:T(8,128)(2,1)S(1)}, bf16[128,512]{1,0:T(8,128)(2,1)S(1)}, u32[]{:S(2)}, u32[]{:S(2)}) collective-permute-start(bf16[128,512]{1,0:T(8,128)(2,1)S(1)} %process_add.6.refs_0_.refs_1_), channel_id=1, source_target_pairs={{0,8},{1,9},{2,10},{3,11},{4,12},{5,13},{6,14},{7,15},{8,0},{9,1},... | collective-permute-start | bytes 393224 | tf_op jit(solution)/shard_map/ppermute | solution.py:381
  63.8 2.9 %collective-permute-done.11.refs_2_ = bf16[192,512]{1,0:T(8,128)(2,1)S(1)} collective-permute-done((bf16[192,512]{1,0:T(8,128)(2,1)S(1)}, bf16[192,512]{1,0:T(8,128)(2,1)S(1)}, u32[]{:S(2)}, u32[]{:S(2)}) %collective-permute-start.11) | collective-permute-done | bytes 196640 | tf_op jit(solution)/shard_map/ppermute | solution.py:381
  67.2 3.9 %collective-permute-done.12.refs_2_ = bf16[128,512]{1,0:T(8,128)(2,1)S(1)} collective-permute-done((bf16[128,512]{1,0:T(8,128)(2,1)S(1)}, bf16[128,512]{1,0:T(8,128)(2,1)S(1)}, u32[]{:S(2)}, u32[]{:S(2)}) %collective-permute-start.12) | collective-permute-done | bytes 131104 | tf_op jit(solution)/shard_map/ppermute | solution.py:381
  71.3 2.7 %collective-permute-start.16 = (bf16[128,512]{1,0:T(8,128)(2,1)S(1)}, bf16[128,512]{1,0:T(8,128)(2,1)S(1)}, u32[]{:S(2)}, u32[]{:S(2)}) collective-permute-start(bf16[128,512]{1,0:T(8,128)(2,1)S(1)} %grid_add.6.refs_0_.refs_1_), channel_id=1, source_target_pairs={{0,8},{1,9},{2,10},{3,11},{4,12},{5,13},{6,14},{7,15},{8,0},{9,1},... | collective-permute-start | bytes 393224 | tf_op jit(solution)/shard_map/ppermute | solution.py:381
  74.0 4.0 %collective-permute-done.14.refs_2_ = bf16[128,512]{1,0:T(8,128)(2,1)S(1)} collective-permute-done((bf16[128,512]{1,0:T(8,128)(2,1)S(1)}, bf16[128,512]{1,0:T(8,128)(2,1)S(1)}, u32[]{:S(2)}, u32[]{:S(2)}) %collective-permute-start.14) | collective-permute-done | bytes 131104 | tf_op jit(solution)/shard_map/ppermute | solution.py:381
  78.2 1.8 %collective-permute-done.15.refs_2_ = bf16[192,512]{1,0:T(8,128)(2,1)S(1)} collective-permute-done((bf16[192,512]{1,0:T(8,128)(2,1)S(1)}, bf16[192,512]{1,0:T(8,128)(2,1)S(1)}, u32[]{:S(2)}, u32[]{:S(2)}) %collective-permute-start.15) | collective-permute-done | bytes 196640 | tf_op jit(solution)/shard_map/ppermute | solution.py:381
  80.2 2.5 %collective-permute-done.16.refs_2_ = bf16[128,512]{1,0:T(8,128)(2,1)S(1)} collective-permute-done((bf16[128,512]{1,0:T(8,128)(2,1)S(1)}, bf16[128,512]{1,0:T(8,128)(2,1)S(1)}, u32[]{:S(2)}, u32[]{:S(2)}) %collective-permute-start.16) | collective-permute-done | bytes 131104 | tf_op jit(solution)/shard_map/ppermute | solution.py:381
  84.7 2.2 %collective-permute-done.18.refs_2_ = bf16[192,512]{1,0:T(8,128)(2,1)S(1)} collective-permute-done((bf16[192,512]{1,0:T(8,128)(2,1)S(1)}, bf16[192,512]{1,0:T(8,128)(2,1)S(1)}, u32[]{:S(2)}, u32[]{:S(2)}) %collective-permute-start.18) | collective-permute-done | bytes 196640 | tf_op jit(solution)/shard_map/ppermute | solution.py:381
  88.6 8.6 %collective-permute-done.19.refs_2_ = bf16[384,512]{1,0:T(8,128)(2,1)S(1)} collective-permute-done((bf16[384,512]{1,0:T(8,128)(2,1)S(1)}, bf16[384,512]{1,0:T(8,128)(2,1)S(1)}, u32[]{:S(2)}, u32[]{:S(2)}) %collective-permute-start.19) | collective-permute-done | bytes 393248 | tf_op jit(solution)/shard_map/ppermute | solution.py:381
  101.8 1.9 %mesh_collect.1 = (f32[512,512]{1,0:T(8,128)}, f32[512,512]{1,0:T(8,128)}, f32[512,512]{1,0:T(8,128)}) custom-call(bf16[512,512]{1,0:T(8,128)(2,1)S(1)} %grid_join.3.refs_1_.refs_0_, bf16[768,512]{1,0:T(8,128)(2,1)S(1)} %mesh_join.3.refs_0_.refs_1_, bf16[768,512]{1,0:T(8,128)(2,1)S(1)} %collective-permute-done.23.refs_2_), custom_call_target="tpu_custom_call" | custom-call | flops 10000000000 | bytes 1 | tf_op jit(solution)/shard_map/mesh_collect/pallas_call | solution.py:129
  (57 shorter events, 18.4 us)
Async XLA Ops:
  2.7 15.3 %all-to-all-start = ((bf16[16,8,474]{2,1,0:T(8,128)(2,1)}), bf16[16,8,474]{2,1,0:T(8,128)(2,1)S(1)}, u32[]{:S(2)}, u32[]{:S(2)}) async-start(bf16[16,8,474]{2,1,0:T(8,128)(2,1)} %bitcast.16), calls=%async_computation | async-start | bytes 262144 | tf_op jit(solution)/shard_map/all_to_all | solution.py:438
  21.0 6.4 %collective-permute-start = (bf16[64,512]{1,0:T(8,128)(2,1)S(1)}, bf16[64,512]{1,0:T(8,128)(2,1)S(1)}, u32[]{:S(2)}, u32[]{:S(2)}) collective-permute-start(bf16[64,512]{1,0:T(8,128)(2,1)S(1)} %get-tuple-element.105), channel_id=1, source_target_pairs={{15,0},{0,1},{1,2},{2,3},{3,4},{4,5},{5,6},{6,7},{7,8},{8,9},{9,10... | collective-permute-start | bytes 196616 | tf_op jit(solution)/shard_map/ppermute | solution.py:415
  21.1 6.4 %collective-permute-start.1 = (bf16[64,512]{1,0:T(8,128)(2,1)S(1)}, bf16[64,512]{1,0:T(8,128)(2,1)S(1)}, u32[]{:S(2)}, u32[]{:S(2)}) collective-permute-start(bf16[64,512]{1,0:T(8,128)(2,1)S(1)} %get-tuple-element.106), channel_id=1, source_target_pairs={{1,0},{2,1},{3,2},{4,3},{5,4},{6,5},{7,6},{8,7},{9,8},{10,9},{11,1... | collective-permute-start | bytes 196616 | tf_op jit(solution)/shard_map/ppermute | solution.py:415
  31.1 4.8 %collective-permute-start.2 = (bf16[512,512]{1,0:T(8,128)(2,1)S(1)}, bf16[512,512]{1,0:T(8,128)(2,1)S(1)}, u32[]{:S(2)}, u32[]{:S(2)}) collective-permute-start(bf16[512,512]{1,0:T(8,128)(2,1)S(1)} %get-tuple-element.116), channel_id=1, source_target_pairs={{0,1},{1,0},{2,3},{3,2},{4,5},{5,4},{6,7},{7,6},{8,9},{9,8},{10,11... | collective-permute-start | bytes 1572872 | tf_op jit(solution)/shard_map/ppermute | solution.py:381
  31.1 6.5 %collective-permute-start.3 = (bf16[64,512]{1,0:T(8,128)(2,1)S(1)}, bf16[64,512]{1,0:T(8,128)(2,1)S(1)}, u32[]{:S(2)}, u32[]{:S(2)}) collective-permute-start(bf16[64,512]{1,0:T(8,128)(2,1)S(1)} %get-tuple-element.118), channel_id=1, source_target_pairs={{15,0},{0,1},{1,2},{2,3},{3,4},{4,5},{5,6},{6,7},{7,8},{8,9},{9,10... | collective-permute-start | bytes 196616 | tf_op jit(solution)/shard_map/ppermute | solution.py:415
  31.6 6.2 %collective-permute-start.4 = (bf16[64,512]{1,0:T(8,128)(2,1)S(1)}, bf16[64,512]{1,0:T(8,128)(2,1)S(1)}, u32[]{:S(2)}, u32[]{:S(2)}) collective-permute-start(bf16[64,512]{1,0:T(8,128)(2,1)S(1)} %get-tuple-element.119), channel_id=1, source_target_pairs={{1,0},{2,1},{3,2},{4,3},{5,4},{6,5},{7,6},{8,7},{9,8},{10,9},{11,1... | collective-permute-start | bytes 196616 | tf_op jit(solution)/shard_map/ppermute | solution.py:415
  40.2 9.2 %collective-permute-start.6 = (bf16[256,512]{1,0:T(8,128)(2,1)S(1)}, bf16[256,512]{1,0:T(8,128)(2,1)S(1)}, u32[]{:S(2)}, u32[]{:S(2)}) collective-permute-start(bf16[256,512]{1,0:T(8,128)(2,1)S(1)} %get-tuple-element.136), channel_id=1, source_target_pairs={{0,2},{1,3},{2,0},{3,1},{4,6},{5,7},{6,4},{7,5},{8,10},{9,11},{10,... | collective-permute-start | bytes 786440 | tf_op jit(solution)/shard_map/ppermute | solution.py:381
  44.3 5.2 %collective-permute-start.7 = (bf16[512,512]{1,0:T(8,128)(2,1)S(1)}, bf16[512,512]{1,0:T(8,128)(2,1)S(1)}, u32[]{:S(2)}, u32[]{:S(2)}) collective-permute-start(bf16[512,512]{1,0:T(8,128)(2,1)S(1)} %get-tuple-element.138), channel_id=1, source_target_pairs={{0,1},{1,0},{2,3},{3,2},{4,5},{5,4},{6,7},{7,6},{8,9},{9,8},{10,11... | collective-permute-start | bytes 1572872 | tf_op jit(solution)/shard_map/ppermute | solution.py:381
  44.5 12.8 %collective-permute-start.8 = (bf16[384,512]{1,0:T(8,128)(2,1)S(1)}, bf16[384,512]{1,0:T(8,128)(2,1)S(1)}, u32[]{:S(2)}, u32[]{:S(2)}) collective-permute-start(bf16[384,512]{1,0:T(8,128)(2,1)S(1)} %get-tuple-element.140), channel_id=1, source_target_pairs={{0,2},{1,3},{2,0},{3,1},{4,6},{5,7},{6,4},{7,5},{8,10},{9,11},{10,... | collective-permute-start | bytes 1179656 | tf_op jit(solution)/shard_map/ppermute | solution.py:381
  49.4 10.4 %collective-permute-start.10 = (bf16[128,512]{1,0:T(8,128)(2,1)S(1)}, bf16[128,512]{1,0:T(8,128)(2,1)S(1)}, u32[]{:S(2)}, u32[]{:S(2)}) collective-permute-start(bf16[128,512]{1,0:T(8,128)(2,1)S(1)} %get-tuple-element.144), channel_id=1, source_target_pairs={{0,4},{1,5},{2,6},{3,7},{4,0},{5,1},{6,2},{7,3},{8,12},{9,13},{10,... | collective-permute-start | bytes 393224 | tf_op jit(solution)/shard_map/ppermute | solution.py:381
  49.7 10.1 %collective-permute-start.9 = (bf16[256,512]{1,0:T(8,128)(2,1)S(1)}, bf16[256,512]{1,0:T(8,128)(2,1)S(1)}, u32[]{:S(2)}, u32[]{:S(2)}) collective-permute-start(bf16[256,512]{1,0:T(8,128)(2,1)S(1)} %get-tuple-element.142), channel_id=1, source_target_pairs={{0,4},{1,5},{2,6},{3,7},{4,0},{5,1},{6,2},{7,3},{8,12},{9,13},{10,... | collective-permute-start | bytes 786440 | tf_op jit(solution)/shard_map/ppermute | solution.py:381
  57.4 9.2 %collective-permute-start.11 = (bf16[192,512]{1,0:T(8,128)(2,1)S(1)}, bf16[192,512]{1,0:T(8,128)(2,1)S(1)}, u32[]{:S(2)}, u32[]{:S(2)}) collective-permute-start(bf16[192,512]{1,0:T(8,128)(2,1)S(1)} %get-tuple-element.145), channel_id=1, source_target_pairs={{0,4},{1,5},{2,6},{3,7},{4,0},{5,1},{6,2},{7,3},{8,12},{9,13},{10,... | collective-permute-start | bytes 589832 | tf_op jit(solution)/shard_map/ppermute | solution.py:381
  59.9 11.2 %collective-permute-start.12 = (bf16[128,512]{1,0:T(8,128)(2,1)S(1)}, bf16[128,512]{1,0:T(8,128)(2,1)S(1)}, u32[]{:S(2)}, u32[]{:S(2)}) collective-permute-start(bf16[128,512]{1,0:T(8,128)(2,1)S(1)} %process_add.6.refs_0_.refs_1_), channel_id=1, source_target_pairs={{0,8},{1,9},{2,10},{3,11},{4,12},{5,13},{6,14},{7,15},{8,0},{9,1},... | collective-permute-start | bytes 393224 | tf_op jit(solution)/shard_map/ppermute | solution.py:381
  62.4 8.9 %collective-permute-start.13 = (bf16[128,512]{1,0:T(8,128)(2,1)S(1)}, bf16[128,512]{1,0:T(8,128)(2,1)S(1)}, u32[]{:S(2)}, u32[]{:S(2)}) collective-permute-start(bf16[128,512]{1,0:T(8,128)(2,1)S(1)} %get-tuple-element.146), channel_id=1, source_target_pairs={{0,2},{1,3},{2,0},{3,1},{4,6},{5,7},{6,4},{7,5},{8,10},{9,11},{10,... | collective-permute-start | bytes 393224 | tf_op jit(solution)/shard_map/ppermute | solution.py:381
  66.8 13.3 %collective-permute-start.15 = (bf16[192,512]{1,0:T(8,128)(2,1)S(1)}, bf16[192,512]{1,0:T(8,128)(2,1)S(1)}, u32[]{:S(2)}, u32[]{:S(2)}) collective-permute-start(bf16[192,512]{1,0:T(8,128)(2,1)S(1)} %mesh_add.6.refs_0_.refs_1_), channel_id=1, source_target_pairs={{0,8},{1,9},{2,10},{3,11},{4,12},{5,13},{6,14},{7,15},{8,0},{9,1},... | collective-permute-start | bytes 589832 | tf_op jit(solution)/shard_map/ppermute | solution.py:381
  71.2 6.9 %collective-permute-start.14 = (bf16[128,512]{1,0:T(8,128)(2,1)S(1)}, bf16[128,512]{1,0:T(8,128)(2,1)S(1)}, u32[]{:S(2)}, u32[]{:S(2)}) collective-permute-start(bf16[128,512]{1,0:T(8,128)(2,1)S(1)} %process_add.7.refs_0_.refs_1_), channel_id=1, source_target_pairs={{0,4},{1,5},{2,6},{3,7},{4,0},{5,1},{6,2},{7,3},{8,12},{9,13},{10,... | collective-permute-start | bytes 393224 | tf_op jit(solution)/shard_map/ppermute | solution.py:381
  71.3 11.4 %collective-permute-start.16 = (bf16[128,512]{1,0:T(8,128)(2,1)S(1)}, bf16[128,512]{1,0:T(8,128)(2,1)S(1)}, u32[]{:S(2)}, u32[]{:S(2)}) collective-permute-start(bf16[128,512]{1,0:T(8,128)(2,1)S(1)} %grid_add.6.refs_0_.refs_1_), channel_id=1, source_target_pairs={{0,8},{1,9},{2,10},{3,11},{4,12},{5,13},{6,14},{7,15},{8,0},{9,1},... | collective-permute-start | bytes 393224 | tf_op jit(solution)/shard_map/ppermute | solution.py:381
  78.1 6.4 %collective-permute-start.17 = (bf16[256,512]{1,0:T(8,128)(2,1)S(1)}, bf16[256,512]{1,0:T(8,128)(2,1)S(1)}, u32[]{:S(2)}, u32[]{:S(2)}) collective-permute-start(bf16[256,512]{1,0:T(8,128)(2,1)S(1)} %process_join.2.refs_0_.refs_1_), channel_id=1, source_target_pairs={{0,2},{1,3},{2,0},{3,1},{4,6},{5,7},{6,4},{7,5},{8,10},{9,11},{10,... | collective-permute-start | bytes 786440 | tf_op jit(solution)/shard_map/ppermute | solution.py:381
  80.1 6.8 %collective-permute-start.18 = (bf16[192,512]{1,0:T(8,128)(2,1)S(1)}, bf16[192,512]{1,0:T(8,128)(2,1)S(1)}, u32[]{:S(2)}, u32[]{:S(2)}) collective-permute-start(bf16[192,512]{1,0:T(8,128)(2,1)S(1)} %mesh_add.7.refs_0_.refs_1_), channel_id=1, source_target_pairs={{0,4},{1,5},{2,6},{3,7},{4,0},{5,1},{6,2},{7,3},{8,12},{9,13},{10,... | collective-permute-start | bytes 589832 | tf_op jit(solution)/shard_map/ppermute | solution.py:381
  82.8 5.5 %collective-permute-start.20 = (bf16[128,512]{1,0:T(8,128)(2,1)S(1)}, bf16[128,512]{1,0:T(8,128)(2,1)S(1)}, u32[]{:S(2)}, u32[]{:S(2)}) collective-permute-start(bf16[128,512]{1,0:T(8,128)(2,1)S(1)} %grid_add.7.refs_0_.refs_1_), channel_id=1, source_target_pairs={{0,2},{1,3},{2,0},{3,1},{4,6},{5,7},{6,4},{7,5},{8,10},{9,11},{10,... | collective-permute-start | bytes 393224 | tf_op jit(solution)/shard_map/ppermute | solution.py:381
  84.6 13.3 %collective-permute-start.24 = (bf16[512,512]{1,0:T(8,128)(2,1)S(1)}, bf16[512,512]{1,0:T(8,128)(2,1)S(1)}, u32[]{:S(2)}, u32[]{:S(2)}) collective-permute-start(bf16[512,512]{1,0:T(8,128)(2,1)S(1)} %process_join.3.refs_0_.refs_1_), channel_id=1, source_target_pairs={{0,1},{1,0},{2,3},{3,2},{4,5},{5,4},{6,7},{7,6},{8,9},{9,8},{10,11... | collective-permute-start | bytes 1572872 | tf_op jit(solution)/shard_map/ppermute | solution.py:381
  87.0 10.2 %collective-permute-start.19 = (bf16[384,512]{1,0:T(8,128)(2,1)S(1)}, bf16[384,512]{1,0:T(8,128)(2,1)S(1)}, u32[]{:S(2)}, u32[]{:S(2)}) collective-permute-start(bf16[384,512]{1,0:T(8,128)(2,1)S(1)} %mesh_join.2.refs_1_.refs_0_), channel_id=1, source_target_pairs={{0,2},{1,3},{2,0},{3,1},{4,6},{5,7},{6,4},{7,5},{8,10},{9,11},{10,... | collective-permute-start | bytes 1179656 | tf_op jit(solution)/shard_map/ppermute | solution.py:381
  88.3 9.0 %collective-permute-start.21 = (bf16[256,512]{1,0:T(8,128)(2,1)S(1)}, bf16[256,512]{1,0:T(8,128)(2,1)S(1)}, u32[]{:S(2)}, u32[]{:S(2)}) collective-permute-start(bf16[256,512]{1,0:T(8,128)(2,1)S(1)} %grid_join.2.refs_1_), channel_id=1, source_target_pairs={{0,4},{1,5},{2,6},{3,7},{4,0},{5,1},{6,2},{7,3},{8,12},{9,13},{10,... | collective-permute-start | bytes 786440 | tf_op jit(solution)/shard_map/ppermute | solution.py:381
  97.3 4.5 %collective-permute-start.23 = (bf16[768,512]{1,0:T(8,128)(2,1)S(1)}, bf16[768,512]{1,0:T(8,128)(2,1)S(1)}, u32[]{:S(2)}, u32[]{:S(2)}) collective-permute-start(bf16[768,512]{1,0:T(8,128)(2,1)S(1)} %mesh_join.3.refs_0_.refs_1_), channel_id=1, source_target_pairs={{0,1},{1,0},{2,3},{3,2},{4,5},{5,4},{6,7},{7,6},{8,9},{9,8},{10,11... | collective-permute-start | bytes 2359304 | tf_op jit(solution)/shard_map/ppermute | solution.py:381
  (2 other events, 5.3 us)

commit v4 on v3

--- a/solution.py
+++ b/solution.py
@@ -12,8 +12,8 @@
 VMEM_BYTES = 16 * 1024 * 1024
 BLOCKS = 8
 ORDER_P, ORDER_M, ORDER_G = (1, 2, 4), (1, 2, 4), (1, 4, 2)
-PLAN = "p2 mesh1 m2 grid2 p2 g2 m2 g2 p2 m2 p2 g2 p2 m2 g2 p2 m2 g2 p2 m2 g2 p2 g2 m2 g2 m2"
-WEIGHTS = (1, 10**9, 10**10, 10**11)
+PLAN = (("p", 3), ("mesh", 3), ("grid", 3), ("m", 3), ("p", 3), ("g", 3), ("p", 2), ("m", 3), ("g", 2), ("m", 3), ("p", 2), ("g", 3), ("p", 3), ("m", 3), ("g", 3), ("p", 3), ("m", 3), ("g", 3), ("p", 3), ("g", 3), ("m", 3), ("g", 4), ("m", 3))
+WEIGHTS = (1, 10**9, 3 * 10**9, 10**10, 3 * 10**10, 10**11)
 FIRST = (0, 0, 0, 0, 0, 0)
 
 
@@ -397,7 +397,7 @@
         if not self.steps:
             body = functools.partial(collect_body, self.order)
             self.results = call(body, f"{self.name}_collect", ins, self.outs, self.scratch, True, after, weight)
-            return self.value
+            return pltpu.with_memory_space_constraint(self.results[0], pltpu.HBM)
         kind, step = self.steps.pop(0)
         if kind == "halve":
             made = [((rows // 2, width), F32), ((rows // 2, width), BF)]
@@ -497,8 +497,7 @@
     )
     sums = {"p": Sum("process", ORDER_P, rest, keep, send, [square] * 2)}
     token = keep
-    for item in PLAN.split():
-        item, weight = item[:-1], int(item[-1])
+    for item, weight in PLAN:
         if item == "mesh":
             keep, send, grad_table = call(
                 functools.partial(mesh_grads_body, ORDER_M),

time: 104 us -> 96.9 us (0.932)
  waiting for transfers between devices: 49 us -> 40.3 us
  starting transfers between devices: 30 us -> 31.5 us
    ppermute x21, waiting for transfers between devices: 42.3 us -> 33.7 us  [exchange(): return lax.ppermute(value, 'space', [(i, i ^ step) for i in range(n)])]
    ppermute x21, starting transfers between devices: 13.3 us -> 14.8 us  [exchange(): return lax.ppermute(value, 'space', [(i, i ^ step) for i in range(n)])]
  transfers between devices with their start and end apart: 26 -> 26, of which waited for: 17 -> 17; matrix products, arithmetic and copies ran while one was open for 0% -> 0% of each run, Pallas kernels for 11% -> 14%
where the time goes in v4:
time: 96.9 us; the launch traced here: 96.6 us
  waiting for transfers between devices  40.3 us (42%)
  starting transfers between devices  31.5 us (33%)
  Pallas kernels  23.7 us (24%)
  between operations  1.13 us (1%)
    ppermute x21, waiting for transfers between devices, exchange(): return lax.ppermute(value, 'space', [(i, i ^ step) for i in range(n)])  33.7 us
    pallas_call x29, Pallas kernels, call(): pl.pallas_call(kernel, name=name, out_shape=[(pltpu.HBM if far else pltpu...  23.7 us
    ppermute x21, starting transfers between devices, exchange(): return lax.ppermute(value, 'space', [(i, i ^ step) for i in range(n)])  14.8 us
    ppermute x4, starting transfers between devices, passed_along(): lax.ppermute(block, 'space', [((i - distance) % n, i) for i in range(n)])  9.23 us
    all_to_all x1, starting transfers between devices, local(): lax.all_to_all(outgoing.reshape(n, -1, fin), 'space', split_axis=0, conca...  7.4 us
    all_to_all x1, waiting for transfers between devices, local(): lax.all_to_all(outgoing.reshape(n, -1, fin), 'space', split_axis=0, conca...  4.73 us
  transfers between devices with their start and end apart: 26, of which 17 were waited for; matrix products, arithmetic and copies ran while one was open for 0% of the time, Pallas kernels for 14%

profile of v4, /device:TPU:0, one launch (start us, length us, event | category | flops | bytes accessed | tf_op | source)
XLA Modules:
  0.0 96.6 jit_solution(10974734703022036528)
XLA Ops:
  0.6 2.0 %pick.1 = bf16[128,474]{1,0:T(8,128)(2,1)} custom-call(s32[8,16]{1,0:T(8,128)} %bitcast.21, bf16[474,512]{1,0:T(8,128)(2,1)} %bitcast.13), custom_call_target="tpu_custom_call" | custom-call | flops 1 | bytes 1 | tf_op jit(solution)/shard_map/pick/pallas_call | solution.py:129
  2.7 7.4 %all-to-all-start = ((bf16[16,8,474]{2,1,0:T(8,128)(2,1)}), bf16[16,8,474]{2,1,0:T(8,128)(2,1)S(1)}, u32[]{:S(2)}, u32[]{:S(2)}) async-start(bf16[16,8,474]{2,1,0:T(8,128)(2,1)} %bitcast.16), calls=%async_computation | async-start | bytes 262144 | tf_op jit(solution)/shard_map/all_to_all | solution.py:438
  10.1 3.2 %embed.1 = (bf16[512,512]{1,0:T(8,128)(2,1)}, bf16[512,512]{1,0:T(8,128)(2,1)}, bf16[512,512]{1,0:T(8,128)(2,1)S(1)}, f32[64,512]{1,0:T(8,128)S(1)}, bf16[474,51...) custom-call(bf16[474,512]{1,0:T(8,128)(2,1)} %bitcast.14, ...), custom_call_target="tpu_custom_call" | custom-call | flops 1 | bytes 1 | tf_op jit(solution)/shard_map/embed/pallas_call | solution.py:129
  13.3 4.7 %all-to-all-done = bf16[16,8,474]{2,1,0:T(8,128)(2,1)S(1)} async-done(((bf16[16,8,474]{2,1,0:T(8,128)(2,1)}), bf16[16,8,474]{2,1,0:T(8,128)(2,1)S(1)}, u32[]{:S(2)}, u32[]{:S(2)}) %all-to-all-start) | async-done | bytes 121376 | tf_op jit(solution)/shard_map/all_to_all | solution.py:438
  18.0 3.0 %encode.1 = (bf16[64,512]{1,0:T(8,128)(2,1)S(1)}, bf16[64,512]{1,0:T(8,128)(2,1)S(1)}, bf16[64,512]{1,0:T(8,128)(2,1)S(1)}, bf16[64,512]{1,0:T(8,128)(2,1)S(1)},...) custom-call(s32[16,64]{1,0:T(8,128)S(1)} %get-tuple-element.83.refs_, ...), custom_call_target="tpu_custom_call" | custom-call | flops 1 | bytes 1 | tf_op jit(solution)/shard_map/encode/pallas_call | solution.py:129
  21.1 4.4 %collective-permute-start.1 = (bf16[64,512]{1,0:T(8,128)(2,1)S(1)}, bf16[64,512]{1,0:T(8,128)(2,1)S(1)}, u32[]{:S(2)}, u32[]{:S(2)}) collective-permute-start(bf16[64,512]{1,0:T(8,128)(2,1)S(1)} %get-tuple-element.106), channel_id=1, source_target_pairs={{1,0},{2,1},{3,2},{4,3},{5,4},{6,5},{7,6},{8,7},{9,8},{10,9},{11,1... | collective-permute-start | bytes 196616 | tf_op jit(solution)/shard_map/ppermute | solution.py:415
  25.5 1.7 %load.1 = (bf16[474,512]{1,0:T(8,128)(2,1)S(1)}, bf16[512,512]{1,0:T(8,128)(2,1)S(1)}, bf16[512,512]{1,0:T(8,128)(2,1)S(1)}, bf16[512,512]{1,0:T(8,128)(2,1)S(1)...) custom-call(bf16[474,512]{1,0:T(8,128)(2,1)} %bitcast.15, ...), custom_call_target="tpu_custom_call" | custom-call | flops 1 | bytes 1 | tf_op jit(solution)/shard_map/load/pallas_call | solution.py:129
  27.5 3.0 %process.1 = (bf16[64,512]{1,0:T(8,128)(2,1)}, bf16[64,512]{1,0:T(8,128)(2,1)S(1)}, bf16[64,512]{1,0:T(8,128)(2,1)S(1)}, f32[64,512]{1,0:T(8,128)S(1)}, f32[64,5...) custom-call(s32[16,64]{1,0:T(8,128)S(1)} %get-tuple-element.102.refs_0_,, ...), custom_call_target="tpu_custom_call" | custom-call | flops 1 | bytes 1 | tf_op jit(solution)/shard_map/process/pallas_call | solution.py:129
  31.6 4.2 %collective-permute-start.4 = (bf16[64,512]{1,0:T(8,128)(2,1)S(1)}, bf16[64,512]{1,0:T(8,128)(2,1)S(1)}, u32[]{:S(2)}, u32[]{:S(2)}) collective-permute-start(bf16[64,512]{1,0:T(8,128)(2,1)S(1)} %get-tuple-element.119), channel_id=1, source_target_pairs={{1,0},{2,1},{3,2},{4,3},{5,4},{6,5},{7,6},{8,7},{9,8},{10,9},{11,1... | collective-permute-start | bytes 196616 | tf_op jit(solution)/shard_map/ppermute | solution.py:415
  36.1 1.6 %collective-permute-done.3.refs_2_ = bf16[64,512]{1,0:T(8,128)(2,1)S(1)} collective-permute-done((bf16[64,512]{1,0:T(8,128)(2,1)S(1)}, bf16[64,512]{1,0:T(8,128)(2,1)S(1)}, u32[]{:S(2)}, u32[]{:S(2)}) %collective-permute-start.3) | collective-permute-done | bytes 65568 | tf_op jit(solution)/shard_map/ppermute | solution.py:415
  37.8 2.3 %mesh_grads.1 = (f32[768,512]{1,0:T(8,128)S(1)}, bf16[768,512]{1,0:T(8,128)(2,1)S(1)}, bf16[640,512]{1,0:T(8,128)(2,1)S(1)}) custom-call(f32[256,512]{1,0:T(8,128)S(1)} %get-tuple-element.117.refs_0_.refs_1_, s32[16,64]{1,0:T(8,128)S(1)} %get-tuple-element.83.refs_0_.refs_1_, bf16[64,512]{1,0:T(8,128)(2,1)S(1)} %collective-permute-done.3.refs_2_, ...), custom_call_target="tpu_custom_call" | custom-call | flops 10000000000 | bytes 1 | tf_op jit(solution)/shard_map/mesh_grads/pallas_call | solution.py:129
  40.2 1.7 %grid_grads.1 = (f32[512,512]{1,0:T(8,128)S(1)}, bf16[512,512]{1,0:T(8,128)(2,1)S(1)}) custom-call(f32[768,512]{1,0:T(8,128)S(1)} %get-tuple-element.126.refs_0_.refs_1_, bf16[640,512]{1,0:T(8,128)(2,1)S(1)} %get-tuple-element.127.refs_1_, bf16[512,512]{1,0:T(8,128)(2,1)S(1)} %get-tuple-element.86.refs_4_.refs_2_, ...), custom_call_target="tpu_custom_call" | custom-call | flops 10000000000 | bytes 1 | tf_op jit(solution)/shard_map/grid_grads/pallas_call | solution.py:129
  45.4 3.8 %collective-permute-done.8.refs_2_ = bf16[128,512]{1,0:T(8,128)(2,1)S(1)} collective-permute-done((bf16[128,512]{1,0:T(8,128)(2,1)S(1)}, bf16[128,512]{1,0:T(8,128)(2,1)S(1)}, u32[]{:S(2)}, u32[]{:S(2)}) %collective-permute-start.8) | collective-permute-done | bytes 131104 | tf_op jit(solution)/shard_map/ppermute | solution.py:381
  50.4 3.6 %collective-permute-done.9.refs_2_ = bf16[384,512]{1,0:T(8,128)(2,1)S(1)} collective-permute-done((bf16[384,512]{1,0:T(8,128)(2,1)S(1)}, bf16[384,512]{1,0:T(8,128)(2,1)S(1)}, u32[]{:S(2)}, u32[]{:S(2)}) %collective-permute-start.9) | collective-permute-done | bytes 393248 | tf_op jit(solution)/shard_map/ppermute | solution.py:381
  54.1 1.7 %collective-permute-start.11 = (bf16[192,512]{1,0:T(8,128)(2,1)S(1)}, bf16[192,512]{1,0:T(8,128)(2,1)S(1)}, u32[]{:S(2)}, u32[]{:S(2)}) collective-permute-start(bf16[192,512]{1,0:T(8,128)(2,1)S(1)} %get-tuple-element.145), channel_id=1, source_target_pairs={{0,4},{1,5},{2,6},{3,7},{4,0},{5,1},{6,2},{7,3},{8,12},{9,13},{10,... | collective-permute-start | bytes 589832 | tf_op jit(solution)/shard_map/ppermute | solution.py:381
  57.8 3.1 %collective-permute-done.11.refs_2_ = bf16[192,512]{1,0:T(8,128)(2,1)S(1)} collective-permute-done((bf16[192,512]{1,0:T(8,128)(2,1)S(1)}, bf16[192,512]{1,0:T(8,128)(2,1)S(1)}, u32[]{:S(2)}, u32[]{:S(2)}) %collective-permute-start.11) | collective-permute-done | bytes 196640 | tf_op jit(solution)/shard_map/ppermute | solution.py:381
  61.0 3.5 %collective-permute-start.15 = (bf16[192,512]{1,0:T(8,128)(2,1)S(1)}, bf16[192,512]{1,0:T(8,128)(2,1)S(1)}, u32[]{:S(2)}, u32[]{:S(2)}) collective-permute-start(bf16[192,512]{1,0:T(8,128)(2,1)S(1)} %mesh_add.6.refs_0_.refs_1_), channel_id=1, source_target_pairs={{0,8},{1,9},{2,10},{3,11},{4,12},{5,13},{6,14},{7,15},{8,0},{9,1},... | collective-permute-start | bytes 589832 | tf_op jit(solution)/shard_map/ppermute | solution.py:381
  65.5 6.3 %collective-permute-done.14.refs_2_ = bf16[128,512]{1,0:T(8,128)(2,1)S(1)} collective-permute-done((bf16[128,512]{1,0:T(8,128)(2,1)S(1)}, bf16[128,512]{1,0:T(8,128)(2,1)S(1)}, u32[]{:S(2)}, u32[]{:S(2)}) %collective-permute-start.14) | collective-permute-done | bytes 131104 | tf_op jit(solution)/shard_map/ppermute | solution.py:381
  73.3 2.6 %collective-permute-done.15.refs_2_ = bf16[192,512]{1,0:T(8,128)(2,1)S(1)} collective-permute-done((bf16[192,512]{1,0:T(8,128)(2,1)S(1)}, bf16[192,512]{1,0:T(8,128)(2,1)S(1)}, u32[]{:S(2)}, u32[]{:S(2)}) %collective-permute-start.15) | collective-permute-done | bytes 196640 | tf_op jit(solution)/shard_map/ppermute | solution.py:381
  76.4 1.8 %collective-permute-done.16.refs_2_ = bf16[128,512]{1,0:T(8,128)(2,1)S(1)} collective-permute-done((bf16[128,512]{1,0:T(8,128)(2,1)S(1)}, bf16[128,512]{1,0:T(8,128)(2,1)S(1)}, u32[]{:S(2)}, u32[]{:S(2)}) %collective-permute-start.16) | collective-permute-done | bytes 131104 | tf_op jit(solution)/shard_map/ppermute | solution.py:381
  79.6 2.7 %collective-permute-done.18.refs_2_ = bf16[192,512]{1,0:T(8,128)(2,1)S(1)} collective-permute-done((bf16[192,512]{1,0:T(8,128)(2,1)S(1)}, bf16[192,512]{1,0:T(8,128)(2,1)S(1)}, u32[]{:S(2)}, u32[]{:S(2)}) %collective-permute-start.18) | collective-permute-done | bytes 196640 | tf_op jit(solution)/shard_map/ppermute | solution.py:381
  85.4 4.9 %collective-permute-done.21.refs_2_ = bf16[256,512]{1,0:T(8,128)(2,1)S(1)} collective-permute-done((bf16[256,512]{1,0:T(8,128)(2,1)S(1)}, bf16[256,512]{1,0:T(8,128)(2,1)S(1)}, u32[]{:S(2)}, u32[]{:S(2)}) %collective-permute-start.21) | collective-permute-done | bytes 262176 | tf_op jit(solution)/shard_map/ppermute | solution.py:381
  90.5 1.7 %collective-permute-done.22.refs_2_ = bf16[384,512]{1,0:T(8,128)(2,1)S(1)} collective-permute-done((bf16[384,512]{1,0:T(8,128)(2,1)S(1)}, bf16[384,512]{1,0:T(8,128)(2,1)S(1)}, u32[]{:S(2)}, u32[]{:S(2)}) %collective-permute-start.22) | collective-permute-done | bytes 393248 | tf_op jit(solution)/shard_map/ppermute | solution.py:381
  94.6 1.9 %mesh_collect.1 = (f32[512,512]{1,0:T(8,128)}, f32[512,512]{1,0:T(8,128)}, f32[512,512]{1,0:T(8,128)}) custom-call(f32[512,512]{1,0:T(8,128)} %get-tuple-element.75.refs_0_, bf16[768,512]{1,0:T(8,128)(2,1)S(1)} %mesh_join.3.refs_0_.refs_1_, bf16[768,512]{1,0:T(8,128)(2,1)S(1)} %collective-permute-done.24.refs_2_), custom_call_target="tpu_custom_call" | custom-call | flops 10000000000 | bytes 1 | tf_op jit(solution)/shard_map/mesh_collect/pallas_call | solution.py:129
  (57 shorter events, 18.4 us)
Async XLA Ops:
  2.7 15.3 %all-to-all-start = ((bf16[16,8,474]{2,1,0:T(8,128)(2,1)}), bf16[16,8,474]{2,1,0:T(8,128)(2,1)S(1)}, u32[]{:S(2)}, u32[]{:S(2)}) async-start(bf16[16,8,474]{2,1,0:T(8,128)(2,1)} %bitcast.16), calls=%async_computation | async-start | bytes 262144 | tf_op jit(solution)/shard_map/all_to_all | solution.py:438
  21.0 6.4 %collective-permute-start = (bf16[64,512]{1,0:T(8,128)(2,1)S(1)}, bf16[64,512]{1,0:T(8,128)(2,1)S(1)}, u32[]{:S(2)}, u32[]{:S(2)}) collective-permute-start(bf16[64,512]{1,0:T(8,128)(2,1)S(1)} %get-tuple-element.105), channel_id=1, source_target_pairs={{15,0},{0,1},{1,2},{2,3},{3,4},{4,5},{5,6},{6,7},{7,8},{8,9},{9,10... | collective-permute-start | bytes 196616 | tf_op jit(solution)/shard_map/ppermute | solution.py:415
  21.1 6.4 %collective-permute-start.1 = (bf16[64,512]{1,0:T(8,128)(2,1)S(1)}, bf16[64,512]{1,0:T(8,128)(2,1)S(1)}, u32[]{:S(2)}, u32[]{:S(2)}) collective-permute-start(bf16[64,512]{1,0:T(8,128)(2,1)S(1)} %get-tuple-element.106), channel_id=1, source_target_pairs={{1,0},{2,1},{3,2},{4,3},{5,4},{6,5},{7,6},{8,7},{9,8},{10,9},{11,1... | collective-permute-start | bytes 196616 | tf_op jit(solution)/shard_map/ppermute | solution.py:415
  31.1 4.8 %collective-permute-start.2 = (bf16[512,512]{1,0:T(8,128)(2,1)S(1)}, bf16[512,512]{1,0:T(8,128)(2,1)S(1)}, u32[]{:S(2)}, u32[]{:S(2)}) collective-permute-start(bf16[512,512]{1,0:T(8,128)(2,1)S(1)} %get-tuple-element.116), channel_id=1, source_target_pairs={{0,1},{1,0},{2,3},{3,2},{4,5},{5,4},{6,7},{7,6},{8,9},{9,8},{10,11... | collective-permute-start | bytes 1572872 | tf_op jit(solution)/shard_map/ppermute | solution.py:381
  31.1 6.6 %collective-permute-start.3 = (bf16[64,512]{1,0:T(8,128)(2,1)S(1)}, bf16[64,512]{1,0:T(8,128)(2,1)S(1)}, u32[]{:S(2)}, u32[]{:S(2)}) collective-permute-start(bf16[64,512]{1,0:T(8,128)(2,1)S(1)} %get-tuple-element.118), channel_id=1, source_target_pairs={{15,0},{0,1},{1,2},{2,3},{3,4},{4,5},{5,6},{6,7},{7,8},{8,9},{9,10... | collective-permute-start | bytes 196616 | tf_op jit(solution)/shard_map/ppermute | solution.py:415
  31.6 6.2 %collective-permute-start.4 = (bf16[64,512]{1,0:T(8,128)(2,1)S(1)}, bf16[64,512]{1,0:T(8,128)(2,1)S(1)}, u32[]{:S(2)}, u32[]{:S(2)}) collective-permute-start(bf16[64,512]{1,0:T(8,128)(2,1)S(1)} %get-tuple-element.119), channel_id=1, source_target_pairs={{1,0},{2,1},{3,2},{4,3},{5,4},{6,5},{7,6},{8,7},{9,8},{10,9},{11,1... | collective-permute-start | bytes 196616 | tf_op jit(solution)/shard_map/ppermute | solution.py:415
  36.0 6.6 %collective-permute-start.6 = (bf16[256,512]{1,0:T(8,128)(2,1)S(1)}, bf16[256,512]{1,0:T(8,128)(2,1)S(1)}, u32[]{:S(2)}, u32[]{:S(2)}) collective-permute-start(bf16[256,512]{1,0:T(8,128)(2,1)S(1)} %get-tuple-element.136), channel_id=1, source_target_pairs={{0,2},{1,3},{2,0},{3,1},{4,6},{5,7},{6,4},{7,5},{8,10},{9,11},{10,... | collective-permute-start | bytes 786440 | tf_op jit(solution)/shard_map/ppermute | solution.py:381
  40.1 2.4 %collective-permute-start.5 = (bf16[768,512]{1,0:T(8,128)(2,1)S(1)}, bf16[768,512]{1,0:T(8,128)(2,1)S(1)}, u32[]{:S(2)}, u32[]{:S(2)}) collective-permute-start(bf16[768,512]{1,0:T(8,128)(2,1)S(1)} %get-tuple-element.134), channel_id=1, source_target_pairs={{0,1},{1,0},{2,3},{3,2},{4,5},{5,4},{6,7},{7,6},{8,9},{9,8},{10,11... | collective-permute-start | bytes 2359304 | tf_op jit(solution)/shard_map/ppermute | solution.py:381
  42.7 6.4 %collective-permute-start.8 = (bf16[128,512]{1,0:T(8,128)(2,1)S(1)}, bf16[128,512]{1,0:T(8,128)(2,1)S(1)}, u32[]{:S(2)}, u32[]{:S(2)}) collective-permute-start(bf16[128,512]{1,0:T(8,128)(2,1)S(1)} %get-tuple-element.140), channel_id=1, source_target_pairs={{0,4},{1,5},{2,6},{3,7},{4,0},{5,1},{6,2},{7,3},{8,12},{9,13},{10,... | collective-permute-start | bytes 393224 | tf_op jit(solution)/shard_map/ppermute | solution.py:381
  42.8 11.2 %collective-permute-start.9 = (bf16[384,512]{1,0:T(8,128)(2,1)S(1)}, bf16[384,512]{1,0:T(8,128)(2,1)S(1)}, u32[]{:S(2)}, u32[]{:S(2)}) collective-permute-start(bf16[384,512]{1,0:T(8,128)(2,1)S(1)} %get-tuple-element.141), channel_id=1, source_target_pairs={{0,2},{1,3},{2,0},{3,1},{4,6},{5,7},{6,4},{7,5},{8,10},{9,11},{10,... | collective-permute-start | bytes 1179656 | tf_op jit(solution)/shard_map/ppermute | solution.py:381
  44.1 13.2 %collective-permute-start.10 = (bf16[256,512]{1,0:T(8,128)(2,1)S(1)}, bf16[256,512]{1,0:T(8,128)(2,1)S(1)}, u32[]{:S(2)}, u32[]{:S(2)}) collective-permute-start(bf16[256,512]{1,0:T(8,128)(2,1)S(1)} %get-tuple-element.143), channel_id=1, source_target_pairs={{0,4},{1,5},{2,6},{3,7},{4,0},{5,1},{6,2},{7,3},{8,12},{9,13},{10,... | collective-permute-start | bytes 786440 | tf_op jit(solution)/shard_map/ppermute | solution.py:381
  49.2 15.4 %collective-permute-start.12 = (bf16[128,512]{1,0:T(8,128)(2,1)S(1)}, bf16[128,512]{1,0:T(8,128)(2,1)S(1)}, u32[]{:S(2)}, u32[]{:S(2)}) collective-permute-start(bf16[128,512]{1,0:T(8,128)(2,1)S(1)} %process_add.6.refs_0_.refs_1_), channel_id=1, source_target_pairs={{0,8},{1,9},{2,10},{3,11},{4,12},{5,13},{6,14},{7,15},{8,0},{9,1},... | collective-permute-start | bytes 393224 | tf_op jit(solution)/shard_map/ppermute | solution.py:381
  54.1 6.8 %collective-permute-start.11 = (bf16[192,512]{1,0:T(8,128)(2,1)S(1)}, bf16[192,512]{1,0:T(8,128)(2,1)S(1)}, u32[]{:S(2)}, u32[]{:S(2)}) collective-permute-start(bf16[192,512]{1,0:T(8,128)(2,1)S(1)} %get-tuple-element.145), channel_id=1, source_target_pairs={{0,4},{1,5},{2,6},{3,7},{4,0},{5,1},{6,2},{7,3},{8,12},{9,13},{10,... | collective-permute-start | bytes 589832 | tf_op jit(solution)/shard_map/ppermute | solution.py:381
  57.4 7.9 %collective-permute-start.13 = (bf16[128,512]{1,0:T(8,128)(2,1)S(1)}, bf16[128,512]{1,0:T(8,128)(2,1)S(1)}, u32[]{:S(2)}, u32[]{:S(2)}) collective-permute-start(bf16[128,512]{1,0:T(8,128)(2,1)S(1)} %get-tuple-element.146), channel_id=1, source_target_pairs={{0,2},{1,3},{2,0},{3,1},{4,6},{5,7},{6,4},{7,5},{8,10},{9,11},{10,... | collective-permute-start | bytes 393224 | tf_op jit(solution)/shard_map/ppermute | solution.py:381
  61.0 14.8 %collective-permute-start.15 = (bf16[192,512]{1,0:T(8,128)(2,1)S(1)}, bf16[192,512]{1,0:T(8,128)(2,1)S(1)}, u32[]{:S(2)}, u32[]{:S(2)}) collective-permute-start(bf16[192,512]{1,0:T(8,128)(2,1)S(1)} %mesh_add.6.refs_0_.refs_1_), channel_id=1, source_target_pairs={{0,8},{1,9},{2,10},{3,11},{4,12},{5,13},{6,14},{7,15},{8,0},{9,1},... | collective-permute-start | bytes 589832 | tf_op jit(solution)/shard_map/ppermute | solution.py:381
  64.7 7.2 %collective-permute-start.14 = (bf16[128,512]{1,0:T(8,128)(2,1)S(1)}, bf16[128,512]{1,0:T(8,128)(2,1)S(1)}, u32[]{:S(2)}, u32[]{:S(2)}) collective-permute-start(bf16[128,512]{1,0:T(8,128)(2,1)S(1)} %process_add.7.refs_0_.refs_1_), channel_id=1, source_target_pairs={{0,4},{1,5},{2,6},{3,7},{4,0},{5,1},{6,2},{7,3},{8,12},{9,13},{10,... | collective-permute-start | bytes 393224 | tf_op jit(solution)/shard_map/ppermute | solution.py:381
  65.4 12.8 %collective-permute-start.16 = (bf16[128,512]{1,0:T(8,128)(2,1)S(1)}, bf16[128,512]{1,0:T(8,128)(2,1)S(1)}, u32[]{:S(2)}, u32[]{:S(2)}) collective-permute-start(bf16[128,512]{1,0:T(8,128)(2,1)S(1)} %grid_add.6.refs_0_.refs_1_), channel_id=1, source_target_pairs={{0,8},{1,9},{2,10},{3,11},{4,12},{5,13},{6,14},{7,15},{8,0},{9,1},... | collective-permute-start | bytes 393224 | tf_op jit(solution)/shard_map/ppermute | solution.py:381
  71.9 7.6 %collective-permute-start.17 = (bf16[256,512]{1,0:T(8,128)(2,1)S(1)}, bf16[256,512]{1,0:T(8,128)(2,1)S(1)}, u32[]{:S(2)}, u32[]{:S(2)}) collective-permute-start(bf16[256,512]{1,0:T(8,128)(2,1)S(1)} %process_join.2.refs_0_.refs_1_), channel_id=1, source_target_pairs={{0,2},{1,3},{2,0},{3,1},{4,6},{5,7},{6,4},{7,5},{8,10},{9,11},{10,... | collective-permute-start | bytes 786440 | tf_op jit(solution)/shard_map/ppermute | solution.py:381
  75.9 6.5 %collective-permute-start.18 = (bf16[192,512]{1,0:T(8,128)(2,1)S(1)}, bf16[192,512]{1,0:T(8,128)(2,1)S(1)}, u32[]{:S(2)}, u32[]{:S(2)}) collective-permute-start(bf16[192,512]{1,0:T(8,128)(2,1)S(1)} %mesh_add.7.refs_0_.refs_1_), channel_id=1, source_target_pairs={{0,4},{1,5},{2,6},{3,7},{4,0},{5,1},{6,2},{7,3},{8,12},{9,13},{10,... | collective-permute-start | bytes 589832 | tf_op jit(solution)/shard_map/ppermute | solution.py:381
  78.3 5.6 %collective-permute-start.19 = (bf16[128,512]{1,0:T(8,128)(2,1)S(1)}, bf16[128,512]{1,0:T(8,128)(2,1)S(1)}, u32[]{:S(2)}, u32[]{:S(2)}) collective-permute-start(bf16[128,512]{1,0:T(8,128)(2,1)S(1)} %grid_add.7.refs_0_.refs_1_), channel_id=1, source_target_pairs={{0,2},{1,3},{2,0},{3,1},{4,6},{5,7},{6,4},{7,5},{8,10},{9,11},{10,... | collective-permute-start | bytes 393224 | tf_op jit(solution)/shard_map/ppermute | solution.py:381
  79.5 4.4 %collective-permute-start.20 = (bf16[512,512]{1,0:T(8,128)(2,1)S(1)}, bf16[512,512]{1,0:T(8,128)(2,1)S(1)}, u32[]{:S(2)}, u32[]{:S(2)}) collective-permute-start(bf16[512,512]{1,0:T(8,128)(2,1)S(1)} %process_join.3.refs_0_.refs_1_), channel_id=1, source_target_pairs={{0,1},{1,0},{2,3},{3,2},{4,5},{5,4},{6,7},{7,6},{8,9},{9,8},{10,11... | collective-permute-start | bytes 1572872 | tf_op jit(solution)/shard_map/ppermute | solution.py:381
  82.4 9.8 %collective-permute-start.22 = (bf16[384,512]{1,0:T(8,128)(2,1)S(1)}, bf16[384,512]{1,0:T(8,128)(2,1)S(1)}, u32[]{:S(2)}, u32[]{:S(2)}) collective-permute-start(bf16[384,512]{1,0:T(8,128)(2,1)S(1)} %mesh_join.2.refs_0_.refs_1_), channel_id=1, source_target_pairs={{0,2},{1,3},{2,0},{3,1},{4,6},{5,7},{6,4},{7,5},{8,10},{9,11},{10,... | collective-permute-start | bytes 1179656 | tf_op jit(solution)/shard_map/ppermute | solution.py:381
  83.9 6.5 %collective-permute-start.21 = (bf16[256,512]{1,0:T(8,128)(2,1)S(1)}, bf16[256,512]{1,0:T(8,128)(2,1)S(1)}, u32[]{:S(2)}, u32[]{:S(2)}) collective-permute-start(bf16[256,512]{1,0:T(8,128)(2,1)S(1)} %grid_join.2.refs_0_.refs_1_), channel_id=1, source_target_pairs={{0,4},{1,5},{2,6},{3,7},{4,0},{5,1},{6,2},{7,3},{8,12},{9,13},{10,... | collective-permute-start | bytes 786440 | tf_op jit(solution)/shard_map/ppermute | solution.py:381
  92.3 2.4 %collective-permute-start.24 = (bf16[768,512]{1,0:T(8,128)(2,1)S(1)}, bf16[768,512]{1,0:T(8,128)(2,1)S(1)}, u32[]{:S(2)}, u32[]{:S(2)}) collective-permute-start(bf16[768,512]{1,0:T(8,128)(2,1)S(1)} %mesh_join.3.refs_0_.refs_1_), channel_id=1, source_target_pairs={{0,1},{1,0},{2,3},{3,2},{4,5},{5,4},{6,7},{7,6},{8,9},{9,8},{10,11... | collective-permute-start | bytes 2359304 | tf_op jit(solution)/shard_map/ppermute | solution.py:381
  (2 other events, 4.1 us)

commit v5 on v4

--- a/solution.py
+++ b/solution.py
@@ -112,7 +112,7 @@
                 inputs.append(Input(sources[i]))
         for i, is_far in enumerate(far_out):
             outputs.append(Output(targets[i], rest.pop(0), out_sems.at[i]) if is_far else Output(targets[i]))
-        where = (lax.axis_index("space").astype(jnp.int32) & (BLOCKS - 1),) if place else ()
+        where = (lax.axis_index("space").astype(jnp.int32),) if place else ()
         body(*where, inputs, outputs, rest)
         for value in inputs:
             value()
@@ -200,18 +200,18 @@
     return total.astype(BF)
 
 
-def encode_body(ins, outs, scratch):
+def encode_body(me, ins, outs, scratch):
     slots_t, mask_t, x, we, ws, proj, recv, wout, latent, wnext, halo = ins
-    mid, to_left, to_right, mesh_proj, agg, y, r, slope, lat_far, slope_far = outs
+    mid, one, two, mesh_proj, agg, y, r, slope, lat_far, slope_far = outs
     table, onehot, rows = scratch
     near = proj.held.shape[0]
     fill_onehot(onehot, slots_t()[...].T)
     mask = mask_t()[...].T
     x()
     pre = dot(x()[...], we()[...])
-    one, two, far = embed_rows(pre, ws()[...])
-    lat_far.set(one)
-    slope_far.set(two)
+    lat, bend, far = embed_rows(pre, ws()[...])
+    lat_far.set(lat)
+    slope_far.set(bend)
     table[near:, :] = far
     table[:near, :] = proj()[...]
     rows[...] = dot(onehot[...], table[...])
@@ -227,23 +227,27 @@
     mesh_proj.set(sent)
     lists = halo()[...]
     subs = lax.broadcasted_iota(jnp.int32, (sent.shape[0], lists.shape[1]), 0)
-    to_left.set(t_dot(jnp.where(lists[0:1, :] == subs, 1.0, 0.0).astype(BF), sent))
-    to_right.set(t_dot(jnp.where(lists[1:2, :] == subs, 1.0, 0.0).astype(BF), sent))
-
-
-def process_body(ins, outs, scratch):
-    slots_t, mask_t, mesh_proj, left, right, mid, wrecv, wout, cotangent = ins
-    out, to_left, to_right, grad_rows, grad_mid, agg, grad_u, grad_recv = outs
+    odd = 1 - me % 2
+    for out, towards in ((one, 1 - odd), (two, odd)):
+        rows = jnp.where(towards == 0, lists[0:1, :], lists[1:2, :])
+        out.set(t_dot(jnp.where(rows == subs, 1.0, 0.0).astype(BF), sent))
+
+
+def process_body(me, ins, outs, scratch):
+    slots_t, mask_t, mesh_proj, one, two, mid, wrecv, wout, cotangent = ins
+    out, back_one, back_two, grad_rows, grad_mid, agg, grad_u, grad_recv = outs
     table, onehot, onehot_t, rows, slope, grad_msg = scratch
     m = mesh_proj.held.shape[0]
-    depth = left.held.shape[0]
+    depth = one.held.shape[0]
+    odd = me % 2 == 0
     slots = slots_t()[...]
     fill_onehot(onehot, slots.T)
     mask = mask_t()[...].T
     fill_onehot_t(onehot_t, slots)
     table[:m, :] = mesh_proj()[...]
-    table[m : m + depth, :] = left()[...]
-    table[m + depth : m + 2 * depth, :] = right()[...]
+    from_one, from_two = one()[...], two()[...]
+    table[m : m + depth, :] = jnp.where(odd, from_one, from_two)
+    table[m + depth : m + 2 * depth, :] = jnp.where(odd, from_two, from_one)
     rows[...] = dot(onehot[...], table[...])
     middle = mid()[...]
     summed = messages(rows, dot(middle, wrecv()[...]), mask, slope)
@@ -256,8 +260,9 @@
     gr = message_grads(grad_msg, slope, dot_t(gu, wout()[...]), mask.shape[1])
     grad_recv.set(gr)
     grads = dot(onehot_t[...], grad_msg[...])
-    to_left.set(grads[m : m + depth, :])
-    to_right.set(grads[m + depth :, :])
+    to_left, to_right = grads[m : m + depth, :], grads[m + depth :, :]
+    back_one.set(jnp.where(odd, to_left, to_right))
+    back_two.set(jnp.where(odd, to_right, to_left))
     grad_rows.set(grads[:m, :])
     grad_mid.set(ct + dot_t(gr, wrecv()[...]))
 
@@ -278,7 +283,7 @@
     for i, step in enumerate(order):
         if place >> (len(order) - 1 - i) & 1:
             flips ^= step
-    return me ^ flips
+    return (me & (BLOCKS - 1)) ^ flips
 
 
 def spread(me, order, grads, keep, send):
@@ -304,21 +309,20 @@
 
 
 def mesh_grads_body(order, me, ins, outs, scratch):
-    slots_t, back_left, back_right, halo, grad_rows, wnext, grad_mid, y, r, wout, slope, mid, agg, latent = ins
-    keep, send, grad_table = outs
-    onehot_t, grad_msg, g_next, g_out, g_recv = scratch
+    back_one, back_two, halo, grad_rows, wnext, grad_mid, y, r, wout, slope, mid, agg, latent = ins
+    keep, send, grad_msg = outs
+    g_next, g_out, g_recv = scratch
     m = mid.held.shape[0]
-    fill_onehot_t(onehot_t, slots_t()[...])
     lists = halo()[...]
     subs = lax.broadcasted_iota(jnp.int32, (m, lists.shape[1]), 0)
-    to_left = jnp.where(lists[0:1, :] == subs, 1.0, 0.0).astype(BF)
-    to_right = jnp.where(lists[1:2, :] == subs, 1.0, 0.0).astype(BF)
-    gp = (grad_rows()[...] + dot(to_right, back_right()[...]) + dot(to_left, back_left()[...])).astype(BF)
+    odd = me % 2 == 0
+    put_one = jnp.where(jnp.where(odd, lists[0:1, :], lists[1:2, :]) == subs, 1.0, 0.0).astype(BF)
+    put_two = jnp.where(jnp.where(odd, lists[1:2, :], lists[0:1, :]) == subs, 1.0, 0.0).astype(BF)
+    gp = (grad_rows()[...] + dot(put_one, back_one()[...]) + dot(put_two, back_two()[...])).astype(BF)
     gmid = grad_mid()[...] + dot_t(gp, wnext()[...])
     gu = normalized_grad(y()[...], r()[:, 0:1], gmid).astype(BF)
     gagg = dot_t(gu, wout()[...])
-    gr = message_grads(grad_msg, slope(), gagg, grad_msg.shape[0] // m)
-    grad_table.set(dot(onehot_t[...], grad_msg[...]))
+    gr = message_grads(grad_msg.held, slope(), gagg, grad_msg.held.shape[0] // m)
     g_next[...] = t_dot(mid()[...], gp)
     g_out[...] = t_dot(agg()[...], gu)
     g_recv[...] = t_dot(latent()[...], gr)
@@ -326,10 +330,12 @@
 
 
 def grid_grads_body(order, me, ins, outs, scratch):
-    grad_table, ws, slope_near, slope_far, x_t, x_far, lat, lat_far = ins
-    g_send, g_embed = scratch
+    slots_t, grad_msg, ws, slope_near, slope_far, x_t, x_far, lat, lat_far = ins
+    onehot_t, g_send, g_embed = scratch
     near = lat.held.shape[0]
-    g_near, g_far = grad_table()[:near, :], grad_table()[near:, :]
+    fill_onehot_t(onehot_t, slots_t()[...])
+    grad_table = dot(onehot_t[...], grad_msg()[...]).astype(BF)
+    g_near, g_far = grad_table[:near, :], grad_table[near:, :]
     p_near = (dot_t(g_near, ws()[...]) * slope_near()[...].astype(F32)).astype(BF)
     p_far = (dot_t(g_far, ws()[...]) * slope_far()[...].astype(F32)).astype(BF)
     fin = x_t.held.shape[0]
@@ -410,9 +416,10 @@
         return self.value
 
 
-def passed_along(block, distance):
+def swapped(rows, first):
     n = lax.axis_size("space")
-    return lax.ppermute(block, "space", [((i - distance) % n, i) for i in range(n)])
+    pairs = [((first + i) % n, (first + i + 1) % n) for i in range(0, n, 2)]
+    return lax.ppermute(rows, "space", [*pairs, *((b, a) for a, b in pairs)])
 
 
 def local(
@@ -433,7 +440,7 @@
     halo = halo_list[0]
 
     (outgoing,) = call(
-        pick_body, "pick", [Far(sends_t), Far(x_t)], [((far, fin), BF, "far")], weight=FIRST[0]
+        pick_body, "pick", [Far(sends_t), Far(x_t)], [((far, fin), BF)], weight=FIRST[0]
     )
     incoming = lax.all_to_all(outgoing.reshape(n, -1, fin), "space", split_axis=0, concat_axis=0, tiled=True)
     x_far = incoming.reshape(far, fin)
@@ -449,17 +456,17 @@
         weight=FIRST[1],
     )
 
-    mid, to_left, to_right, mesh_proj, agg, y, r, slope, lat_far, slope_far = call(
+    mid, to_one, to_two, mesh_proj, agg, y, r, slope, lat_far, slope_far = call(
         encode_body,
         "encode",
         [enc_slot_t, enc_mask_t, x_far, w_embed, enc_send, proj, recv, enc_out, latent, proc_send, halo],
         [patch, edge_rows, edge_rows, patch, patch, patch_f32, ((m, 128), F32), ((edges_e, width), BF), far_rows,
          far_rows],
         [((near + far, width), BF), ((edges_e, near + far), BF), ((edges_e, width), F32)],
-    )
-
-    from_left = passed_along(to_right, 1)
-    from_right = passed_along(to_left, -1)
+        place=True,
+    )
+
+    from_one, from_two = swapped(to_one, 1), swapped(to_two, 0)
 
     after = (x_t, lat, slope_near, proc_recv, proc_out, cotangent, proc_slot_t, proc_mask_t, mid)
     x_t, lat, slope_near, proc_recv, proc_out, cotangent, proc_slot_t, proc_mask_t, mid = lax.optimization_barrier(after)
@@ -472,18 +479,18 @@
     )
 
     wide = m + 2 * depth
-    out, back_to_left, back_to_right, grad_rows, grad_mid, agg2, grad_u, grad_recv = call(
+    out, back_one, back_two, grad_rows, grad_mid, agg2, grad_u, grad_recv = call(
         process_body,
         "process",
-        [proc_slot_t, proc_mask_t, mesh_proj, from_left, from_right, mid, proc_recv, proc_out, cotangent],
+        [proc_slot_t, proc_mask_t, mesh_proj, from_one, from_two, mid, proc_recv, proc_out, cotangent],
         [(*patch, "far"), edge_rows, edge_rows, patch_f32, patch_f32, patch, patch, patch],
         [((wide, width), BF), ((edges_p, wide), BF), ((wide, edges_p), BF), ((edges_p, width), F32),
          ((edges_p, width), F32), ((edges_p, width), BF)],
+        place=True,
         weight=FIRST[4],
     )
 
-    back_right = passed_along(back_to_left, -1)
-    back_left = passed_along(back_to_right, 1)
+    back_one, back_two = swapped(back_one, 1), swapped(back_two, 0)
 
     def halves(count):
         rows = count * width // 2
@@ -493,19 +500,19 @@
 
     keep, send = call(
         functools.partial(process_grads_body, ORDER_P), "process_grads", [agg2, grad_u, mid, grad_recv], halves(2),
-        [square] * 2, True, weight=FIRST[5],
+        [square] * 2, True, None, FIRST[5],
     )
     sums = {"p": Sum("process", ORDER_P, rest, keep, send, [square] * 2)}
     token = keep
     for item, weight in PLAN:
         if item == "mesh":
-            keep, send, grad_table = call(
+            keep, send, grad_msg = call(
                 functools.partial(mesh_grads_body, ORDER_M),
                 "mesh_grads",
-                [enc_slot_t, back_left, back_right, halo, grad_rows, proc_send, grad_mid, y, r, enc_out, slope, mid,
+                [back_one, back_two, halo, grad_rows, proc_send, grad_mid, y, r, enc_out, slope, mid,
                  agg, latent],
-                halves(3) + [((near + far, width), BF)],
-                [((near + far, edges_e), BF), ((edges_e, width), BF)] + [square] * 3,
+                halves(3) + [((edges_e, width), BF)],
+                [square] * 3,
                 True,
                 token,
                 weight,
@@ -516,9 +523,9 @@
             keep, send = call(
                 functools.partial(grid_grads_body, ORDER_G),
                 "grid_grads",
-                [grad_table, enc_send, slope_near, slope_far, x_t, x_far, lat, lat_far],
+                [enc_slot_t, grad_msg, enc_send, slope_near, slope_far, x_t, x_far, lat, lat_far],
                 halves(2),
-                [square] * 2,
+                [((near + far, edges_e), BF)] + [square] * 2,
                 True,
                 token,
                 weight,

time: 96.9 us -> 94.2 us (0.972)
  starting transfers between devices: 31.5 us -> 18.8 us
  waiting for transfers between devices: 40.3 us -> 50.9 us
    ppermute x4, starting transfers between devices: 9.23 us -> 1.53 us  [swapped(): return lax.ppermute(rows, 'space', [*pairs, *((b, a) for a, b in pairs)])]
    ppermute x4, waiting for transfers between devices: 1.88 us -> 8.15 us  [swapped(): return lax.ppermute(rows, 'space', [*pairs, *((b, a) for a, b in pairs)])]
    ppermute x21, starting transfers between devices: 14.8 us -> 9.83 us  [exchange(): return lax.ppermute(value, 'space', [(i, i ^ step) for i in range(n)])]
    ppermute x21, waiting for transfers between devices: 33.7 us -> 38.1 us  [exchange(): return lax.ppermute(value, 'space', [(i, i ^ step) for i in range(n)])]
  transfers between devices with their start and end apart: 26 -> 26, of which waited for: 17 -> 16; matrix products, arithmetic and copies ran while one was open for 0% -> 0% of each run, Pallas kernels for 14% -> 14%
where the time goes in v5:
time: 94.2 us; the launch traced here: 93.9 us
  waiting for transfers between devices  50.9 us (54%)
  Pallas kernels  23.2 us (25%)
  starting transfers between devices  18.8 us (20%)
  between operations  0.98 us (1%)
    ppermute x21, waiting for transfers between devices, exchange(): return lax.ppermute(value, 'space', [(i, i ^ step) for i in range(n)])  38.1 us
    pallas_call x29, Pallas kernels, call(): pl.pallas_call(kernel, name=name, out_shape=[(pltpu.HBM if far else pltpu...  23.2 us
    ppermute x21, starting transfers between devices, exchange(): return lax.ppermute(value, 'space', [(i, i ^ step) for i in range(n)])  9.83 us
    ppermute x4, waiting for transfers between devices, swapped(): return lax.ppermute(rows, 'space', [*pairs, *((b, a) for a, b in pairs)])  8.15 us
    all_to_all x1, starting transfers between devices, local(): lax.all_to_all(outgoing.reshape(n, -1, fin), 'space', split_axis=0, conca...  7.4 us
    all_to_all x1, waiting for transfers between devices, local(): lax.all_to_all(outgoing.reshape(n, -1, fin), 'space', split_axis=0, conca...  4.74 us
  transfers between devices with their start and end apart: 26, of which 16 were waited for; matrix products, arithmetic and copies ran while one was open for 0% of the time, Pallas kernels for 14%

profile of v5, /device:TPU:0, one launch (start us, length us, event | category | flops | bytes accessed | tf_op | source)
XLA Modules:
  0.0 93.9 jit_solution(14782104629562078276)
XLA Ops:
  0.6 2.0 %pick.1 = bf16[128,474]{1,0:T(8,128)(2,1)} custom-call(s32[8,16]{1,0:T(8,128)} %bitcast.20, bf16[474,512]{1,0:T(8,128)(2,1)} %bitcast.13), custom_call_target="tpu_custom_call" | custom-call | flops 1 | bytes 1 | tf_op jit(solution)/shard_map/pick/pallas_call | solution.py:129
  2.7 7.4 %all-to-all-start = ((bf16[16,8,474]{2,1,0:T(8,128)(2,1)}), bf16[16,8,474]{2,1,0:T(8,128)(2,1)S(1)}, u32[]{:S(2)}, u32[]{:S(2)}) async-start(bf16[16,8,474]{2,1,0:T(8,128)(2,1)} %bitcast.8), calls=%async_computation | async-start | bytes 262144 | tf_op jit(solution)/shard_map/all_to_all | solution.py:445
  10.1 3.2 %embed.1 = (bf16[512,512]{1,0:T(8,128)(2,1)}, bf16[512,512]{1,0:T(8,128)(2,1)}, bf16[512,512]{1,0:T(8,128)(2,1)S(1)}, f32[64,512]{1,0:T(8,128)S(1)}, bf16[474,51...) custom-call(bf16[474,512]{1,0:T(8,128)(2,1)} %bitcast.14, ...), custom_call_target="tpu_custom_call" | custom-call | flops 1 | bytes 1 | tf_op jit(solution)/shard_map/embed/pallas_call | solution.py:129
  13.3 4.7 %all-to-all-done = bf16[16,8,474]{2,1,0:T(8,128)(2,1)S(1)} async-done(((bf16[16,8,474]{2,1,0:T(8,128)(2,1)}), bf16[16,8,474]{2,1,0:T(8,128)(2,1)S(1)}, u32[]{:S(2)}, u32[]{:S(2)}) %all-to-all-start) | async-done | bytes 121376 | tf_op jit(solution)/shard_map/all_to_all | solution.py:445
  18.0 3.0 %encode.1 = (bf16[64,512]{1,0:T(8,128)(2,1)S(1)}, bf16[64,512]{1,0:T(8,128)(2,1)S(1)}, bf16[64,512]{1,0:T(8,128)(2,1)S(1)}, bf16[64,512]{1,0:T(8,128)(2,1)S(1)},...) custom-call(s32[16,64]{1,0:T(8,128)S(1)} %get-tuple-element.83.refs_, ...), custom_call_target="tpu_custom_call" | custom-call | flops 1 | bytes 1 | tf_op jit(solution)/shard_map/encode/pallas_call | solution.py:129
  21.7 1.7 %load.1 = (bf16[474,512]{1,0:T(8,128)(2,1)S(1)}, bf16[512,512]{1,0:T(8,128)(2,1)S(1)}, bf16[512,512]{1,0:T(8,128)(2,1)S(1)}, bf16[512,512]{1,0:T(8,128)(2,1)S(1)...) custom-call(bf16[474,512]{1,0:T(8,128)(2,1)} %bitcast.15, ...), custom_call_target="tpu_custom_call" | custom-call | flops 1 | bytes 1 | tf_op jit(solution)/shard_map/load/pallas_call | solution.py:129
  23.5 3.9 %collective-permute-done.refs_3_ = bf16[64,512]{1,0:T(8,128)(2,1)S(1)} collective-permute-done((bf16[64,512]{1,0:T(8,128)(2,1)S(1)}, bf16[64,512]{1,0:T(8,128)(2,1)S(1)}, u32[]{:S(2)}, u32[]{:S(2)}) %collective-permute-start) | collective-permute-done | bytes 65568 | tf_op jit(solution)/shard_map/ppermute | solution.py:422
  27.4 2.5 %process.1 = (bf16[64,512]{1,0:T(8,128)(2,1)}, bf16[64,512]{1,0:T(8,128)(2,1)S(1)}, bf16[64,512]{1,0:T(8,128)(2,1)S(1)}, f32[64,512]{1,0:T(8,128)S(1)}, f32[64,5...) custom-call(s32[16,64]{1,0:T(8,128)S(1)} %get-tuple-element.102.refs_0_,, ...), custom_call_target="tpu_custom_call" | custom-call | flops 1 | bytes 1 | tf_op jit(solution)/shard_map/process/pallas_call | solution.py:129
  33.0 4.2 %collective-permute-done.3.refs_1_ = bf16[64,512]{1,0:T(8,128)(2,1)S(1)} collective-permute-done((bf16[64,512]{1,0:T(8,128)(2,1)S(1)}, bf16[64,512]{1,0:T(8,128)(2,1)S(1)}, u32[]{:S(2)}, u32[]{:S(2)}) %collective-permute-start.3) | collective-permute-done | bytes 65568 | tf_op jit(solution)/shard_map/ppermute | solution.py:422
  37.2 1.5 %mesh_grads.1 = (f32[768,512]{1,0:T(8,128)S(1)}, bf16[768,512]{1,0:T(8,128)(2,1)S(1)}, bf16[1024,512]{1,0:T(8,128)(2,1)S(1)}) custom-call(f32[256,512]{1,0:T(8,128)S(1)} %get-tuple-element.117.refs_0_.refs_1_, bf16[64,512]{1,0:T(8,128)(2,1)S(1)} %collective-permute-done.3.refs_1_, bf16[64,512]{1,0:T(8,128)(2,1)S(1)} %collective-permute-done.4.refs_2_, ...), custom_call_target="tpu_custom_call" | custom-call | flops 10000000000 | bytes 1 | tf_op jit(solution)/shard_map/mesh_grads/pallas_call | solution.py:129
  38.8 2.4 %grid_grads.1 = (f32[512,512]{1,0:T(8,128)S(1)}, bf16[512,512]{1,0:T(8,128)(2,1)S(1)}) custom-call(f32[768,512]{1,0:T(8,128)S(1)} %get-tuple-element.126.refs_0_.refs_1_, s32[16,64]{1,0:T(8,128)S(1)} %get-tuple-element.83.refs_0_.refs_1_, bf16[1024,512]{1,0:T(8,128)(2,1)S(1)} %get-tuple-element.127.refs_2_, ...), custom_call_target="tpu_custom_call" | custom-call | flops 10000000000 | bytes 1 | tf_op jit(solution)/shard_map/grid_grads/pallas_call | solution.py:129
  44.5 4.1 %collective-permute-done.8.refs_2_ = bf16[128,512]{1,0:T(8,128)(2,1)S(1)} collective-permute-done((bf16[128,512]{1,0:T(8,128)(2,1)S(1)}, bf16[128,512]{1,0:T(8,128)(2,1)S(1)}, u32[]{:S(2)}, u32[]{:S(2)}) %collective-permute-start.8) | collective-permute-done | bytes 131104 | tf_op jit(solution)/shard_map/ppermute | solution.py:387
  48.7 4.6 %collective-permute-done.9.refs_2_ = bf16[384,512]{1,0:T(8,128)(2,1)S(1)} collective-permute-done((bf16[384,512]{1,0:T(8,128)(2,1)S(1)}, bf16[384,512]{1,0:T(8,128)(2,1)S(1)}, u32[]{:S(2)}, u32[]{:S(2)}) %collective-permute-start.9) | collective-permute-done | bytes 393248 | tf_op jit(solution)/shard_map/ppermute | solution.py:387
  53.5 1.7 %collective-permute-start.11 = (bf16[192,512]{1,0:T(8,128)(2,1)S(1)}, bf16[192,512]{1,0:T(8,128)(2,1)S(1)}, u32[]{:S(2)}, u32[]{:S(2)}) collective-permute-start(bf16[192,512]{1,0:T(8,128)(2,1)S(1)} %get-tuple-element.145), channel_id=1, source_target_pairs={{0,4},{1,5},{2,6},{3,7},{4,0},{5,1},{6,2},{7,3},{8,12},{9,13},{10,... | collective-permute-start | bytes 589832 | tf_op jit(solution)/shard_map/ppermute | solution.py:387
  55.6 4.7 %collective-permute-done.11.refs_2_ = bf16[192,512]{1,0:T(8,128)(2,1)S(1)} collective-permute-done((bf16[192,512]{1,0:T(8,128)(2,1)S(1)}, bf16[192,512]{1,0:T(8,128)(2,1)S(1)}, u32[]{:S(2)}, u32[]{:S(2)}) %collective-permute-start.11) | collective-permute-done | bytes 196640 | tf_op jit(solution)/shard_map/ppermute | solution.py:387
  61.4 2.8 %collective-permute-start.16 = (bf16[128,512]{1,0:T(8,128)(2,1)S(1)}, bf16[128,512]{1,0:T(8,128)(2,1)S(1)}, u32[]{:S(2)}, u32[]{:S(2)}) collective-permute-start(bf16[128,512]{1,0:T(8,128)(2,1)S(1)} %grid_add.6.refs_0_.refs_1_), channel_id=1, source_target_pairs={{0,8},{1,9},{2,10},{3,11},{4,12},{5,13},{6,14},{7,15},{8,0},{9,1},... | collective-permute-start | bytes 393224 | tf_op jit(solution)/shard_map/ppermute | solution.py:387
  64.2 4.1 %collective-permute-done.14.refs_2_ = bf16[128,512]{1,0:T(8,128)(2,1)S(1)} collective-permute-done((bf16[128,512]{1,0:T(8,128)(2,1)S(1)}, bf16[128,512]{1,0:T(8,128)(2,1)S(1)}, u32[]{:S(2)}, u32[]{:S(2)}) %collective-permute-start.14) | collective-permute-done | bytes 131104 | tf_op jit(solution)/shard_map/ppermute | solution.py:387
  68.5 5.6 %collective-permute-done.15.refs_2_ = bf16[192,512]{1,0:T(8,128)(2,1)S(1)} collective-permute-done((bf16[192,512]{1,0:T(8,128)(2,1)S(1)}, bf16[192,512]{1,0:T(8,128)(2,1)S(1)}, u32[]{:S(2)}, u32[]{:S(2)}) %collective-permute-start.15) | collective-permute-done | bytes 196640 | tf_op jit(solution)/shard_map/ppermute | solution.py:387
  74.2 1.8 %collective-permute-done.16.refs_2_ = bf16[128,512]{1,0:T(8,128)(2,1)S(1)} collective-permute-done((bf16[128,512]{1,0:T(8,128)(2,1)S(1)}, bf16[128,512]{1,0:T(8,128)(2,1)S(1)}, u32[]{:S(2)}, u32[]{:S(2)}) %collective-permute-start.16) | collective-permute-done | bytes 131104 | tf_op jit(solution)/shard_map/ppermute | solution.py:387
  76.7 3.5 %collective-permute-done.18.refs_2_ = bf16[192,512]{1,0:T(8,128)(2,1)S(1)} collective-permute-done((bf16[192,512]{1,0:T(8,128)(2,1)S(1)}, bf16[192,512]{1,0:T(8,128)(2,1)S(1)}, u32[]{:S(2)}, u32[]{:S(2)}) %collective-permute-start.18) | collective-permute-done | bytes 196640 | tf_op jit(solution)/shard_map/ppermute | solution.py:387
  81.9 1.5 %process_collect.1 = (f32[512,512]{1,0:T(8,128)}, f32[512,512]{1,0:T(8,128)}) custom-call(bf16[256,512]{1,0:T(8,128)(2,1)S(1)} %grid_join.2.refs_0_.refs_1_, bf16[512,512]{1,0:T(8,128)(2,1)S(1)} %process_join.3.refs_0_.refs_1_, bf16[512,512]{1,0:T(8,128)(2,1)S(1)} %collective-permute-done.20.refs_2_), custom_call_target="tpu_custom_call" | custom-call | flops 10000000000 | bytes 1 | tf_op jit(solution)/shard_map/process_collect/pallas_call | solution.py:129
  83.4 4.3 %collective-permute-done.21.refs_2_ = bf16[256,512]{1,0:T(8,128)(2,1)S(1)} collective-permute-done((bf16[256,512]{1,0:T(8,128)(2,1)S(1)}, bf16[256,512]{1,0:T(8,128)(2,1)S(1)}, u32[]{:S(2)}, u32[]{:S(2)}) %collective-permute-start.21) | collective-permute-done | bytes 262176 | tf_op jit(solution)/shard_map/ppermute | solution.py:387
  87.9 1.7 %collective-permute-done.22.refs_2_ = bf16[384,512]{1,0:T(8,128)(2,1)S(1)} collective-permute-done((bf16[384,512]{1,0:T(8,128)(2,1)S(1)}, bf16[384,512]{1,0:T(8,128)(2,1)S(1)}, u32[]{:S(2)}, u32[]{:S(2)}) %collective-permute-start.22) | collective-permute-done | bytes 393248 | tf_op jit(solution)/shard_map/ppermute | solution.py:387
  92.0 1.9 %mesh_collect.1 = (f32[512,512]{1,0:T(8,128)}, f32[512,512]{1,0:T(8,128)}, f32[512,512]{1,0:T(8,128)}) custom-call(f32[512,512]{1,0:T(8,128)} %get-tuple-element.75.refs_0_, bf16[768,512]{1,0:T(8,128)(2,1)S(1)} %mesh_join.3.refs_0_.refs_1_, bf16[768,512]{1,0:T(8,128)(2,1)S(1)} %collective-permute-done.24.refs_2_), custom_call_target="tpu_custom_call" | custom-call | flops 10000000000 | bytes 1 | tf_op jit(solution)/shard_map/mesh_collect/pallas_call | solution.py:129
  (57 shorter events, 13.9 us)
Async XLA Ops:
  2.7 15.3 %all-to-all-start = ((bf16[16,8,474]{2,1,0:T(8,128)(2,1)}), bf16[16,8,474]{2,1,0:T(8,128)(2,1)S(1)}, u32[]{:S(2)}, u32[]{:S(2)}) async-start(bf16[16,8,474]{2,1,0:T(8,128)(2,1)} %bitcast.8), calls=%async_computation | async-start | bytes 262144 | tf_op jit(solution)/shard_map/all_to_all | solution.py:445
  21.0 6.5 %collective-permute-start = (bf16[64,512]{1,0:T(8,128)(2,1)S(1)}, bf16[64,512]{1,0:T(8,128)(2,1)S(1)}, u32[]{:S(2)}, u32[]{:S(2)}) collective-permute-start(bf16[64,512]{1,0:T(8,128)(2,1)S(1)} %get-tuple-element.105), channel_id=1, source_target_pairs={{1,2},{3,4},{5,6},{7,8},{9,10},{11,12},{13,14},{15,0},{2,1},{4,3},... | collective-permute-start | bytes 196616 | tf_op jit(solution)/shard_map/ppermute | solution.py:422
  21.7 5.7 %collective-permute-start.1 = (bf16[64,512]{1,0:T(8,128)(2,1)S(1)}, bf16[64,512]{1,0:T(8,128)(2,1)S(1)}, u32[]{:S(2)}, u32[]{:S(2)}) collective-permute-start(bf16[64,512]{1,0:T(8,128)(2,1)S(1)} %get-tuple-element.106), channel_id=1, source_target_pairs={{0,1},{2,3},{4,5},{6,7},{8,9},{10,11},{12,13},{14,15},{1,0},{3,2},... | collective-permute-start | bytes 196616 | tf_op jit(solution)/shard_map/ppermute | solution.py:422
  30.7 6.6 %collective-permute-start.3 = (bf16[64,512]{1,0:T(8,128)(2,1)S(1)}, bf16[64,512]{1,0:T(8,128)(2,1)S(1)}, u32[]{:S(2)}, u32[]{:S(2)}) collective-permute-start(bf16[64,512]{1,0:T(8,128)(2,1)S(1)} %get-tuple-element.118), channel_id=1, source_target_pairs={{1,2},{3,4},{5,6},{7,8},{9,10},{11,12},{13,14},{15,0},{2,1},{4,3},... | collective-permute-start | bytes 196616 | tf_op jit(solution)/shard_map/ppermute | solution.py:422
  31.4 5.8 %collective-permute-start.4 = (bf16[64,512]{1,0:T(8,128)(2,1)S(1)}, bf16[64,512]{1,0:T(8,128)(2,1)S(1)}, u32[]{:S(2)}, u32[]{:S(2)}) collective-permute-start(bf16[64,512]{1,0:T(8,128)(2,1)S(1)} %get-tuple-element.119), channel_id=1, source_target_pairs={{0,1},{2,3},{4,5},{6,7},{8,9},{10,11},{12,13},{14,15},{1,0},{3,2},... | collective-permute-start | bytes 196616 | tf_op jit(solution)/shard_map/ppermute | solution.py:422
  32.7 9.3 %collective-permute-start.6 = (bf16[256,512]{1,0:T(8,128)(2,1)S(1)}, bf16[256,512]{1,0:T(8,128)(2,1)S(1)}, u32[]{:S(2)}, u32[]{:S(2)}) collective-permute-start(bf16[256,512]{1,0:T(8,128)(2,1)S(1)} %get-tuple-element.136), channel_id=1, source_target_pairs={{0,2},{1,3},{2,0},{3,1},{4,6},{5,7},{6,4},{7,5},{8,10},{9,11},{10,... | collective-permute-start | bytes 786440 | tf_op jit(solution)/shard_map/ppermute | solution.py:387
  38.8 3.1 %collective-permute-start.5 = (bf16[768,512]{1,0:T(8,128)(2,1)S(1)}, bf16[768,512]{1,0:T(8,128)(2,1)S(1)}, u32[]{:S(2)}, u32[]{:S(2)}) collective-permute-start(bf16[768,512]{1,0:T(8,128)(2,1)S(1)} %get-tuple-element.134), channel_id=1, source_target_pairs={{0,1},{1,0},{2,3},{3,2},{4,5},{5,4},{6,7},{7,6},{8,9},{9,8},{10,11... | collective-permute-start | bytes 2359304 | tf_op jit(solution)/shard_map/ppermute | solution.py:387
  41.3 2.1 %collective-permute-start.7 = (bf16[512,512]{1,0:T(8,128)(2,1)S(1)}, bf16[512,512]{1,0:T(8,128)(2,1)S(1)}, u32[]{:S(2)}, u32[]{:S(2)}) collective-permute-start(bf16[512,512]{1,0:T(8,128)(2,1)S(1)} %get-tuple-element.138), channel_id=1, source_target_pairs={{0,1},{1,0},{2,3},{3,2},{4,5},{5,4},{6,7},{7,6},{8,9},{9,8},{10,11... | collective-permute-start | bytes 1572872 | tf_op jit(solution)/shard_map/ppermute | solution.py:387
  42.2 6.4 %collective-permute-start.8 = (bf16[128,512]{1,0:T(8,128)(2,1)S(1)}, bf16[128,512]{1,0:T(8,128)(2,1)S(1)}, u32[]{:S(2)}, u32[]{:S(2)}) collective-permute-start(bf16[128,512]{1,0:T(8,128)(2,1)S(1)} %get-tuple-element.140), channel_id=1, source_target_pairs={{0,4},{1,5},{2,6},{3,7},{4,0},{5,1},{6,2},{7,3},{8,12},{9,13},{10,... | collective-permute-start | bytes 393224 | tf_op jit(solution)/shard_map/ppermute | solution.py:387
  42.2 11.1 %collective-permute-start.9 = (bf16[384,512]{1,0:T(8,128)(2,1)S(1)}, bf16[384,512]{1,0:T(8,128)(2,1)S(1)}, u32[]{:S(2)}, u32[]{:S(2)}) collective-permute-start(bf16[384,512]{1,0:T(8,128)(2,1)S(1)} %get-tuple-element.141), channel_id=1, source_target_pairs={{0,2},{1,3},{2,0},{3,1},{4,6},{5,7},{6,4},{7,5},{8,10},{9,11},{10,... | collective-permute-start | bytes 1179656 | tf_op jit(solution)/shard_map/ppermute | solution.py:387
  43.5 11.7 %collective-permute-start.10 = (bf16[256,512]{1,0:T(8,128)(2,1)S(1)}, bf16[256,512]{1,0:T(8,128)(2,1)S(1)}, u32[]{:S(2)}, u32[]{:S(2)}) collective-permute-start(bf16[256,512]{1,0:T(8,128)(2,1)S(1)} %get-tuple-element.143), channel_id=1, source_target_pairs={{0,4},{1,5},{2,6},{3,7},{4,0},{5,1},{6,2},{7,3},{8,12},{9,13},{10,... | collective-permute-start | bytes 786440 | tf_op jit(solution)/shard_map/ppermute | solution.py:387
  48.6 11.8 %collective-permute-start.12 = (bf16[128,512]{1,0:T(8,128)(2,1)S(1)}, bf16[128,512]{1,0:T(8,128)(2,1)S(1)}, u32[]{:S(2)}, u32[]{:S(2)}) collective-permute-start(bf16[128,512]{1,0:T(8,128)(2,1)S(1)} %process_add.6.refs_0_.refs_1_), channel_id=1, source_target_pairs={{0,8},{1,9},{2,10},{3,11},{4,12},{5,13},{6,14},{7,15},{8,0},{9,1},... | collective-permute-start | bytes 393224 | tf_op jit(solution)/shard_map/ppermute | solution.py:387
  53.5 6.8 %collective-permute-start.11 = (bf16[192,512]{1,0:T(8,128)(2,1)S(1)}, bf16[192,512]{1,0:T(8,128)(2,1)S(1)}, u32[]{:S(2)}, u32[]{:S(2)}) collective-permute-start(bf16[192,512]{1,0:T(8,128)(2,1)S(1)} %get-tuple-element.145), channel_id=1, source_target_pairs={{0,4},{1,5},{2,6},{3,7},{4,0},{5,1},{6,2},{7,3},{8,12},{9,13},{10,... | collective-permute-start | bytes 589832 | tf_op jit(solution)/shard_map/ppermute | solution.py:387
  55.3 6.1 %collective-permute-start.13 = (bf16[128,512]{1,0:T(8,128)(2,1)S(1)}, bf16[128,512]{1,0:T(8,128)(2,1)S(1)}, u32[]{:S(2)}, u32[]{:S(2)}) collective-permute-start(bf16[128,512]{1,0:T(8,128)(2,1)S(1)} %get-tuple-element.146), channel_id=1, source_target_pairs={{0,2},{1,3},{2,0},{3,1},{4,6},{5,7},{6,4},{7,5},{8,10},{9,11},{10,... | collective-permute-start | bytes 393224 | tf_op jit(solution)/shard_map/ppermute | solution.py:387
  60.4 13.7 %collective-permute-start.15 = (bf16[192,512]{1,0:T(8,128)(2,1)S(1)}, bf16[192,512]{1,0:T(8,128)(2,1)S(1)}, u32[]{:S(2)}, u32[]{:S(2)}) collective-permute-start(bf16[192,512]{1,0:T(8,128)(2,1)S(1)} %mesh_add.6.refs_0_.refs_1_), channel_id=1, source_target_pairs={{0,8},{1,9},{2,10},{3,11},{4,12},{5,13},{6,14},{7,15},{8,0},{9,1},... | collective-permute-start | bytes 589832 | tf_op jit(solution)/shard_map/ppermute | solution.py:387
  60.5 7.8 %collective-permute-start.14 = (bf16[128,512]{1,0:T(8,128)(2,1)S(1)}, bf16[128,512]{1,0:T(8,128)(2,1)S(1)}, u32[]{:S(2)}, u32[]{:S(2)}) collective-permute-start(bf16[128,512]{1,0:T(8,128)(2,1)S(1)} %process_add.7.refs_0_.refs_1_), channel_id=1, source_target_pairs={{0,4},{1,5},{2,6},{3,7},{4,0},{5,1},{6,2},{7,3},{8,12},{9,13},{10,... | collective-permute-start | bytes 393224 | tf_op jit(solution)/shard_map/ppermute | solution.py:387
  61.4 14.7 %collective-permute-start.16 = (bf16[128,512]{1,0:T(8,128)(2,1)S(1)}, bf16[128,512]{1,0:T(8,128)(2,1)S(1)}, u32[]{:S(2)}, u32[]{:S(2)}) collective-permute-start(bf16[128,512]{1,0:T(8,128)(2,1)S(1)} %grid_add.6.refs_0_.refs_1_), channel_id=1, source_target_pairs={{0,8},{1,9},{2,10},{3,11},{4,12},{5,13},{6,14},{7,15},{8,0},{9,1},... | collective-permute-start | bytes 393224 | tf_op jit(solution)/shard_map/ppermute | solution.py:387
  68.4 8.2 %collective-permute-start.17 = (bf16[256,512]{1,0:T(8,128)(2,1)S(1)}, bf16[256,512]{1,0:T(8,128)(2,1)S(1)}, u32[]{:S(2)}, u32[]{:S(2)}) collective-permute-start(bf16[256,512]{1,0:T(8,128)(2,1)S(1)} %process_join.2.refs_0_.refs_1_), channel_id=1, source_target_pairs={{0,2},{1,3},{2,0},{3,1},{4,6},{5,7},{6,4},{7,5},{8,10},{9,11},{10,... | collective-permute-start | bytes 786440 | tf_op jit(solution)/shard_map/ppermute | solution.py:387
  74.2 6.0 %collective-permute-start.18 = (bf16[192,512]{1,0:T(8,128)(2,1)S(1)}, bf16[192,512]{1,0:T(8,128)(2,1)S(1)}, u32[]{:S(2)}, u32[]{:S(2)}) collective-permute-start(bf16[192,512]{1,0:T(8,128)(2,1)S(1)} %mesh_add.7.refs_0_.refs_1_), channel_id=1, source_target_pairs={{0,4},{1,5},{2,6},{3,7},{4,0},{5,1},{6,2},{7,3},{8,12},{9,13},{10,... | collective-permute-start | bytes 589832 | tf_op jit(solution)/shard_map/ppermute | solution.py:387
  76.1 5.0 %collective-permute-start.19 = (bf16[128,512]{1,0:T(8,128)(2,1)S(1)}, bf16[128,512]{1,0:T(8,128)(2,1)S(1)}, u32[]{:S(2)}, u32[]{:S(2)}) collective-permute-start(bf16[128,512]{1,0:T(8,128)(2,1)S(1)} %grid_add.7.refs_0_.refs_1_), channel_id=1, source_target_pairs={{0,2},{1,3},{2,0},{3,1},{4,6},{5,7},{6,4},{7,5},{8,10},{9,11},{10,... | collective-permute-start | bytes 393224 | tf_op jit(solution)/shard_map/ppermute | solution.py:387
  76.6 5.3 %collective-permute-start.20 = (bf16[512,512]{1,0:T(8,128)(2,1)S(1)}, bf16[512,512]{1,0:T(8,128)(2,1)S(1)}, u32[]{:S(2)}, u32[]{:S(2)}) collective-permute-start(bf16[512,512]{1,0:T(8,128)(2,1)S(1)} %process_join.3.refs_0_.refs_1_), channel_id=1, source_target_pairs={{0,1},{1,0},{2,3},{3,2},{4,5},{5,4},{6,7},{7,6},{8,9},{9,8},{10,11... | collective-permute-start | bytes 1572872 | tf_op jit(solution)/shard_map/ppermute | solution.py:387
  80.3 9.3 %collective-permute-start.22 = (bf16[384,512]{1,0:T(8,128)(2,1)S(1)}, bf16[384,512]{1,0:T(8,128)(2,1)S(1)}, u32[]{:S(2)}, u32[]{:S(2)}) collective-permute-start(bf16[384,512]{1,0:T(8,128)(2,1)S(1)} %mesh_join.2.refs_0_.refs_1_), channel_id=1, source_target_pairs={{0,2},{1,3},{2,0},{3,1},{4,6},{5,7},{6,4},{7,5},{8,10},{9,11},{10,... | collective-permute-start | bytes 1179656 | tf_op jit(solution)/shard_map/ppermute | solution.py:387
  81.2 6.5 %collective-permute-start.21 = (bf16[256,512]{1,0:T(8,128)(2,1)S(1)}, bf16[256,512]{1,0:T(8,128)(2,1)S(1)}, u32[]{:S(2)}, u32[]{:S(2)}) collective-permute-start(bf16[256,512]{1,0:T(8,128)(2,1)S(1)} %grid_join.2.refs_0_.refs_1_), channel_id=1, source_target_pairs={{0,4},{1,5},{2,6},{3,7},{4,0},{5,1},{6,2},{7,3},{8,12},{9,13},{10,... | collective-permute-start | bytes 786440 | tf_op jit(solution)/shard_map/ppermute | solution.py:387
  89.7 2.4 %collective-permute-start.24 = (bf16[768,512]{1,0:T(8,128)(2,1)S(1)}, bf16[768,512]{1,0:T(8,128)(2,1)S(1)}, u32[]{:S(2)}, u32[]{:S(2)}) collective-permute-start(bf16[768,512]{1,0:T(8,128)(2,1)S(1)} %mesh_join.3.refs_0_.refs_1_), channel_id=1, source_target_pairs={{0,1},{1,0},{2,3},{3,2},{4,5},{5,4},{6,7},{7,6},{8,9},{9,8},{10,11... | collective-permute-start | bytes 2359304 | tf_op jit(solution)/shard_map/ppermute | solution.py:387
  (2 other events, 4.0 us)

commit v6 on v5

--- a/solution.py
+++ b/solution.py
@@ -157,15 +157,17 @@
     return lat, silu_slope(pre, s).astype(BF), dot(lat, ws).astype(BF)
 
 
-def embed_body(ins, outs, _):
-    x_t, we, ws, latent, wrecv = ins[:5]
-    lat, slope, proj, recv = outs
+def embed_body(ins, outs, scratch):
+    slots_t, x_t, we, ws, latent, wrecv = ins[:6]
+    lat, slope, rows, recv = outs
+    (onehot,) = scratch
+    fill_onehot(onehot, slots_t()[...].T)
     x_t()
     at = t_dot(x_t()[...], we()[...])
     one, two, three = embed_rows(at, ws()[...])
     lat.set(one)
     slope.set(two)
-    proj.set(three)
+    rows.set(dot(onehot[...], three))
     recv.set(dot(latent()[...], wrecv()[...]))
 
 
@@ -200,21 +202,18 @@
     return total.astype(BF)
 
 
-def encode_body(me, ins, outs, scratch):
-    slots_t, mask_t, x, we, ws, proj, recv, wout, latent, wnext, halo = ins
+def encode_body(near, me, ins, outs, scratch):
+    slots_t, mask_t, x, we, ws, rows_near, recv, wout, latent, wnext, halo = ins
     mid, one, two, mesh_proj, agg, y, r, slope, lat_far, slope_far = outs
-    table, onehot, rows = scratch
-    near = proj.held.shape[0]
-    fill_onehot(onehot, slots_t()[...].T)
+    onehot, rows = scratch
+    fill_onehot(onehot, slots_t()[...].T - near)
     mask = mask_t()[...].T
     x()
     pre = dot(x()[...], we()[...])
     lat, bend, far = embed_rows(pre, ws()[...])
     lat_far.set(lat)
     slope_far.set(bend)
-    table[near:, :] = far
-    table[:near, :] = proj()[...]
-    rows[...] = dot(onehot[...], table[...])
+    rows[...] = rows_near()[...].astype(F32) + dot(onehot[...], far)
     summed = messages(rows, recv()[...], mask, slope.held)
     slope.send()
     agg.set(summed)
@@ -234,23 +233,20 @@
 
 
 def process_body(me, ins, outs, scratch):
-    slots_t, mask_t, mesh_proj, one, two, mid, wrecv, wout, cotangent = ins
+    onehot, onehot_t, recv, mask_t, mesh_proj, one, two, mid, wrecv, wout, cotangent = ins
     out, back_one, back_two, grad_rows, grad_mid, agg, grad_u, grad_recv = outs
-    table, onehot, onehot_t, rows, slope, grad_msg = scratch
+    table, rows, slope, grad_msg = scratch
     m = mesh_proj.held.shape[0]
     depth = one.held.shape[0]
     odd = me % 2 == 0
-    slots = slots_t()[...]
-    fill_onehot(onehot, slots.T)
     mask = mask_t()[...].T
-    fill_onehot_t(onehot_t, slots)
     table[:m, :] = mesh_proj()[...]
     from_one, from_two = one()[...], two()[...]
     table[m : m + depth, :] = jnp.where(odd, from_one, from_two)
     table[m + depth : m + 2 * depth, :] = jnp.where(odd, from_two, from_one)
-    rows[...] = dot(onehot[...], table[...])
+    rows[...] = dot(onehot()[...], table[...])
     middle = mid()[...]
-    summed = messages(rows, dot(middle, wrecv()[...]), mask, slope)
+    summed = messages(rows, recv()[...], mask, slope)
     agg.set(summed)
     normed, scale = normalized(dot(summed, wout()[...]))
     out.set(middle.astype(F32) + normed)
@@ -259,7 +255,7 @@
     grad_u.set(gu)
     gr = message_grads(grad_msg, slope, dot_t(gu, wout()[...]), mask.shape[1])
     grad_recv.set(gr)
-    grads = dot(onehot_t[...], grad_msg[...])
+    grads = dot(onehot_t()[...], grad_msg[...])
     to_left, to_right = grads[m : m + depth, :], grads[m + depth :, :]
     back_one.set(jnp.where(odd, to_left, to_right))
     back_two.set(jnp.where(odd, to_right, to_left))
@@ -330,11 +326,10 @@
 
 
 def grid_grads_body(order, me, ins, outs, scratch):
-    slots_t, grad_msg, ws, slope_near, slope_far, x_t, x_far, lat, lat_far = ins
-    onehot_t, g_send, g_embed = scratch
+    onehot_t, grad_msg, ws, slope_near, slope_far, x_t, x_far, lat, lat_far = ins
+    g_send, g_embed = scratch
     near = lat.held.shape[0]
-    fill_onehot_t(onehot_t, slots_t()[...])
-    grad_table = dot(onehot_t[...], grad_msg()[...]).astype(BF)
+    grad_table = dot(onehot_t()[...], grad_msg()[...]).astype(BF)
     g_near, g_far = grad_table[:near, :], grad_table[near:, :]
     p_near = (dot_t(g_near, ws()[...]) * slope_near()[...].astype(F32)).astype(BF)
     p_far = (dot_t(g_far, ws()[...]) * slope_far()[...].astype(F32)).astype(BF)
@@ -378,8 +373,13 @@
 
 
 def load_body(ins, outs, _):
-    for value in ins:
-        value()
+    slots_t, mid, wrecv, enc_slots_t = ins[:4]
+    onehot, onehot_t, enc_onehot_t, recv = outs
+    slots = slots_t()[...]
+    fill_onehot(onehot.held, slots.T)
+    fill_onehot_t(onehot_t.held, slots)
+    fill_onehot_t(enc_onehot_t.held, enc_slots_t()[...])
+    recv.set(dot(mid()[...], wrecv()[...]))
 
 
 def exchange(value, step):
@@ -447,45 +447,45 @@
 
     patch, edge_rows, patch_f32 = ((m, width), BF), ((depth, width), BF), ((m, width), F32)
     grid_rows, far_rows = ((near, width), BF), ((far, width), BF)
-    lat, slope_near, proj, recv, w_embed, enc_send, latent, enc_out, proc_send, halo, enc_slot_t, enc_mask_t = call(
+    lat, slope_near, rows_near, recv, enc_slot_t, w_embed, enc_send, latent, enc_out, proc_send, halo, enc_mask_t = call(
         embed_body,
         "embed",
-        [Far(x_t), Kept(w_embed), Kept(enc_send), Kept(mesh_latent), Far(enc_recv), Kept(enc_out), Kept(proc_send),
-         Kept(halo), Kept(enc_slot_t), Kept(enc_mask_t)],
-        [(*grid_rows, "far"), (*grid_rows, "far"), grid_rows, patch_f32],
+        [Kept(enc_slot_t), Far(x_t), Kept(w_embed), Kept(enc_send), Kept(mesh_latent), Far(enc_recv), Kept(enc_out),
+         Kept(proc_send), Kept(halo), Kept(enc_mask_t)],
+        [(*grid_rows, "far"), (*grid_rows, "far"), ((edges_e, width), BF), patch_f32],
+        [((edges_e, near), BF)],
         weight=FIRST[1],
     )
 
     mid, to_one, to_two, mesh_proj, agg, y, r, slope, lat_far, slope_far = call(
-        encode_body,
+        functools.partial(encode_body, near),
         "encode",
-        [enc_slot_t, enc_mask_t, x_far, w_embed, enc_send, proj, recv, enc_out, latent, proc_send, halo],
+        [enc_slot_t, enc_mask_t, x_far, w_embed, enc_send, rows_near, recv, enc_out, latent, proc_send, halo],
         [patch, edge_rows, edge_rows, patch, patch, patch_f32, ((m, 128), F32), ((edges_e, width), BF), far_rows,
          far_rows],
-        [((near + far, width), BF), ((edges_e, near + far), BF), ((edges_e, width), F32)],
+        [((edges_e, far), BF), ((edges_e, width), F32)],
         place=True,
     )
 
     from_one, from_two = swapped(to_one, 1), swapped(to_two, 0)
 
-    after = (x_t, lat, slope_near, proc_recv, proc_out, cotangent, proc_slot_t, proc_mask_t, mid)
-    x_t, lat, slope_near, proc_recv, proc_out, cotangent, proc_slot_t, proc_mask_t, mid = lax.optimization_barrier(after)
-    x_t, lat, slope_near, proc_recv, proc_out, cotangent, proc_slot_t, proc_mask_t = call(
+    wide = m + 2 * depth
+    later = (proc_slot_t, proc_recv, x_t, lat, slope_near, proc_out, cotangent, proc_mask_t)
+    *later, mid = lax.optimization_barrier((*later, mid))
+    onehot_p, onehot_p_t, onehot_e_t, recv_p, proc_recv, x_t, lat, slope_near, proc_out, cotangent, proc_mask_t = call(
         load_body,
         "load",
-        [Kept(v) for v in (x_t, lat, slope_near, proc_recv, proc_out, cotangent, proc_slot_t, proc_mask_t)],
-        [],
+        [Far(later[0]), mid, Kept(later[1]), enc_slot_t, *(Kept(v) for v in later[2:])],
+        [((edges_p, wide), BF), ((wide, edges_p), BF), ((near + far, edges_e), BF), patch_f32],
         weight=FIRST[3],
     )
 
-    wide = m + 2 * depth
     out, back_one, back_two, grad_rows, grad_mid, agg2, grad_u, grad_recv = call(
         process_body,
         "process",
-        [proc_slot_t, proc_mask_t, mesh_proj, from_one, from_two, mid, proc_recv, proc_out, cotangent],
+        [onehot_p, onehot_p_t, recv_p, proc_mask_t, mesh_proj, from_one, from_two, mid, proc_recv, proc_out, cotangent],
         [(*patch, "far"), edge_rows, edge_rows, patch_f32, patch_f32, patch, patch, patch],
-        [((wide, width), BF), ((edges_p, wide), BF), ((wide, edges_p), BF), ((edges_p, width), F32),
-         ((edges_p, width), F32), ((edges_p, width), BF)],
+        [((wide, width), BF), ((edges_p, width), F32), ((edges_p, width), F32), ((edges_p, width), BF)],
         place=True,
         weight=FIRST[4],
     )
@@ -523,9 +523,9 @@
             keep, send = call(
                 functools.partial(grid_grads_body, ORDER_G),
                 "grid_grads",
-                [enc_slot_t, grad_msg, enc_send, slope_near, slope_far, x_t, x_far, lat, lat_far],
+                [onehot_e_t, grad_msg, enc_send, slope_near, slope_far, x_t, x_far, lat, lat_far],
                 halves(2),
-                [((near + far, edges_e), BF)] + [square] * 2,
+                [square] * 2,
                 True,
                 token,
                 weight,

time: 94.2 us -> 93.7 us (level)
  transfers between devices with their start and end apart: 26 -> 26, of which waited for: 16 -> 16; matrix products, arithmetic and copies ran while one was open for 0% -> 0% of each run, Pallas kernels for 14% -> 15%
where the time goes in v6:
time: 93.7 us; the launch traced here: 93.3 us
  waiting for transfers between devices  50.4 us (54%)
  Pallas kernels  23.1 us (25%)
  starting transfers between devices  18.8 us (20%)
  between operations  0.98 us (1%)
    ppermute x21, waiting for transfers between devices, exchange(): return lax.ppermute(value, 'space', [(i, i ^ step) for i in range(n)])  38 us
    pallas_call x29, Pallas kernels, call(): pl.pallas_call(kernel, name=name, out_shape=[(pltpu.HBM if far else pltpu...  23.1 us
    ppermute x21, starting transfers between devices, exchange(): return lax.ppermute(value, 'space', [(i, i ^ step) for i in range(n)])  9.9 us
    ppermute x4, waiting for transfers between devices, swapped(): return lax.ppermute(rows, 'space', [*pairs, *((b, a) for a, b in pairs)])  7.7 us
    all_to_all x1, starting transfers between devices, local(): lax.all_to_all(outgoing.reshape(n, -1, fin), 'space', split_axis=0, conca...  7.4 us
    all_to_all x1, waiting for transfers between devices, local(): lax.all_to_all(outgoing.reshape(n, -1, fin), 'space', split_axis=0, conca...  4.69 us
  transfers between devices with their start and end apart: 26, of which 16 were waited for; matrix products, arithmetic and copies ran while one was open for 0% of the time, Pallas kernels for 15%

profile of v6, /device:TPU:0, one launch (start us, length us, event | category | flops | bytes accessed | tf_op | source)
XLA Modules:
  0.0 93.3 jit_solution(17443758979909614538)
XLA Ops:
  0.6 2.0 %pick.1 = bf16[128,474]{1,0:T(8,128)(2,1)} custom-call(s32[8,16]{1,0:T(8,128)} %bitcast.20, bf16[474,512]{1,0:T(8,128)(2,1)} %bitcast.13), custom_call_target="tpu_custom_call" | custom-call | flops 1 | bytes 1 | tf_op jit(solution)/shard_map/pick/pallas_call | solution.py:129
  2.7 7.4 %all-to-all-start = ((bf16[16,8,474]{2,1,0:T(8,128)(2,1)}), bf16[16,8,474]{2,1,0:T(8,128)(2,1)S(1)}, u32[]{:S(2)}, u32[]{:S(2)}) async-start(bf16[16,8,474]{2,1,0:T(8,128)(2,1)} %bitcast.8), calls=%async_computation | async-start | bytes 262144 | tf_op jit(solution)/shard_map/all_to_all | solution.py:445
  10.1 3.2 %embed.1 = (bf16[512,512]{1,0:T(8,128)(2,1)}, bf16[512,512]{1,0:T(8,128)(2,1)}, bf16[1024,512]{1,0:T(8,128)(2,1)S(1)}, f32[64,512]{1,0:T(8,128)S(1)}, s32[16,64]...) custom-call(s32[16,64]{1,0:T(8,128)} %bitcast.16, ...), custom_call_target="tpu_custom_call" | custom-call | flops 1 | bytes 1 | tf_op jit(solution)/shard_map/embed/pallas_call | solution.py:129
  13.3 4.7 %all-to-all-done = bf16[16,8,474]{2,1,0:T(8,128)(2,1)S(1)} async-done(((bf16[16,8,474]{2,1,0:T(8,128)(2,1)}), bf16[16,8,474]{2,1,0:T(8,128)(2,1)S(1)}, u32[]{:S(2)}, u32[]{:S(2)}) %all-to-all-start) | async-done | bytes 121376 | tf_op jit(solution)/shard_map/all_to_all | solution.py:445
  18.0 2.5 %encode.1 = (bf16[64,512]{1,0:T(8,128)(2,1)S(1)}, bf16[64,512]{1,0:T(8,128)(2,1)S(1)}, bf16[64,512]{1,0:T(8,128)(2,1)S(1)}, bf16[64,512]{1,0:T(8,128)(2,1)S(1)},...) custom-call(s32[16,64]{1,0:T(8,128)S(1)} %get-tuple-element.86.refs_, ...), custom_call_target="tpu_custom_call" | custom-call | flops 1 | bytes 1 | tf_op jit(solution)/shard_map/encode/pallas_call | solution.py:129
  21.3 2.2 %load.1 = (bf16[1024,192]{1,0:T(8,128)(2,1)S(1)}, bf16[192,1024]{1,0:T(8,128)(2,1)S(1)}, bf16[640,1024]{1,0:T(8,128)(2,1)S(1)}, f32[64,512]{1,0:T(8,128)S(1)}, b...) custom-call(s32[16,64]{1,0:T(8,128)} %bitcast.18, ...), custom_call_target="tpu_custom_call" | custom-call | flops 1 | bytes 1 | tf_op jit(solution)/shard_map/load/pallas_call | solution.py:129
  23.5 3.5 %collective-permute-done.refs_5_ = bf16[64,512]{1,0:T(8,128)(2,1)S(1)} collective-permute-done((bf16[64,512]{1,0:T(8,128)(2,1)S(1)}, bf16[64,512]{1,0:T(8,128)(2,1)S(1)}, u32[]{:S(2)}, u32[]{:S(2)}) %collective-permute-start) | collective-permute-done | bytes 65568 | tf_op jit(solution)/shard_map/ppermute | solution.py:422
  27.0 2.5 %process.1 = (bf16[64,512]{1,0:T(8,128)(2,1)}, bf16[64,512]{1,0:T(8,128)(2,1)S(1)}, bf16[64,512]{1,0:T(8,128)(2,1)S(1)}, f32[64,512]{1,0:T(8,128)S(1)}, f32[64,5...) custom-call(bf16[1024,192]{1,0:T(8,128)(2,1)S(1)} %get-tuple-element.106, ...), custom_call_target="tpu_custom_call" | custom-call | flops 1 | bytes 1 | tf_op jit(solution)/shard_map/process/pallas_call | solution.py:129
  32.5 4.2 %collective-permute-done.3.refs_1_ = bf16[64,512]{1,0:T(8,128)(2,1)S(1)} collective-permute-done((bf16[64,512]{1,0:T(8,128)(2,1)S(1)}, bf16[64,512]{1,0:T(8,128)(2,1)S(1)}, u32[]{:S(2)}, u32[]{:S(2)}) %collective-permute-start.3) | collective-permute-done | bytes 65568 | tf_op jit(solution)/shard_map/ppermute | solution.py:422
  36.7 1.5 %mesh_grads.1 = (f32[768,512]{1,0:T(8,128)S(1)}, bf16[768,512]{1,0:T(8,128)(2,1)S(1)}, bf16[1024,512]{1,0:T(8,128)(2,1)S(1)}) custom-call(f32[256,512]{1,0:T(8,128)S(1)} %get-tuple-element.122.refs_0_.refs_1_, bf16[64,512]{1,0:T(8,128)(2,1)S(1)} %collective-permute-done.3.refs_1_, bf16[64,512]{1,0:T(8,128)(2,1)S(1)} %collective-permute-done.4.refs_2_, ...), custom_call_target="tpu_custom_call" | custom-call | flops 10000000000 | bytes 1 | tf_op jit(solution)/shard_map/mesh_grads/pallas_call | solution.py:129
  38.3 2.4 %grid_grads.1 = (f32[512,512]{1,0:T(8,128)S(1)}, bf16[512,512]{1,0:T(8,128)(2,1)S(1)}) custom-call(f32[768,512]{1,0:T(8,128)S(1)} %get-tuple-element.131.refs_0_.refs_1_, bf16[640,1024]{1,0:T(8,128)(2,1)S(1)} %get-tuple-element.132.refs_1_, bf16[1024,512]{1,0:T(8,128)(2,1)S(1)} %get-tuple-element.133.refs_2_, ...), custom_call_target="tpu_custom_call" | custom-call | flops 10000000000 | bytes 1 | tf_op jit(solution)/shard_map/grid_grads/pallas_call | solution.py:129
  43.8 4.1 %collective-permute-done.8.refs_2_ = bf16[128,512]{1,0:T(8,128)(2,1)S(1)} collective-permute-done((bf16[128,512]{1,0:T(8,128)(2,1)S(1)}, bf16[128,512]{1,0:T(8,128)(2,1)S(1)}, u32[]{:S(2)}, u32[]{:S(2)}) %collective-permute-start.8) | collective-permute-done | bytes 131104 | tf_op jit(solution)/shard_map/ppermute | solution.py:387
  48.1 4.6 %collective-permute-done.9.refs_2_ = bf16[384,512]{1,0:T(8,128)(2,1)S(1)} collective-permute-done((bf16[384,512]{1,0:T(8,128)(2,1)S(1)}, bf16[384,512]{1,0:T(8,128)(2,1)S(1)}, u32[]{:S(2)}, u32[]{:S(2)}) %collective-permute-start.9) | collective-permute-done | bytes 393248 | tf_op jit(solution)/shard_map/ppermute | solution.py:387
  52.8 1.7 %collective-permute-start.11 = (bf16[192,512]{1,0:T(8,128)(2,1)S(1)}, bf16[192,512]{1,0:T(8,128)(2,1)S(1)}, u32[]{:S(2)}, u32[]{:S(2)}) collective-permute-start(bf16[192,512]{1,0:T(8,128)(2,1)S(1)} %get-tuple-element.151), channel_id=1, source_target_pairs={{0,4},{1,5},{2,6},{3,7},{4,0},{5,1},{6,2},{7,3},{8,12},{9,13},{10,... | collective-permute-start | bytes 589832 | tf_op jit(solution)/shard_map/ppermute | solution.py:387
  55.1 4.5 %collective-permute-done.11.refs_2_ = bf16[192,512]{1,0:T(8,128)(2,1)S(1)} collective-permute-done((bf16[192,512]{1,0:T(8,128)(2,1)S(1)}, bf16[192,512]{1,0:T(8,128)(2,1)S(1)}, u32[]{:S(2)}, u32[]{:S(2)}) %collective-permute-start.11) | collective-permute-done | bytes 196640 | tf_op jit(solution)/shard_map/ppermute | solution.py:387
  60.9 2.6 %collective-permute-start.16 = (bf16[128,512]{1,0:T(8,128)(2,1)S(1)}, bf16[128,512]{1,0:T(8,128)(2,1)S(1)}, u32[]{:S(2)}, u32[]{:S(2)}) collective-permute-start(bf16[128,512]{1,0:T(8,128)(2,1)S(1)} %grid_add.6.refs_0_.refs_1_), channel_id=1, source_target_pairs={{0,8},{1,9},{2,10},{3,11},{4,12},{5,13},{6,14},{7,15},{8,0},{9,1},... | collective-permute-start | bytes 393224 | tf_op jit(solution)/shard_map/ppermute | solution.py:387
  63.6 4.1 %collective-permute-done.14.refs_2_ = bf16[128,512]{1,0:T(8,128)(2,1)S(1)} collective-permute-done((bf16[128,512]{1,0:T(8,128)(2,1)S(1)}, bf16[128,512]{1,0:T(8,128)(2,1)S(1)}, u32[]{:S(2)}, u32[]{:S(2)}) %collective-permute-start.14) | collective-permute-done | bytes 131104 | tf_op jit(solution)/shard_map/ppermute | solution.py:387
  67.8 5.6 %collective-permute-done.15.refs_2_ = bf16[192,512]{1,0:T(8,128)(2,1)S(1)} collective-permute-done((bf16[192,512]{1,0:T(8,128)(2,1)S(1)}, bf16[192,512]{1,0:T(8,128)(2,1)S(1)}, u32[]{:S(2)}, u32[]{:S(2)}) %collective-permute-start.15) | collective-permute-done | bytes 196640 | tf_op jit(solution)/shard_map/ppermute | solution.py:387
  73.6 1.8 %collective-permute-done.16.refs_2_ = bf16[128,512]{1,0:T(8,128)(2,1)S(1)} collective-permute-done((bf16[128,512]{1,0:T(8,128)(2,1)S(1)}, bf16[128,512]{1,0:T(8,128)(2,1)S(1)}, u32[]{:S(2)}, u32[]{:S(2)}) %collective-permute-start.16) | collective-permute-done | bytes 131104 | tf_op jit(solution)/shard_map/ppermute | solution.py:387
  76.1 3.5 %collective-permute-done.18.refs_2_ = bf16[192,512]{1,0:T(8,128)(2,1)S(1)} collective-permute-done((bf16[192,512]{1,0:T(8,128)(2,1)S(1)}, bf16[192,512]{1,0:T(8,128)(2,1)S(1)}, u32[]{:S(2)}, u32[]{:S(2)}) %collective-permute-start.18) | collective-permute-done | bytes 196640 | tf_op jit(solution)/shard_map/ppermute | solution.py:387
  81.3 1.5 %process_collect.1 = (f32[512,512]{1,0:T(8,128)}, f32[512,512]{1,0:T(8,128)}) custom-call(bf16[256,512]{1,0:T(8,128)(2,1)S(1)} %grid_join.2.refs_0_.refs_1_, bf16[512,512]{1,0:T(8,128)(2,1)S(1)} %process_join.3.refs_0_.refs_1_, bf16[512,512]{1,0:T(8,128)(2,1)S(1)} %collective-permute-done.20.refs_2_), custom_call_target="tpu_custom_call" | custom-call | flops 10000000000 | bytes 1 | tf_op jit(solution)/shard_map/process_collect/pallas_call | solution.py:129
  82.8 4.3 %collective-permute-done.21.refs_2_ = bf16[256,512]{1,0:T(8,128)(2,1)S(1)} collective-permute-done((bf16[256,512]{1,0:T(8,128)(2,1)S(1)}, bf16[256,512]{1,0:T(8,128)(2,1)S(1)}, u32[]{:S(2)}, u32[]{:S(2)}) %collective-permute-start.21) | collective-permute-done | bytes 262176 | tf_op jit(solution)/shard_map/ppermute | solution.py:387
  87.3 1.7 %collective-permute-done.22.refs_2_ = bf16[384,512]{1,0:T(8,128)(2,1)S(1)} collective-permute-done((bf16[384,512]{1,0:T(8,128)(2,1)S(1)}, bf16[384,512]{1,0:T(8,128)(2,1)S(1)}, u32[]{:S(2)}, u32[]{:S(2)}) %collective-permute-start.22) | collective-permute-done | bytes 393248 | tf_op jit(solution)/shard_map/ppermute | solution.py:387
  91.4 1.9 %mesh_collect.1 = (f32[512,512]{1,0:T(8,128)}, f32[512,512]{1,0:T(8,128)}, f32[512,512]{1,0:T(8,128)}) custom-call(f32[512,512]{1,0:T(8,128)} %get-tuple-element.78.refs_0_, bf16[768,512]{1,0:T(8,128)(2,1)S(1)} %mesh_join.3.refs_0_.refs_1_, bf16[768,512]{1,0:T(8,128)(2,1)S(1)} %collective-permute-done.24.refs_2_), custom_call_target="tpu_custom_call" | custom-call | flops 10000000000 | bytes 1 | tf_op jit(solution)/shard_map/mesh_collect/pallas_call | solution.py:129
  (57 shorter events, 14.1 us)
Async XLA Ops:
  2.7 15.3 %all-to-all-start = ((bf16[16,8,474]{2,1,0:T(8,128)(2,1)}), bf16[16,8,474]{2,1,0:T(8,128)(2,1)S(1)}, u32[]{:S(2)}, u32[]{:S(2)}) async-start(bf16[16,8,474]{2,1,0:T(8,128)(2,1)} %bitcast.8), calls=%async_computation | async-start | bytes 262144 | tf_op jit(solution)/shard_map/all_to_all | solution.py:445
  20.6 6.5 %collective-permute-start = (bf16[64,512]{1,0:T(8,128)(2,1)S(1)}, bf16[64,512]{1,0:T(8,128)(2,1)S(1)}, u32[]{:S(2)}, u32[]{:S(2)}) collective-permute-start(bf16[64,512]{1,0:T(8,128)(2,1)S(1)} %get-tuple-element.111), channel_id=1, source_target_pairs={{1,2},{3,4},{5,6},{7,8},{9,10},{11,12},{13,14},{15,0},{2,1},{4,3},... | collective-permute-start | bytes 196616 | tf_op jit(solution)/shard_map/ppermute | solution.py:422
  21.3 5.7 %collective-permute-start.1 = (bf16[64,512]{1,0:T(8,128)(2,1)S(1)}, bf16[64,512]{1,0:T(8,128)(2,1)S(1)}, u32[]{:S(2)}, u32[]{:S(2)}) collective-permute-start(bf16[64,512]{1,0:T(8,128)(2,1)S(1)} %get-tuple-element.112), channel_id=1, source_target_pairs={{0,1},{2,3},{4,5},{6,7},{8,9},{10,11},{12,13},{14,15},{1,0},{3,2},... | collective-permute-start | bytes 196616 | tf_op jit(solution)/shard_map/ppermute | solution.py:422
  30.2 6.6 %collective-permute-start.3 = (bf16[64,512]{1,0:T(8,128)(2,1)S(1)}, bf16[64,512]{1,0:T(8,128)(2,1)S(1)}, u32[]{:S(2)}, u32[]{:S(2)}) collective-permute-start(bf16[64,512]{1,0:T(8,128)(2,1)S(1)} %get-tuple-element.123), channel_id=1, source_target_pairs={{1,2},{3,4},{5,6},{7,8},{9,10},{11,12},{13,14},{15,0},{2,1},{4,3},... | collective-permute-start | bytes 196616 | tf_op jit(solution)/shard_map/ppermute | solution.py:422
  30.9 5.8 %collective-permute-start.4 = (bf16[64,512]{1,0:T(8,128)(2,1)S(1)}, bf16[64,512]{1,0:T(8,128)(2,1)S(1)}, u32[]{:S(2)}, u32[]{:S(2)}) collective-permute-start(bf16[64,512]{1,0:T(8,128)(2,1)S(1)} %get-tuple-element.124), channel_id=1, source_target_pairs={{0,1},{2,3},{4,5},{6,7},{8,9},{10,11},{12,13},{14,15},{1,0},{3,2},... | collective-permute-start | bytes 196616 | tf_op jit(solution)/shard_map/ppermute | solution.py:422
  32.2 9.2 %collective-permute-start.6 = (bf16[256,512]{1,0:T(8,128)(2,1)S(1)}, bf16[256,512]{1,0:T(8,128)(2,1)S(1)}, u32[]{:S(2)}, u32[]{:S(2)}) collective-permute-start(bf16[256,512]{1,0:T(8,128)(2,1)S(1)} %get-tuple-element.142), channel_id=1, source_target_pairs={{0,2},{1,3},{2,0},{3,1},{4,6},{5,7},{6,4},{7,5},{8,10},{9,11},{10,... | collective-permute-start | bytes 786440 | tf_op jit(solution)/shard_map/ppermute | solution.py:387
  38.3 3.0 %collective-permute-start.5 = (bf16[768,512]{1,0:T(8,128)(2,1)S(1)}, bf16[768,512]{1,0:T(8,128)(2,1)S(1)}, u32[]{:S(2)}, u32[]{:S(2)}) collective-permute-start(bf16[768,512]{1,0:T(8,128)(2,1)S(1)} %get-tuple-element.140), channel_id=1, source_target_pairs={{0,1},{1,0},{2,3},{3,2},{4,5},{5,4},{6,7},{7,6},{8,9},{9,8},{10,11... | collective-permute-start | bytes 2359304 | tf_op jit(solution)/shard_map/ppermute | solution.py:387
  40.7 2.1 %collective-permute-start.7 = (bf16[512,512]{1,0:T(8,128)(2,1)S(1)}, bf16[512,512]{1,0:T(8,128)(2,1)S(1)}, u32[]{:S(2)}, u32[]{:S(2)}) collective-permute-start(bf16[512,512]{1,0:T(8,128)(2,1)S(1)} %get-tuple-element.144), channel_id=1, source_target_pairs={{0,1},{1,0},{2,3},{3,2},{4,5},{5,4},{6,7},{7,6},{8,9},{9,8},{10,11... | collective-permute-start | bytes 1572872 | tf_op jit(solution)/shard_map/ppermute | solution.py:387
  41.5 6.4 %collective-permute-start.8 = (bf16[128,512]{1,0:T(8,128)(2,1)S(1)}, bf16[128,512]{1,0:T(8,128)(2,1)S(1)}, u32[]{:S(2)}, u32[]{:S(2)}) collective-permute-start(bf16[128,512]{1,0:T(8,128)(2,1)S(1)} %get-tuple-element.146), channel_id=1, source_target_pairs={{0,4},{1,5},{2,6},{3,7},{4,0},{5,1},{6,2},{7,3},{8,12},{9,13},{10,... | collective-permute-start | bytes 393224 | tf_op jit(solution)/shard_map/ppermute | solution.py:387
  41.6 11.1 %collective-permute-start.9 = (bf16[384,512]{1,0:T(8,128)(2,1)S(1)}, bf16[384,512]{1,0:T(8,128)(2,1)S(1)}, u32[]{:S(2)}, u32[]{:S(2)}) collective-permute-start(bf16[384,512]{1,0:T(8,128)(2,1)S(1)} %get-tuple-element.147), channel_id=1, source_target_pairs={{0,2},{1,3},{2,0},{3,1},{4,6},{5,7},{6,4},{7,5},{8,10},{9,11},{10,... | collective-permute-start | bytes 1179656 | tf_op jit(solution)/shard_map/ppermute | solution.py:387
  42.9 11.6 %collective-permute-start.10 = (bf16[256,512]{1,0:T(8,128)(2,1)S(1)}, bf16[256,512]{1,0:T(8,128)(2,1)S(1)}, u32[]{:S(2)}, u32[]{:S(2)}) collective-permute-start(bf16[256,512]{1,0:T(8,128)(2,1)S(1)} %get-tuple-element.149), channel_id=1, source_target_pairs={{0,4},{1,5},{2,6},{3,7},{4,0},{5,1},{6,2},{7,3},{8,12},{9,13},{10,... | collective-permute-start | bytes 786440 | tf_op jit(solution)/shard_map/ppermute | solution.py:387
  48.0 11.8 %collective-permute-start.12 = (bf16[128,512]{1,0:T(8,128)(2,1)S(1)}, bf16[128,512]{1,0:T(8,128)(2,1)S(1)}, u32[]{:S(2)}, u32[]{:S(2)}) collective-permute-start(bf16[128,512]{1,0:T(8,128)(2,1)S(1)} %process_add.6.refs_0_.refs_1_), channel_id=1, source_target_pairs={{0,8},{1,9},{2,10},{3,11},{4,12},{5,13},{6,14},{7,15},{8,0},{9,1},... | collective-permute-start | bytes 393224 | tf_op jit(solution)/shard_map/ppermute | solution.py:387
  52.8 6.8 %collective-permute-start.11 = (bf16[192,512]{1,0:T(8,128)(2,1)S(1)}, bf16[192,512]{1,0:T(8,128)(2,1)S(1)}, u32[]{:S(2)}, u32[]{:S(2)}) collective-permute-start(bf16[192,512]{1,0:T(8,128)(2,1)S(1)} %get-tuple-element.151), channel_id=1, source_target_pairs={{0,4},{1,5},{2,6},{3,7},{4,0},{5,1},{6,2},{7,3},{8,12},{9,13},{10,... | collective-permute-start | bytes 589832 | tf_op jit(solution)/shard_map/ppermute | solution.py:387
  54.7 6.2 %collective-permute-start.13 = (bf16[128,512]{1,0:T(8,128)(2,1)S(1)}, bf16[128,512]{1,0:T(8,128)(2,1)S(1)}, u32[]{:S(2)}, u32[]{:S(2)}) collective-permute-start(bf16[128,512]{1,0:T(8,128)(2,1)S(1)} %get-tuple-element.152), channel_id=1, source_target_pairs={{0,2},{1,3},{2,0},{3,1},{4,6},{5,7},{6,4},{7,5},{8,10},{9,11},{10,... | collective-permute-start | bytes 393224 | tf_op jit(solution)/shard_map/ppermute | solution.py:387
  59.7 13.7 %collective-permute-start.15 = (bf16[192,512]{1,0:T(8,128)(2,1)S(1)}, bf16[192,512]{1,0:T(8,128)(2,1)S(1)}, u32[]{:S(2)}, u32[]{:S(2)}) collective-permute-start(bf16[192,512]{1,0:T(8,128)(2,1)S(1)} %mesh_add.6.refs_0_.refs_1_), channel_id=1, source_target_pairs={{0,8},{1,9},{2,10},{3,11},{4,12},{5,13},{6,14},{7,15},{8,0},{9,1},... | collective-permute-start | bytes 589832 | tf_op jit(solution)/shard_map/ppermute | solution.py:387
  59.9 7.8 %collective-permute-start.14 = (bf16[128,512]{1,0:T(8,128)(2,1)S(1)}, bf16[128,512]{1,0:T(8,128)(2,1)S(1)}, u32[]{:S(2)}, u32[]{:S(2)}) collective-permute-start(bf16[128,512]{1,0:T(8,128)(2,1)S(1)} %process_add.7.refs_0_.refs_1_), channel_id=1, source_target_pairs={{0,4},{1,5},{2,6},{3,7},{4,0},{5,1},{6,2},{7,3},{8,12},{9,13},{10,... | collective-permute-start | bytes 393224 | tf_op jit(solution)/shard_map/ppermute | solution.py:387
  60.9 14.5 %collective-permute-start.16 = (bf16[128,512]{1,0:T(8,128)(2,1)S(1)}, bf16[128,512]{1,0:T(8,128)(2,1)S(1)}, u32[]{:S(2)}, u32[]{:S(2)}) collective-permute-start(bf16[128,512]{1,0:T(8,128)(2,1)S(1)} %grid_add.6.refs_0_.refs_1_), channel_id=1, source_target_pairs={{0,8},{1,9},{2,10},{3,11},{4,12},{5,13},{6,14},{7,15},{8,0},{9,1},... | collective-permute-start | bytes 393224 | tf_op jit(solution)/shard_map/ppermute | solution.py:387
  67.8 8.2 %collective-permute-start.17 = (bf16[256,512]{1,0:T(8,128)(2,1)S(1)}, bf16[256,512]{1,0:T(8,128)(2,1)S(1)}, u32[]{:S(2)}, u32[]{:S(2)}) collective-permute-start(bf16[256,512]{1,0:T(8,128)(2,1)S(1)} %process_join.2.refs_0_.refs_1_), channel_id=1, source_target_pairs={{0,2},{1,3},{2,0},{3,1},{4,6},{5,7},{6,4},{7,5},{8,10},{9,11},{10,... | collective-permute-start | bytes 786440 | tf_op jit(solution)/shard_map/ppermute | solution.py:387
  73.5 6.0 %collective-permute-start.18 = (bf16[192,512]{1,0:T(8,128)(2,1)S(1)}, bf16[192,512]{1,0:T(8,128)(2,1)S(1)}, u32[]{:S(2)}, u32[]{:S(2)}) collective-permute-start(bf16[192,512]{1,0:T(8,128)(2,1)S(1)} %mesh_add.7.refs_0_.refs_1_), channel_id=1, source_target_pairs={{0,4},{1,5},{2,6},{3,7},{4,0},{5,1},{6,2},{7,3},{8,12},{9,13},{10,... | collective-permute-start | bytes 589832 | tf_op jit(solution)/shard_map/ppermute | solution.py:387
  75.5 5.0 %collective-permute-start.19 = (bf16[128,512]{1,0:T(8,128)(2,1)S(1)}, bf16[128,512]{1,0:T(8,128)(2,1)S(1)}, u32[]{:S(2)}, u32[]{:S(2)}) collective-permute-start(bf16[128,512]{1,0:T(8,128)(2,1)S(1)} %grid_add.7.refs_0_.refs_1_), channel_id=1, source_target_pairs={{0,2},{1,3},{2,0},{3,1},{4,6},{5,7},{6,4},{7,5},{8,10},{9,11},{10,... | collective-permute-start | bytes 393224 | tf_op jit(solution)/shard_map/ppermute | solution.py:387
  76.0 5.3 %collective-permute-start.20 = (bf16[512,512]{1,0:T(8,128)(2,1)S(1)}, bf16[512,512]{1,0:T(8,128)(2,1)S(1)}, u32[]{:S(2)}, u32[]{:S(2)}) collective-permute-start(bf16[512,512]{1,0:T(8,128)(2,1)S(1)} %process_join.3.refs_0_.refs_1_), channel_id=1, source_target_pairs={{0,1},{1,0},{2,3},{3,2},{4,5},{5,4},{6,7},{7,6},{8,9},{9,8},{10,11... | collective-permute-start | bytes 1572872 | tf_op jit(solution)/shard_map/ppermute | solution.py:387
  79.6 9.3 %collective-permute-start.22 = (bf16[384,512]{1,0:T(8,128)(2,1)S(1)}, bf16[384,512]{1,0:T(8,128)(2,1)S(1)}, u32[]{:S(2)}, u32[]{:S(2)}) collective-permute-start(bf16[384,512]{1,0:T(8,128)(2,1)S(1)} %mesh_join.2.refs_0_.refs_1_), channel_id=1, source_target_pairs={{0,2},{1,3},{2,0},{3,1},{4,6},{5,7},{6,4},{7,5},{8,10},{9,11},{10,... | collective-permute-start | bytes 1179656 | tf_op jit(solution)/shard_map/ppermute | solution.py:387
  80.6 6.5 %collective-permute-start.21 = (bf16[256,512]{1,0:T(8,128)(2,1)S(1)}, bf16[256,512]{1,0:T(8,128)(2,1)S(1)}, u32[]{:S(2)}, u32[]{:S(2)}) collective-permute-start(bf16[256,512]{1,0:T(8,128)(2,1)S(1)} %grid_join.2.refs_0_.refs_1_), channel_id=1, source_target_pairs={{0,4},{1,5},{2,6},{3,7},{4,0},{5,1},{6,2},{7,3},{8,12},{9,13},{10,... | collective-permute-start | bytes 786440 | tf_op jit(solution)/shard_map/ppermute | solution.py:387
  89.1 2.4 %collective-permute-start.24 = (bf16[768,512]{1,0:T(8,128)(2,1)S(1)}, bf16[768,512]{1,0:T(8,128)(2,1)S(1)}, u32[]{:S(2)}, u32[]{:S(2)}) collective-permute-start(bf16[768,512]{1,0:T(8,128)(2,1)S(1)} %mesh_join.3.refs_0_.refs_1_), channel_id=1, source_target_pairs={{0,1},{1,0},{2,3},{3,2},{4,5},{5,4},{6,7},{7,6},{8,9},{9,8},{10,11... | collective-permute-start | bytes 2359304 | tf_op jit(solution)/shard_map/ppermute | solution.py:387
  (2 other events, 4.0 us)

commit v7 on v6

--- a/solution.py
+++ b/solution.py
@@ -168,7 +168,7 @@
     lat.set(one)
     slope.set(two)
     rows.set(dot(onehot[...], three))
-    recv.set(dot(latent()[...], wrecv()[...]))
+    recv.set(0.5 * dot(latent()[...], wrecv()[...]))
 
 
 def fill_onehot(onehot, slots):
@@ -176,7 +176,7 @@
     wide = onehot.shape[1]
     lanes = lax.broadcasted_iota(jnp.int32, (m, wide), 1)
     for f in range(fan):
-        onehot[f * m : (f + 1) * m, :] = jnp.where(slots[:, f : f + 1] == lanes, 1.0, 0.0).astype(BF)
+        onehot[f * m : (f + 1) * m, :] = jnp.where(slots[:, f : f + 1] == lanes, 0.5, 0.0).astype(BF)
 
 
 def fill_onehot_t(onehot, slots_t):
@@ -193,11 +193,13 @@
     total = None
     for f in range(fan):
         at = slice(f * m, (f + 1) * m)
-        v = rows[at, :] + recv
-        s = sigmoid(v)
+        h = rows[at, :] + recv
+        t = jnp.tanh(h)
+        q = 1.0 + t
+        p = h * q
         k = mask[:, f : f + 1].astype(F32)
-        slope[at, :] = (silu_slope(v, s) * k).astype(slope.dtype)
-        part = v * s * k
+        slope[at, :] = ((q + p * (1.0 - t)) * (0.5 * k)).astype(slope.dtype)
+        part = p * k
         total = part if total is None else total + part
     return total.astype(BF)
 
@@ -379,7 +381,7 @@
     fill_onehot(onehot.held, slots.T)
     fill_onehot_t(onehot_t.held, slots)
     fill_onehot_t(enc_onehot_t.held, enc_slots_t()[...])
-    recv.set(dot(mid()[...], wrecv()[...]))
+    recv.set(0.5 * dot(mid()[...], wrecv()[...]))
 
 
 def exchange(value, step):

time: 93.7 us -> 93.3 us (level)
  no operation moved by 1% of the time
where the time goes in v7:
time: 93.3 us; the launch traced here: 92.9 us
  waiting for transfers between devices  50.3 us (54%)
  Pallas kernels  22.7 us (24%)
  starting transfers between devices  18.9 us (20%)
  between operations  0.98 us (1%)
    ppermute x21, waiting for transfers between devices, exchange(): return lax.ppermute(value, 'space', [(i, i ^ step) for i in range(n)])  38 us
    pallas_call x29, Pallas kernels, call(): pl.pallas_call(kernel, name=name, out_shape=[(pltpu.HBM if far else pltpu...  22.7 us
    ppermute x21, starting transfers between devices, exchange(): return lax.ppermute(value, 'space', [(i, i ^ step) for i in range(n)])  9.9 us
    ppermute x4, waiting for transfers between devices, swapped(): return lax.ppermute(rows, 'space', [*pairs, *((b, a) for a, b in pairs)])  7.67 us
    all_to_all x1, starting transfers between devices, local(): lax.all_to_all(outgoing.reshape(n, -1, fin), 'space', split_axis=0, conca...  7.4 us
    all_to_all x1, waiting for transfers between devices, local(): lax.all_to_all(outgoing.reshape(n, -1, fin), 'space', split_axis=0, conca...  4.69 us
  transfers between devices with their start and end apart: 26, of which 16 were waited for; matrix products, arithmetic and copies ran while one was open for 0% of the time, Pallas kernels for 15%

profile of v7, /device:TPU:0, one launch (start us, length us, event | category | flops | bytes accessed | tf_op | source)
XLA Modules:
  0.0 92.9 jit_solution(14884941589585135696)
XLA Ops:
  0.6 2.0 %pick.1 = bf16[128,474]{1,0:T(8,128)(2,1)} custom-call(s32[8,16]{1,0:T(8,128)} %bitcast.20, bf16[474,512]{1,0:T(8,128)(2,1)} %bitcast.13), custom_call_target="tpu_custom_call" | custom-call | flops 1 | bytes 1 | tf_op jit(solution)/shard_map/pick/pallas_call | solution.py:129
  2.7 7.4 %all-to-all-start = ((bf16[16,8,474]{2,1,0:T(8,128)(2,1)}), bf16[16,8,474]{2,1,0:T(8,128)(2,1)S(1)}, u32[]{:S(2)}, u32[]{:S(2)}) async-start(bf16[16,8,474]{2,1,0:T(8,128)(2,1)} %bitcast.8), calls=%async_computation | async-start | bytes 262144 | tf_op jit(solution)/shard_map/all_to_all | solution.py:447
  10.1 3.2 %embed.1 = (bf16[512,512]{1,0:T(8,128)(2,1)}, bf16[512,512]{1,0:T(8,128)(2,1)}, bf16[1024,512]{1,0:T(8,128)(2,1)S(1)}, f32[64,512]{1,0:T(8,128)S(1)}, s32[16,64]...) custom-call(s32[16,64]{1,0:T(8,128)} %bitcast.16, ...), custom_call_target="tpu_custom_call" | custom-call | flops 1 | bytes 1 | tf_op jit(solution)/shard_map/embed/pallas_call | solution.py:129
  13.3 4.7 %all-to-all-done = bf16[16,8,474]{2,1,0:T(8,128)(2,1)S(1)} async-done(((bf16[16,8,474]{2,1,0:T(8,128)(2,1)}), bf16[16,8,474]{2,1,0:T(8,128)(2,1)S(1)}, u32[]{:S(2)}, u32[]{:S(2)}) %all-to-all-start) | async-done | bytes 121376 | tf_op jit(solution)/shard_map/all_to_all | solution.py:447
  18.0 2.3 %encode.1 = (bf16[64,512]{1,0:T(8,128)(2,1)S(1)}, bf16[64,512]{1,0:T(8,128)(2,1)S(1)}, bf16[64,512]{1,0:T(8,128)(2,1)S(1)}, bf16[64,512]{1,0:T(8,128)(2,1)S(1)},...) custom-call(s32[16,64]{1,0:T(8,128)S(1)} %get-tuple-element.86.refs_, ...), custom_call_target="tpu_custom_call" | custom-call | flops 1 | bytes 1 | tf_op jit(solution)/shard_map/encode/pallas_call | solution.py:129
  21.1 2.2 %load.1 = (bf16[1024,192]{1,0:T(8,128)(2,1)S(1)}, bf16[192,1024]{1,0:T(8,128)(2,1)S(1)}, bf16[640,1024]{1,0:T(8,128)(2,1)S(1)}, f32[64,512]{1,0:T(8,128)S(1)}, b...) custom-call(s32[16,64]{1,0:T(8,128)} %bitcast.18, ...), custom_call_target="tpu_custom_call" | custom-call | flops 1 | bytes 1 | tf_op jit(solution)/shard_map/load/pallas_call | solution.py:129
  23.3 3.5 %collective-permute-done.refs_5_ = bf16[64,512]{1,0:T(8,128)(2,1)S(1)} collective-permute-done((bf16[64,512]{1,0:T(8,128)(2,1)S(1)}, bf16[64,512]{1,0:T(8,128)(2,1)S(1)}, u32[]{:S(2)}, u32[]{:S(2)}) %collective-permute-start) | collective-permute-done | bytes 65568 | tf_op jit(solution)/shard_map/ppermute | solution.py:424
  26.8 2.3 %process.1 = (bf16[64,512]{1,0:T(8,128)(2,1)}, bf16[64,512]{1,0:T(8,128)(2,1)S(1)}, bf16[64,512]{1,0:T(8,128)(2,1)S(1)}, f32[64,512]{1,0:T(8,128)S(1)}, f32[64,5...) custom-call(bf16[1024,192]{1,0:T(8,128)(2,1)S(1)} %get-tuple-element.106, ...), custom_call_target="tpu_custom_call" | custom-call | flops 1 | bytes 1 | tf_op jit(solution)/shard_map/process/pallas_call | solution.py:129
  32.2 4.2 %collective-permute-done.3.refs_1_ = bf16[64,512]{1,0:T(8,128)(2,1)S(1)} collective-permute-done((bf16[64,512]{1,0:T(8,128)(2,1)S(1)}, bf16[64,512]{1,0:T(8,128)(2,1)S(1)}, u32[]{:S(2)}, u32[]{:S(2)}) %collective-permute-start.3) | collective-permute-done | bytes 65568 | tf_op jit(solution)/shard_map/ppermute | solution.py:424
  36.4 1.5 %mesh_grads.1 = (f32[768,512]{1,0:T(8,128)S(1)}, bf16[768,512]{1,0:T(8,128)(2,1)S(1)}, bf16[1024,512]{1,0:T(8,128)(2,1)S(1)}) custom-call(f32[256,512]{1,0:T(8,128)S(1)} %get-tuple-element.122.refs_0_.refs_1_, bf16[64,512]{1,0:T(8,128)(2,1)S(1)} %collective-permute-done.3.refs_1_, bf16[64,512]{1,0:T(8,128)(2,1)S(1)} %collective-permute-done.4.refs_2_, ...), custom_call_target="tpu_custom_call" | custom-call | flops 10000000000 | bytes 1 | tf_op jit(solution)/shard_map/mesh_grads/pallas_call | solution.py:129
  38.0 2.4 %grid_grads.1 = (f32[512,512]{1,0:T(8,128)S(1)}, bf16[512,512]{1,0:T(8,128)(2,1)S(1)}) custom-call(f32[768,512]{1,0:T(8,128)S(1)} %get-tuple-element.131.refs_0_.refs_1_, bf16[640,1024]{1,0:T(8,128)(2,1)S(1)} %get-tuple-element.132.refs_1_, bf16[1024,512]{1,0:T(8,128)(2,1)S(1)} %get-tuple-element.133.refs_2_, ...), custom_call_target="tpu_custom_call" | custom-call | flops 10000000000 | bytes 1 | tf_op jit(solution)/shard_map/grid_grads/pallas_call | solution.py:129
  43.5 4.1 %collective-permute-done.8.refs_2_ = bf16[128,512]{1,0:T(8,128)(2,1)S(1)} collective-permute-done((bf16[128,512]{1,0:T(8,128)(2,1)S(1)}, bf16[128,512]{1,0:T(8,128)(2,1)S(1)}, u32[]{:S(2)}, u32[]{:S(2)}) %collective-permute-start.8) | collective-permute-done | bytes 131104 | tf_op jit(solution)/shard_map/ppermute | solution.py:389
  47.7 4.6 %collective-permute-done.9.refs_2_ = bf16[384,512]{1,0:T(8,128)(2,1)S(1)} collective-permute-done((bf16[384,512]{1,0:T(8,128)(2,1)S(1)}, bf16[384,512]{1,0:T(8,128)(2,1)S(1)}, u32[]{:S(2)}, u32[]{:S(2)}) %collective-permute-start.9) | collective-permute-done | bytes 393248 | tf_op jit(solution)/shard_map/ppermute | solution.py:389
  52.5 1.7 %collective-permute-start.11 = (bf16[192,512]{1,0:T(8,128)(2,1)S(1)}, bf16[192,512]{1,0:T(8,128)(2,1)S(1)}, u32[]{:S(2)}, u32[]{:S(2)}) collective-permute-start(bf16[192,512]{1,0:T(8,128)(2,1)S(1)} %get-tuple-element.151), channel_id=1, source_target_pairs={{0,4},{1,5},{2,6},{3,7},{4,0},{5,1},{6,2},{7,3},{8,12},{9,13},{10,... | collective-permute-start | bytes 589832 | tf_op jit(solution)/shard_map/ppermute | solution.py:389
  54.8 4.5 %collective-permute-done.11.refs_2_ = bf16[192,512]{1,0:T(8,128)(2,1)S(1)} collective-permute-done((bf16[192,512]{1,0:T(8,128)(2,1)S(1)}, bf16[192,512]{1,0:T(8,128)(2,1)S(1)}, u32[]{:S(2)}, u32[]{:S(2)}) %collective-permute-start.11) | collective-permute-done | bytes 196640 | tf_op jit(solution)/shard_map/ppermute | solution.py:389
  60.6 2.6 %collective-permute-start.16 = (bf16[128,512]{1,0:T(8,128)(2,1)S(1)}, bf16[128,512]{1,0:T(8,128)(2,1)S(1)}, u32[]{:S(2)}, u32[]{:S(2)}) collective-permute-start(bf16[128,512]{1,0:T(8,128)(2,1)S(1)} %grid_add.6.refs_0_.refs_1_), channel_id=1, source_target_pairs={{0,8},{1,9},{2,10},{3,11},{4,12},{5,13},{6,14},{7,15},{8,0},{9,1},... | collective-permute-start | bytes 393224 | tf_op jit(solution)/shard_map/ppermute | solution.py:389
  63.2 4.1 %collective-permute-done.14.refs_2_ = bf16[128,512]{1,0:T(8,128)(2,1)S(1)} collective-permute-done((bf16[128,512]{1,0:T(8,128)(2,1)S(1)}, bf16[128,512]{1,0:T(8,128)(2,1)S(1)}, u32[]{:S(2)}, u32[]{:S(2)}) %collective-permute-start.14) | collective-permute-done | bytes 131104 | tf_op jit(solution)/shard_map/ppermute | solution.py:389
  67.5 5.6 %collective-permute-done.15.refs_2_ = bf16[192,512]{1,0:T(8,128)(2,1)S(1)} collective-permute-done((bf16[192,512]{1,0:T(8,128)(2,1)S(1)}, bf16[192,512]{1,0:T(8,128)(2,1)S(1)}, u32[]{:S(2)}, u32[]{:S(2)}) %collective-permute-start.15) | collective-permute-done | bytes 196640 | tf_op jit(solution)/shard_map/ppermute | solution.py:389
  73.3 1.8 %collective-permute-done.16.refs_2_ = bf16[128,512]{1,0:T(8,128)(2,1)S(1)} collective-permute-done((bf16[128,512]{1,0:T(8,128)(2,1)S(1)}, bf16[128,512]{1,0:T(8,128)(2,1)S(1)}, u32[]{:S(2)}, u32[]{:S(2)}) %collective-permute-start.16) | collective-permute-done | bytes 131104 | tf_op jit(solution)/shard_map/ppermute | solution.py:389
  75.7 3.5 %collective-permute-done.18.refs_2_ = bf16[192,512]{1,0:T(8,128)(2,1)S(1)} collective-permute-done((bf16[192,512]{1,0:T(8,128)(2,1)S(1)}, bf16[192,512]{1,0:T(8,128)(2,1)S(1)}, u32[]{:S(2)}, u32[]{:S(2)}) %collective-permute-start.18) | collective-permute-done | bytes 196640 | tf_op jit(solution)/shard_map/ppermute | solution.py:389
  81.0 1.5 %process_collect.1 = (f32[512,512]{1,0:T(8,128)}, f32[512,512]{1,0:T(8,128)}) custom-call(bf16[256,512]{1,0:T(8,128)(2,1)S(1)} %grid_join.2.refs_0_.refs_1_, bf16[512,512]{1,0:T(8,128)(2,1)S(1)} %process_join.3.refs_0_.refs_1_, bf16[512,512]{1,0:T(8,128)(2,1)S(1)} %collective-permute-done.20.refs_2_), custom_call_target="tpu_custom_call" | custom-call | flops 10000000000 | bytes 1 | tf_op jit(solution)/shard_map/process_collect/pallas_call | solution.py:129
  82.4 4.3 %collective-permute-done.21.refs_2_ = bf16[256,512]{1,0:T(8,128)(2,1)S(1)} collective-permute-done((bf16[256,512]{1,0:T(8,128)(2,1)S(1)}, bf16[256,512]{1,0:T(8,128)(2,1)S(1)}, u32[]{:S(2)}, u32[]{:S(2)}) %collective-permute-start.21) | collective-permute-done | bytes 262176 | tf_op jit(solution)/shard_map/ppermute | solution.py:389
  86.9 1.7 %collective-permute-done.22.refs_2_ = bf16[384,512]{1,0:T(8,128)(2,1)S(1)} collective-permute-done((bf16[384,512]{1,0:T(8,128)(2,1)S(1)}, bf16[384,512]{1,0:T(8,128)(2,1)S(1)}, u32[]{:S(2)}, u32[]{:S(2)}) %collective-permute-start.22) | collective-permute-done | bytes 393248 | tf_op jit(solution)/shard_map/ppermute | solution.py:389
  91.1 1.9 %mesh_collect.1 = (f32[512,512]{1,0:T(8,128)}, f32[512,512]{1,0:T(8,128)}, f32[512,512]{1,0:T(8,128)}) custom-call(f32[512,512]{1,0:T(8,128)} %get-tuple-element.78.refs_0_, bf16[768,512]{1,0:T(8,128)(2,1)S(1)} %mesh_join.3.refs_0_.refs_1_, bf16[768,512]{1,0:T(8,128)(2,1)S(1)} %collective-permute-done.24.refs_2_), custom_call_target="tpu_custom_call" | custom-call | flops 10000000000 | bytes 1 | tf_op jit(solution)/shard_map/mesh_collect/pallas_call | solution.py:129
  (57 shorter events, 14.1 us)
Async XLA Ops:
  2.7 15.3 %all-to-all-start = ((bf16[16,8,474]{2,1,0:T(8,128)(2,1)}), bf16[16,8,474]{2,1,0:T(8,128)(2,1)S(1)}, u32[]{:S(2)}, u32[]{:S(2)}) async-start(bf16[16,8,474]{2,1,0:T(8,128)(2,1)} %bitcast.8), calls=%async_computation | async-start | bytes 262144 | tf_op jit(solution)/shard_map/all_to_all | solution.py:447
  20.3 6.5 %collective-permute-start = (bf16[64,512]{1,0:T(8,128)(2,1)S(1)}, bf16[64,512]{1,0:T(8,128)(2,1)S(1)}, u32[]{:S(2)}, u32[]{:S(2)}) collective-permute-start(bf16[64,512]{1,0:T(8,128)(2,1)S(1)} %get-tuple-element.111), channel_id=1, source_target_pairs={{1,2},{3,4},{5,6},{7,8},{9,10},{11,12},{13,14},{15,0},{2,1},{4,3},... | collective-permute-start | bytes 196616 | tf_op jit(solution)/shard_map/ppermute | solution.py:424
  21.1 5.7 %collective-permute-start.1 = (bf16[64,512]{1,0:T(8,128)(2,1)S(1)}, bf16[64,512]{1,0:T(8,128)(2,1)S(1)}, u32[]{:S(2)}, u32[]{:S(2)}) collective-permute-start(bf16[64,512]{1,0:T(8,128)(2,1)S(1)} %get-tuple-element.112), channel_id=1, source_target_pairs={{0,1},{2,3},{4,5},{6,7},{8,9},{10,11},{12,13},{14,15},{1,0},{3,2},... | collective-permute-start | bytes 196616 | tf_op jit(solution)/shard_map/ppermute | solution.py:424
  29.8 6.6 %collective-permute-start.3 = (bf16[64,512]{1,0:T(8,128)(2,1)S(1)}, bf16[64,512]{1,0:T(8,128)(2,1)S(1)}, u32[]{:S(2)}, u32[]{:S(2)}) collective-permute-start(bf16[64,512]{1,0:T(8,128)(2,1)S(1)} %get-tuple-element.123), channel_id=1, source_target_pairs={{1,2},{3,4},{5,6},{7,8},{9,10},{11,12},{13,14},{15,0},{2,1},{4,3},... | collective-permute-start | bytes 196616 | tf_op jit(solution)/shard_map/ppermute | solution.py:424
  30.6 5.8 %collective-permute-start.4 = (bf16[64,512]{1,0:T(8,128)(2,1)S(1)}, bf16[64,512]{1,0:T(8,128)(2,1)S(1)}, u32[]{:S(2)}, u32[]{:S(2)}) collective-permute-start(bf16[64,512]{1,0:T(8,128)(2,1)S(1)} %get-tuple-element.124), channel_id=1, source_target_pairs={{0,1},{2,3},{4,5},{6,7},{8,9},{10,11},{12,13},{14,15},{1,0},{3,2},... | collective-permute-start | bytes 196616 | tf_op jit(solution)/shard_map/ppermute | solution.py:424
  31.9 9.2 %collective-permute-start.6 = (bf16[256,512]{1,0:T(8,128)(2,1)S(1)}, bf16[256,512]{1,0:T(8,128)(2,1)S(1)}, u32[]{:S(2)}, u32[]{:S(2)}) collective-permute-start(bf16[256,512]{1,0:T(8,128)(2,1)S(1)} %get-tuple-element.142), channel_id=1, source_target_pairs={{0,2},{1,3},{2,0},{3,1},{4,6},{5,7},{6,4},{7,5},{8,10},{9,11},{10,... | collective-permute-start | bytes 786440 | tf_op jit(solution)/shard_map/ppermute | solution.py:389
  37.9 3.0 %collective-permute-start.5 = (bf16[768,512]{1,0:T(8,128)(2,1)S(1)}, bf16[768,512]{1,0:T(8,128)(2,1)S(1)}, u32[]{:S(2)}, u32[]{:S(2)}) collective-permute-start(bf16[768,512]{1,0:T(8,128)(2,1)S(1)} %get-tuple-element.140), channel_id=1, source_target_pairs={{0,1},{1,0},{2,3},{3,2},{4,5},{5,4},{6,7},{7,6},{8,9},{9,8},{10,11... | collective-permute-start | bytes 2359304 | tf_op jit(solution)/shard_map/ppermute | solution.py:389
  40.3 2.1 %collective-permute-start.7 = (bf16[512,512]{1,0:T(8,128)(2,1)S(1)}, bf16[512,512]{1,0:T(8,128)(2,1)S(1)}, u32[]{:S(2)}, u32[]{:S(2)}) collective-permute-start(bf16[512,512]{1,0:T(8,128)(2,1)S(1)} %get-tuple-element.144), channel_id=1, source_target_pairs={{0,1},{1,0},{2,3},{3,2},{4,5},{5,4},{6,7},{7,6},{8,9},{9,8},{10,11... | collective-permute-start | bytes 1572872 | tf_op jit(solution)/shard_map/ppermute | solution.py:389
  41.2 6.4 %collective-permute-start.8 = (bf16[128,512]{1,0:T(8,128)(2,1)S(1)}, bf16[128,512]{1,0:T(8,128)(2,1)S(1)}, u32[]{:S(2)}, u32[]{:S(2)}) collective-permute-start(bf16[128,512]{1,0:T(8,128)(2,1)S(1)} %get-tuple-element.146), channel_id=1, source_target_pairs={{0,4},{1,5},{2,6},{3,7},{4,0},{5,1},{6,2},{7,3},{8,12},{9,13},{10,... | collective-permute-start | bytes 393224 | tf_op jit(solution)/shard_map/ppermute | solution.py:389
  41.3 11.1 %collective-permute-start.9 = (bf16[384,512]{1,0:T(8,128)(2,1)S(1)}, bf16[384,512]{1,0:T(8,128)(2,1)S(1)}, u32[]{:S(2)}, u32[]{:S(2)}) collective-permute-start(bf16[384,512]{1,0:T(8,128)(2,1)S(1)} %get-tuple-element.147), channel_id=1, source_target_pairs={{0,2},{1,3},{2,0},{3,1},{4,6},{5,7},{6,4},{7,5},{8,10},{9,11},{10,... | collective-permute-start | bytes 1179656 | tf_op jit(solution)/shard_map/ppermute | solution.py:389
  42.6 11.6 %collective-permute-start.10 = (bf16[256,512]{1,0:T(8,128)(2,1)S(1)}, bf16[256,512]{1,0:T(8,128)(2,1)S(1)}, u32[]{:S(2)}, u32[]{:S(2)}) collective-permute-start(bf16[256,512]{1,0:T(8,128)(2,1)S(1)} %get-tuple-element.149), channel_id=1, source_target_pairs={{0,4},{1,5},{2,6},{3,7},{4,0},{5,1},{6,2},{7,3},{8,12},{9,13},{10,... | collective-permute-start | bytes 786440 | tf_op jit(solution)/shard_map/ppermute | solution.py:389
  47.7 11.8 %collective-permute-start.12 = (bf16[128,512]{1,0:T(8,128)(2,1)S(1)}, bf16[128,512]{1,0:T(8,128)(2,1)S(1)}, u32[]{:S(2)}, u32[]{:S(2)}) collective-permute-start(bf16[128,512]{1,0:T(8,128)(2,1)S(1)} %process_add.6.refs_0_.refs_1_), channel_id=1, source_target_pairs={{0,8},{1,9},{2,10},{3,11},{4,12},{5,13},{6,14},{7,15},{8,0},{9,1},... | collective-permute-start | bytes 393224 | tf_op jit(solution)/shard_map/ppermute | solution.py:389
  52.5 6.8 %collective-permute-start.11 = (bf16[192,512]{1,0:T(8,128)(2,1)S(1)}, bf16[192,512]{1,0:T(8,128)(2,1)S(1)}, u32[]{:S(2)}, u32[]{:S(2)}) collective-permute-start(bf16[192,512]{1,0:T(8,128)(2,1)S(1)} %get-tuple-element.151), channel_id=1, source_target_pairs={{0,4},{1,5},{2,6},{3,7},{4,0},{5,1},{6,2},{7,3},{8,12},{9,13},{10,... | collective-permute-start | bytes 589832 | tf_op jit(solution)/shard_map/ppermute | solution.py:389
  54.3 6.2 %collective-permute-start.13 = (bf16[128,512]{1,0:T(8,128)(2,1)S(1)}, bf16[128,512]{1,0:T(8,128)(2,1)S(1)}, u32[]{:S(2)}, u32[]{:S(2)}) collective-permute-start(bf16[128,512]{1,0:T(8,128)(2,1)S(1)} %get-tuple-element.152), channel_id=1, source_target_pairs={{0,2},{1,3},{2,0},{3,1},{4,6},{5,7},{6,4},{7,5},{8,10},{9,11},{10,... | collective-permute-start | bytes 393224 | tf_op jit(solution)/shard_map/ppermute | solution.py:389
  59.4 13.7 %collective-permute-start.15 = (bf16[192,512]{1,0:T(8,128)(2,1)S(1)}, bf16[192,512]{1,0:T(8,128)(2,1)S(1)}, u32[]{:S(2)}, u32[]{:S(2)}) collective-permute-start(bf16[192,512]{1,0:T(8,128)(2,1)S(1)} %mesh_add.6.refs_0_.refs_1_), channel_id=1, source_target_pairs={{0,8},{1,9},{2,10},{3,11},{4,12},{5,13},{6,14},{7,15},{8,0},{9,1},... | collective-permute-start | bytes 589832 | tf_op jit(solution)/shard_map/ppermute | solution.py:389
  59.5 7.8 %collective-permute-start.14 = (bf16[128,512]{1,0:T(8,128)(2,1)S(1)}, bf16[128,512]{1,0:T(8,128)(2,1)S(1)}, u32[]{:S(2)}, u32[]{:S(2)}) collective-permute-start(bf16[128,512]{1,0:T(8,128)(2,1)S(1)} %process_add.7.refs_0_.refs_1_), channel_id=1, source_target_pairs={{0,4},{1,5},{2,6},{3,7},{4,0},{5,1},{6,2},{7,3},{8,12},{9,13},{10,... | collective-permute-start | bytes 393224 | tf_op jit(solution)/shard_map/ppermute | solution.py:389
  60.6 14.5 %collective-permute-start.16 = (bf16[128,512]{1,0:T(8,128)(2,1)S(1)}, bf16[128,512]{1,0:T(8,128)(2,1)S(1)}, u32[]{:S(2)}, u32[]{:S(2)}) collective-permute-start(bf16[128,512]{1,0:T(8,128)(2,1)S(1)} %grid_add.6.refs_0_.refs_1_), channel_id=1, source_target_pairs={{0,8},{1,9},{2,10},{3,11},{4,12},{5,13},{6,14},{7,15},{8,0},{9,1},... | collective-permute-start | bytes 393224 | tf_op jit(solution)/shard_map/ppermute | solution.py:389
  67.4 8.2 %collective-permute-start.17 = (bf16[256,512]{1,0:T(8,128)(2,1)S(1)}, bf16[256,512]{1,0:T(8,128)(2,1)S(1)}, u32[]{:S(2)}, u32[]{:S(2)}) collective-permute-start(bf16[256,512]{1,0:T(8,128)(2,1)S(1)} %process_join.2.refs_0_.refs_1_), channel_id=1, source_target_pairs={{0,2},{1,3},{2,0},{3,1},{4,6},{5,7},{6,4},{7,5},{8,10},{9,11},{10,... | collective-permute-start | bytes 786440 | tf_op jit(solution)/shard_map/ppermute | solution.py:389
  73.2 6.0 %collective-permute-start.18 = (bf16[192,512]{1,0:T(8,128)(2,1)S(1)}, bf16[192,512]{1,0:T(8,128)(2,1)S(1)}, u32[]{:S(2)}, u32[]{:S(2)}) collective-permute-start(bf16[192,512]{1,0:T(8,128)(2,1)S(1)} %mesh_add.7.refs_0_.refs_1_), channel_id=1, source_target_pairs={{0,4},{1,5},{2,6},{3,7},{4,0},{5,1},{6,2},{7,3},{8,12},{9,13},{10,... | collective-permute-start | bytes 589832 | tf_op jit(solution)/shard_map/ppermute | solution.py:389
  75.2 5.0 %collective-permute-start.19 = (bf16[128,512]{1,0:T(8,128)(2,1)S(1)}, bf16[128,512]{1,0:T(8,128)(2,1)S(1)}, u32[]{:S(2)}, u32[]{:S(2)}) collective-permute-start(bf16[128,512]{1,0:T(8,128)(2,1)S(1)} %grid_add.7.refs_0_.refs_1_), channel_id=1, source_target_pairs={{0,2},{1,3},{2,0},{3,1},{4,6},{5,7},{6,4},{7,5},{8,10},{9,11},{10,... | collective-permute-start | bytes 393224 | tf_op jit(solution)/shard_map/ppermute | solution.py:389
  75.6 5.3 %collective-permute-start.20 = (bf16[512,512]{1,0:T(8,128)(2,1)S(1)}, bf16[512,512]{1,0:T(8,128)(2,1)S(1)}, u32[]{:S(2)}, u32[]{:S(2)}) collective-permute-start(bf16[512,512]{1,0:T(8,128)(2,1)S(1)} %process_join.3.refs_0_.refs_1_), channel_id=1, source_target_pairs={{0,1},{1,0},{2,3},{3,2},{4,5},{5,4},{6,7},{7,6},{8,9},{9,8},{10,11... | collective-permute-start | bytes 1572872 | tf_op jit(solution)/shard_map/ppermute | solution.py:389
  79.3 9.3 %collective-permute-start.22 = (bf16[384,512]{1,0:T(8,128)(2,1)S(1)}, bf16[384,512]{1,0:T(8,128)(2,1)S(1)}, u32[]{:S(2)}, u32[]{:S(2)}) collective-permute-start(bf16[384,512]{1,0:T(8,128)(2,1)S(1)} %mesh_join.2.refs_0_.refs_1_), channel_id=1, source_target_pairs={{0,2},{1,3},{2,0},{3,1},{4,6},{5,7},{6,4},{7,5},{8,10},{9,11},{10,... | collective-permute-start | bytes 1179656 | tf_op jit(solution)/shard_map/ppermute | solution.py:389
  80.2 6.5 %collective-permute-start.21 = (bf16[256,512]{1,0:T(8,128)(2,1)S(1)}, bf16[256,512]{1,0:T(8,128)(2,1)S(1)}, u32[]{:S(2)}, u32[]{:S(2)}) collective-permute-start(bf16[256,512]{1,0:T(8,128)(2,1)S(1)} %grid_join.2.refs_0_.refs_1_), channel_id=1, source_target_pairs={{0,4},{1,5},{2,6},{3,7},{4,0},{5,1},{6,2},{7,3},{8,12},{9,13},{10,... | collective-permute-start | bytes 786440 | tf_op jit(solution)/shard_map/ppermute | solution.py:389
  88.7 2.4 %collective-permute-start.24 = (bf16[768,512]{1,0:T(8,128)(2,1)S(1)}, bf16[768,512]{1,0:T(8,128)(2,1)S(1)}, u32[]{:S(2)}, u32[]{:S(2)}) collective-permute-start(bf16[768,512]{1,0:T(8,128)(2,1)S(1)} %mesh_join.3.refs_0_.refs_1_), channel_id=1, source_target_pairs={{0,1},{1,0},{2,3},{3,2},{4,5},{5,4},{6,7},{7,6},{8,9},{9,8},{10,11... | collective-permute-start | bytes 2359304 | tf_op jit(solution)/shard_map/ppermute | solution.py:389
  (2 other events, 4.0 us)
